TPU v7x, 512 devices: a whole 4x8x8 slice. The times are simulated.
512 devices in a mesh: axial: 32 (over x, z), girth: 16 (over y, core).
Axes of the slice: x: 4, y: 8, z: 8, core: 2. Of those that a mesh axis runs over, the one named last changes fastest.
Arguments:
- field: float32 [4, 16, 512, 2048], P(None, None, 'axial', 'girth'), may hold values from -6 to 6
- geometry: float32 [3, 16, 512, 2048], P(None, None, 'axial', 'girth'), may hold values from 5e-05 to 0.0003
- mass: float32 [16, 512, 2048], P(None, 'axial', 'girth'), may hold values from 0.4 to 2
- cycle_id: int32 [2048], P('axial'), may hold values from -1 to 511, as said below
- cycle_radial: int32 [2048], P('axial'), may hold values from 0 to 1
- cycle_axial: int32 [2048], P('axial'), may hold values from 0 to 1
- cycle_weights: float32 [2, 8, 2048], P(None, None, 'axial'), as said below
- az_elem: int32 [2048], P('girth'), may hold values from 0 to 15
- az_weights: float32 [8, 2048], P(None, 'girth'), as said below
Outputs:
- field_out: float32 [4, 16, 512, 2048], P(None, None, 'axial', 'girth')
- spectrum: float32 [2, 512, 4, 2048], P(None, 'axial', None, 'girth')
Inputs may be any that keep to these rules, and one draw needn't show every extreme that they name: `cycle_id`: every cycle 0 to 511 is named by exactly one slot; empty slots hold -1. The 64 slots of one index of axial hold at most 64 cycles, and one index of axial holds exactly 64. `cycle_weights`: the values of the 8 Lagrange polynomials of the Gauss-Lobatto-Legendre nodes at a point of [-1, 1], for the radial and for the axial direction of each slot. `az_weights`: the values of the 8 Lagrange polynomials of the Gauss-Lobatto-Legendre nodes at a point of [-1, 1] for each azimuth probe.
All inputs are finite; a program needn't handle non-finite values.
Results may differ from a plain program's by a relative error of at most 0.0003.
Values sent between devices are 32-bit elements; how exact they have to be, the bound alone decides.
No kernel may reach another device: no remote copies, remote signals or barrier semaphores. Data moves between devices by JAX's collectives and lax.ppermute only.
A program may use at most 64 MiB of HBM per device.

v0:
```python
import math

import jax
import jax.numpy as jnp
from jax import lax
from jax.sharding import PartitionSpec as P

C = 4
P_SIZE = 8
ITERS = 4
CYCLE_DEV = 16


LOBATTO = (
    -1.0,
    -0.8717401485096066,
    -0.5917001814331423,
    -0.2092992179024789,
    0.2092992179024789,
    0.5917001814331423,
    0.8717401485096066,
    1.0,
)
HIGHEST = lax.Precision.HIGHEST


def with_halo(array, sides, width, wrap):
    for axis, dim in sides:
        size, length = (lax.axis_size(axis), array.shape[dim])
        up = [(i, (i + 1) % size) for i in range(size if wrap else size - 1)]
        down = [(j, i) for i, j in up]
        last = lax.slice_in_dim(array, length - width, length, axis=dim)
        initial = lax.slice_in_dim(array, 0, width, axis=dim)
        before = lax.ppermute(last, axis, up)
        after = lax.ppermute(initial, axis, down)
        array = jnp.concatenate([before, array, after], axis=dim)
    return array


def derivative_table():
    node_count = len(LOBATTO)
    barycentric = []
    for row_index in range(node_count):
        product = 1.0
        for col_index in range(node_count):
            if col_index != row_index:
                product = product * (LOBATTO[row_index] - LOBATTO[col_index])
        barycentric.append(1.0 / product)
    table_rows = []
    for row_index in range(node_count):
        entries = []
        for col_index in range(node_count):
            if col_index != row_index:
                entries.append(
                    barycentric[col_index]
                    / barycentric[row_index]
                    / (LOBATTO[row_index] - LOBATTO[col_index])
                )
            else:
                entries.append(0.0)
        entries[row_index] = -sum(entries)
        table_rows.append(entries)
    return table_rows


def apply_matrix(values, matrix, dimension):
    extent = values.shape
    split_shape = (
        extent[:dimension] + (extent[dimension] // P_SIZE, P_SIZE) + extent[dimension + 1 :]
    )
    blocks = values.reshape(split_shape)
    rotated = jnp.tensordot(blocks, matrix, axes=[[dimension + 1], [1]], precision=HIGHEST)
    return jnp.moveaxis(rotated, -1, dimension + 1).reshape(extent)


def add_shared(core, padded, dimension):
    length = core.shape[dimension]
    lower = lax.slice_in_dim(padded, 0, length, axis=dimension)
    upper = lax.slice_in_dim(padded, 2, length + 2, axis=dimension)
    broadcast_shape = [1] * core.ndim
    broadcast_shape[dimension] = length
    position = (jnp.arange(length, dtype=jnp.int32) % P_SIZE).reshape(broadcast_shape)
    nothing = jnp.zeros((), core.dtype)
    partner = jnp.where(position == 0, lower, jnp.where(position == P_SIZE - 1, upper, nothing))
    return core + partner


def pad_one(values, dimension):
    widths = [(0, 0)] * values.ndim
    widths[dimension] = (1, 1)
    return jnp.pad(values, widths, mode="constant")


def shared_sum(values):
    values = add_shared(values, pad_one(values, 1), 1)
    padded = with_halo(values, (("axial", 2),), 1, False)
    values = add_shared(values, padded, 2)
    padded = with_halo(values, (("girth", 3),), 1, True)
    return add_shared(values, padded, 3)


def body(
    field, geometry, mass, cycle_id, cycle_radial, cycle_axial, cycle_weights, az_elem, az_weights
):
    matrix = jnp.asarray(derivative_table(), jnp.float32)
    girth_length = field.shape[3]
    block_matrix = jnp.kron(jnp.eye(girth_length // P_SIZE, dtype=jnp.float32), matrix)
    current = field
    assembled = mass
    for step_index in range(ITERS):
        total = apply_matrix(geometry[0][None] * apply_matrix(current, matrix, 1), matrix.T, 1)
        total = total + apply_matrix(
            geometry[1][None] * apply_matrix(current, matrix, 2), matrix.T, 2
        )
        girth_slope = jnp.einsum("crag,hg->crah", current, block_matrix, precision=HIGHEST)
        total = total + jnp.einsum(
            "crah,hg->crag", geometry[2][None] * girth_slope, block_matrix, precision=HIGHEST
        )
        if step_index == 0:
            stacked = shared_sum(jnp.concatenate([total, mass[None]], axis=0))
            summed = stacked[:-1]
            assembled = stacked[-1]
        else:
            summed = shared_sum(total)
        current = current - summed / assembled
    slot_count = cycle_id.shape[0]
    radial_nodes, axial_nodes, girth_nodes = (current.shape[1], current.shape[2], current.shape[3])
    radial_owner = jnp.arange(radial_nodes, dtype=jnp.int32) // P_SIZE
    radial_weight = jnp.where(
        radial_owner[None, :] == cycle_radial[:, None],
        jnp.tile(cycle_weights[0].T, (1, radial_nodes // P_SIZE)),
        0.0,
    )
    axial_owner = jnp.arange(axial_nodes, dtype=jnp.int32) // P_SIZE
    axial_weight = jnp.where(
        axial_owner[None, :] == cycle_axial[:, None],
        jnp.tile(cycle_weights[1].T, (1, axial_nodes // P_SIZE)),
        0.0,
    )
    slab_weight = (radial_weight[:, :, None] * axial_weight[:, None, :]).reshape(
        slot_count, radial_nodes * axial_nodes
    )
    cycle_values = jnp.einsum(
        "kq,cqg->kcg",
        slab_weight,
        current.reshape(C, radial_nodes * axial_nodes, girth_nodes),
        precision=HIGHEST,
    )
    girth_owner = jnp.arange(girth_nodes, dtype=jnp.int32) // P_SIZE
    girth_weight = jnp.where(
        girth_owner[:, None] == az_elem[None, :],
        jnp.tile(az_weights, (girth_nodes // P_SIZE, 1)),
        0.0,
    )
    probe_values = jnp.einsum("kcg,ga->kca", cycle_values, girth_weight, precision=HIGHEST)
    wanted = jnp.arange(CYCLE_DEV * lax.axis_size("axial"), dtype=jnp.int32)
    select = (cycle_id[:, None] == wanted[None, :]).astype(jnp.float32)
    probe_rows = lax.psum_scatter(
        jnp.einsum("kr,kca->rca", select, probe_values, precision=HIGHEST),
        "axial",
        scatter_dimension=0,
        tiled=True,
    )
    pa_dev = probe_rows.shape[2]
    girth_count = lax.axis_size("girth")
    total_az = pa_dev * girth_count
    own_index = lax.axis_index("girth") * pa_dev + jnp.arange(pa_dev, dtype=jnp.int32)
    norm_scale = 1.0 / math.sqrt(total_az)
    piece = lax.all_gather(probe_rows, "girth", axis=2, tiled=True)
    phase = jnp.arange(piece.shape[2], dtype=jnp.int32)[:, None] * own_index[None, :] % total_az
    angle = phase.astype(jnp.float32) * (2.0 * math.pi / total_az)
    cos_part = jnp.cos(angle) * norm_scale
    sin_part = -jnp.sin(angle) * norm_scale
    real_sum = jnp.einsum("rca,af->rcf", piece, cos_part, precision=HIGHEST)
    imag_sum = jnp.einsum("rca,af->rcf", piece, sin_part, precision=HIGHEST)
    spectrum = jnp.stack([real_sum, imag_sum])
    return (current, spectrum)


def solution(mesh):
    return jax.shard_map(
        body,
        mesh=mesh,
        in_specs=(
            P(None, None, "axial", "girth"),
            P(None, None, "axial", "girth"),
            P(None, "axial", "girth"),
            P("axial"),
            P("axial"),
            P("axial"),
            P(None, None, "axial"),
            P("girth"),
            P(None, "girth"),
        ),
        out_specs=(P(None, None, "axial", "girth"), P(None, "axial", None, "girth")),
        check_vma=False,
    )
```

profile of v0, /device:TPU:1, one launch (start us, length us, event | category | flops | bytes accessed | tf_op | source)
XLA Modules:
  0.0 371.2 jit_solution(12138488922539463529)
XLA Ops:
  7.2 0.6 copy-done.7
  9.1 0.9 copy-done
  10.0 0.7 fusion
  10.7 0.6 convolution_bitcast_fusion.15
  12.0 0.6 fusion.2
  12.6 0.6 fusion.9
  14.4 4.8 %collective-permute-start = (f32[5,16,1,128]{3,2,1,0:T(1,128)S(1)}, f32[5,16,1,128]{3,2,1,0:T(1,128)S(1)}, u32[]{:S(2)}, u32[]{:S(2)}) collective-permute-start(f32[5,16,1,128]{3,2,1,0:T(1,128)S(1)} %get-tuple-element.10), channel_id=1, source_target_pairs={{0,16},{16,32},{32,48},{48,64},{64,80},{80,96},{96,112},{112,128},... | collective-permute-start | bytes 122888 | tf_op jit(solution)/shard_map/ppermute | solution.py:34
  19.3 1.3 collective-permute-start.1
  20.6 4.1 %collective-permute-done.1 = f32[5,16,1,128]{3,2,1,0:T(1,128)S(1)} collective-permute-done((f32[5,16,1,128]{3,2,1,0:T(1,128)S(1)}, f32[5,16,1,128]{3,2,1,0:T(1,128)S(1)}, u32[]{:S(2)}, u32[]{:S(2)}) %collective-permute-start.1) | collective-permute-done | bytes 40992 | tf_op jit(solution)/shard_map/ppermute | solution.py:35
  25.7 3.0 collective-permute-start.2
  29.2 0.9 collective-permute-start.3
  30.8 1.9 collective-permute-done.3
  35.1 0.7 fusion.3
  35.8 0.6 convolution_bitcast_fusion.10
  36.5 0.6 fusion.10
  37.9 4.0 %collective-permute-start.4 = (f32[4,16,1,128]{3,2,1,0:T(1,128)S(1)}, f32[4,16,1,128]{3,2,1,0:T(1,128)S(1)}, u32[]{:S(2)}, u32[]{:S(2)}) collective-permute-start(f32[4,16,1,128]{3,2,1,0:T(1,128)S(1)} %get-tuple-element.22), channel_id=1, source_target_pairs={{0,16},{16,32},{32,48},{48,64},{64,80},{80,96},{96,112},{112,128},... | collective-permute-start | bytes 98312 | tf_op jit(solution)/shard_map/ppermute | solution.py:34
  41.9 1.5 collective-permute-start.5
  43.4 5.0 %collective-permute-done.5 = f32[4,16,1,128]{3,2,1,0:T(1,128)S(1)} collective-permute-done((f32[4,16,1,128]{3,2,1,0:T(1,128)S(1)}, f32[4,16,1,128]{3,2,1,0:T(1,128)S(1)}, u32[]{:S(2)}, u32[]{:S(2)}) %collective-permute-start.5) | collective-permute-done | bytes 32800 | tf_op jit(solution)/shard_map/ppermute | solution.py:35
  48.8 1.2 collective-permute-start.6
  50.0 6.1 %collective-permute-done.6 = f32[4,16,16,1]{3,2,1,0:T(8,128)S(1)} collective-permute-done((f32[4,16,16,1]{3,2,1,0:T(8,128)S(1)}, f32[4,16,16,1]{3,2,1,0:T(8,128)S(1)}, u32[]{:S(2)}, u32[]{:S(2)}) %collective-permute-start.6) | collective-permute-done | bytes 4128 | tf_op jit(solution)/shard_map/ppermute | solution.py:34
  56.1 2.8 collective-permute-done.7
  60.5 0.7 fusion.5
  61.2 0.6 convolution_bitcast_fusion.6
  62.0 0.6 fusion.11
  63.4 4.8 %collective-permute-start.8 = (f32[4,16,1,128]{3,2,1,0:T(1,128)S(1)}, f32[4,16,1,128]{3,2,1,0:T(1,128)S(1)}, u32[]{:S(2)}, u32[]{:S(2)}) collective-permute-start(f32[4,16,1,128]{3,2,1,0:T(1,128)S(1)} %get-tuple-element.18), channel_id=1, source_target_pairs={{0,16},{16,32},{32,48},{48,64},{64,80},{80,96},{96,112},{112,128},... | collective-permute-start | bytes 98312 | tf_op jit(solution)/shard_map/ppermute | solution.py:34
  68.2 1.3 collective-permute-start.9
  69.6 3.6 collective-permute-done.9
  73.6 0.9 collective-permute-start.10
  74.5 1.3 collective-permute-start.11
  75.7 4.9 %collective-permute-done.10 = f32[4,16,16,1]{3,2,1,0:T(8,128)S(1)} collective-permute-done((f32[4,16,16,1]{3,2,1,0:T(8,128)S(1)}, f32[4,16,16,1]{3,2,1,0:T(8,128)S(1)}, u32[]{:S(2)}, u32[]{:S(2)}) %collective-permute-start.10) | collective-permute-done | bytes 4128 | tf_op jit(solution)/shard_map/ppermute | solution.py:34
  80.6 2.8 collective-permute-done.11
  85.0 0.7 fusion.7
  85.7 0.6 convolution_bitcast_fusion.2
  86.4 0.6 fusion.12
  87.9 3.6 collective-permute-start.12
  91.5 1.3 collective-permute-start.13
  92.8 0.6 copy-done.10
  93.6 2.6 collective-permute-done.13
  96.6 1.1 collective-permute-start.14
  97.7 2.5 collective-permute-start.15
  100.2 3.6 collective-permute-done.14
  103.9 2.8 collective-permute-done.15
  108.5 1.7 fusion.84
  110.2 219.7 %reduce-scatter.2.cloned.1.call-done = f32[16,4,128]{2,0,1:T(8,128)} async-done(((f32[512,4,128]{2,0,1:T(8,128)}), f32[16,4,128]{2,0,1:T(8,128)}) %reduce-scatter.2.cloned.1.call-update) | async-done | bytes 32784 | tf_op jit(solution)/shard_map/reduce_scatter | solution.py:158
  329.9 24.5 %all_gather.3 = f32[16,4,2048]{2,0,1:T(8,128)S(1)} all-gather(f32[16,4,128]{2,0,1:T(8,128)} %reduce-scatter.2.cloned.1.call-done), channel_id=1, replica_groups=mesh['axial'=32,'girth'=16] {'girth'}, dimensions={2}, use_global_device_ids=true | all-gather | bytes 557056 | tf_op jit(solution)/shard_map/all_gather | solution.py:169
  354.5 4.6 %convolution_bitcast_fusion.18 = f32[1,16,4,128]{3,1,2,0:T(8,128)S(1)} fusion(f32[16,4,2048]{2,0,1:T(8,128)S(1)} %all_gather.3, s32[128]{0:T(128)S(1)} %iota_add_fusion), kind=kOutput, calls=%fused_computation.41 | convolution fusion | flops 205520896 | bytes 557568 | tf_op jit(solution)/shard_map/rca,af->rcf/dot_general | solution.py:175
  359.1 4.6 %convolution_bitcast_fusion.19 = f32[1,16,4,128]{3,1,2,0:T(8,128)S(1)} fusion(f32[16,4,2048]{2,0,1:T(8,128)S(1)} %all_gather.3, s32[128]{0:T(128)S(1)} %iota_add_fusion), kind=kOutput, calls=%fused_computation.42 | convolution fusion | flops 205258752 | bytes 557568 | tf_op jit(solution)/shard_map/rca,af->rcf/dot_general | solution.py:174
  363.7 0.7 copy.50
  (86 shorter events, 16.9 us)
Async XLA Ops:
  7.2 0.7 copy-start.7
  7.2 322.8 %reduce-scatter.2.cloned.1.call-start = ((), (), s32[]{:S(2)}) async-start(), calls=%async_computation.1 | async-start | bytes 1081344 | tf_op jit(solution)/shard_map/reduce_scatter | solution.py:158
  8.0 1.0 copy-start.3
  9.0 1.0 copy-start
  9.0 1.0 copy-start.2
  13.2 0.9 copy-start.4
  14.4 6.1 %collective-permute-start = (f32[5,16,1,128]{3,2,1,0:T(1,128)S(1)}, f32[5,16,1,128]{3,2,1,0:T(1,128)S(1)}, u32[]{:S(2)}, u32[]{:S(2)}) collective-permute-start(f32[5,16,1,128]{3,2,1,0:T(1,128)S(1)} %get-tuple-element.10), channel_id=1, source_target_pairs={{0,16},{16,32},{32,48},{48,64},{64,80},{80,96},{96,112},{112,128},... | collective-permute-start | bytes 122888 | tf_op jit(solution)/shard_map/ppermute | solution.py:34
  19.3 5.4 %collective-permute-start.1 = (f32[5,16,1,128]{3,2,1,0:T(1,128)S(1)}, f32[5,16,1,128]{3,2,1,0:T(1,128)S(1)}, u32[]{:S(2)}, u32[]{:S(2)}) collective-permute-start(f32[5,16,1,128]{3,2,1,0:T(1,128)S(1)} %get-tuple-element.11), channel_id=1, source_target_pairs={{16,0},{32,16},{48,32},{64,48},{80,64},{96,80},{112,96},{128,112},... | collective-permute-start | bytes 122888 | tf_op jit(solution)/shard_map/ppermute | solution.py:35
  25.7 4.6 %collective-permute-start.2 = (f32[5,16,16,1]{2,1,3,0:T(8,128)S(1)}, f32[5,16,16,1]{2,1,3,0:T(8,128)S(1)}, u32[]{:S(2)}, u32[]{:S(2)}) collective-permute-start(f32[5,16,16,1]{2,1,3,0:T(8,128)S(1)} %copy.34), channel_id=1, source_target_pairs={{0,1},{1,2},{2,3},{3,4},{4,5},{5,6},{6,7},{7,8},{8,9},{9,10},{10,1... | collective-permute-start | bytes 15368 | tf_op jit(solution)/shard_map/ppermute | solution.py:34
  29.2 3.4 collective-permute-start.3
  37.9 5.5 %collective-permute-start.4 = (f32[4,16,1,128]{3,2,1,0:T(1,128)S(1)}, f32[4,16,1,128]{3,2,1,0:T(1,128)S(1)}, u32[]{:S(2)}, u32[]{:S(2)}) collective-permute-start(f32[4,16,1,128]{3,2,1,0:T(1,128)S(1)} %get-tuple-element.22), channel_id=1, source_target_pairs={{0,16},{16,32},{32,48},{48,64},{64,80},{80,96},{96,112},{112,128},... | collective-permute-start | bytes 98312 | tf_op jit(solution)/shard_map/ppermute | solution.py:34
  41.9 6.5 %collective-permute-start.5 = (f32[4,16,1,128]{3,2,1,0:T(1,128)S(1)}, f32[4,16,1,128]{3,2,1,0:T(1,128)S(1)}, u32[]{:S(2)}, u32[]{:S(2)}) collective-permute-start(f32[4,16,1,128]{3,2,1,0:T(1,128)S(1)} %get-tuple-element.23), channel_id=1, source_target_pairs={{16,0},{32,16},{48,32},{64,48},{80,64},{96,80},{112,96},{128,112},... | collective-permute-start | bytes 98312 | tf_op jit(solution)/shard_map/ppermute | solution.py:35
  48.8 7.3 %collective-permute-start.6 = (f32[4,16,16,1]{3,2,1,0:T(8,128)S(1)}, f32[4,16,16,1]{3,2,1,0:T(8,128)S(1)}, u32[]{:S(2)}, u32[]{:S(2)}) collective-permute-start(f32[4,16,16,1]{3,2,1,0:T(8,128)S(1)} %get-tuple-element.20), channel_id=1, source_target_pairs={{0,1},{1,2},{2,3},{3,4},{4,5},{5,6},{6,7},{7,8},{8,9},{9,10},{10,1... | collective-permute-start | bytes 12296 | tf_op jit(solution)/shard_map/ppermute | solution.py:34
  50.0 8.9 %collective-permute-start.7 = (f32[4,16,16,1]{3,2,1,0:T(8,128)S(1)}, f32[4,16,16,1]{3,2,1,0:T(8,128)S(1)}, u32[]{:S(2)}, u32[]{:S(2)}) collective-permute-start(f32[4,16,16,1]{3,2,1,0:T(8,128)S(1)} %get-tuple-element.21), channel_id=1, source_target_pairs={{1,0},{2,1},{3,2},{4,3},{5,4},{6,5},{7,6},{8,7},{9,8},{10,9},{11,1... | collective-permute-start | bytes 12296 | tf_op jit(solution)/shard_map/ppermute | solution.py:35
  63.1 6.4 %copy-start.5 = (f32[2,8,64]{2,1,0:T(8,128)S(1)}, f32[2,8,64]{2,1,0:T(8,128)}, u32[]{:S(2)}) copy-start(f32[2,8,64]{2,1,0:T(8,128)} %param.16) | copy-start | bytes 12292
  63.4 6.2 %collective-permute-start.8 = (f32[4,16,1,128]{3,2,1,0:T(1,128)S(1)}, f32[4,16,1,128]{3,2,1,0:T(1,128)S(1)}, u32[]{:S(2)}, u32[]{:S(2)}) collective-permute-start(f32[4,16,1,128]{3,2,1,0:T(1,128)S(1)} %get-tuple-element.18), channel_id=1, source_target_pairs={{0,16},{16,32},{32,48},{48,64},{64,80},{80,96},{96,112},{112,128},... | collective-permute-start | bytes 98312 | tf_op jit(solution)/shard_map/ppermute | solution.py:34
  68.2 4.9 %collective-permute-start.9 = (f32[4,16,1,128]{3,2,1,0:T(1,128)S(1)}, f32[4,16,1,128]{3,2,1,0:T(1,128)S(1)}, u32[]{:S(2)}, u32[]{:S(2)}) collective-permute-start(f32[4,16,1,128]{3,2,1,0:T(1,128)S(1)} %get-tuple-element.19), channel_id=1, source_target_pairs={{16,0},{32,16},{48,32},{64,48},{80,64},{96,80},{112,96},{128,112},... | collective-permute-start | bytes 98312 | tf_op jit(solution)/shard_map/ppermute | solution.py:35
  73.6 7.0 %collective-permute-start.10 = (f32[4,16,16,1]{3,2,1,0:T(8,128)S(1)}, f32[4,16,16,1]{3,2,1,0:T(8,128)S(1)}, u32[]{:S(2)}, u32[]{:S(2)}) collective-permute-start(f32[4,16,16,1]{3,2,1,0:T(8,128)S(1)} %get-tuple-element.16), channel_id=1, source_target_pairs={{0,1},{1,2},{2,3},{3,4},{4,5},{5,6},{6,7},{7,8},{8,9},{9,10},{10,1... | collective-permute-start | bytes 12296 | tf_op jit(solution)/shard_map/ppermute | solution.py:34
  74.5 8.9 %collective-permute-start.11 = (f32[4,16,16,1]{3,2,1,0:T(8,128)S(1)}, f32[4,16,16,1]{3,2,1,0:T(8,128)S(1)}, u32[]{:S(2)}, u32[]{:S(2)}) collective-permute-start(f32[4,16,16,1]{3,2,1,0:T(8,128)S(1)} %get-tuple-element.17), channel_id=1, source_target_pairs={{1,0},{2,1},{3,2},{4,3},{5,4},{6,5},{7,6},{8,7},{9,8},{10,9},{11,1... | collective-permute-start | bytes 12296 | tf_op jit(solution)/shard_map/ppermute | solution.py:35
  87.9 5.7 %collective-permute-start.12 = (f32[4,16,1,128]{3,2,1,0:T(1,128)S(1)}, f32[4,16,1,128]{3,2,1,0:T(1,128)S(1)}, u32[]{:S(2)}, u32[]{:S(2)}) collective-permute-start(f32[4,16,1,128]{3,2,1,0:T(1,128)S(1)} %get-tuple-element.14), channel_id=1, source_target_pairs={{0,16},{16,32},{32,48},{48,64},{64,80},{80,96},{96,112},{112,128},... | collective-permute-start | bytes 98312 | tf_op jit(solution)/shard_map/ppermute | solution.py:34
  91.5 4.7 %collective-permute-start.13 = (f32[4,16,1,128]{3,2,1,0:T(1,128)S(1)}, f32[4,16,1,128]{3,2,1,0:T(1,128)S(1)}, u32[]{:S(2)}, u32[]{:S(2)}) collective-permute-start(f32[4,16,1,128]{3,2,1,0:T(1,128)S(1)} %get-tuple-element.15), channel_id=1, source_target_pairs={{16,0},{32,16},{48,32},{64,48},{80,64},{96,80},{112,96},{128,112},... | collective-permute-start | bytes 98312 | tf_op jit(solution)/shard_map/ppermute | solution.py:35
  92.8 0.7 copy-start.10
  92.8 0.7 copy-start.11
  96.6 7.3 %collective-permute-start.14 = (f32[4,16,16,1]{3,2,1,0:T(8,128)S(1)}, f32[4,16,16,1]{3,2,1,0:T(8,128)S(1)}, u32[]{:S(2)}, u32[]{:S(2)}) collective-permute-start(f32[4,16,16,1]{3,2,1,0:T(8,128)S(1)} %get-tuple-element.12), channel_id=1, source_target_pairs={{0,1},{1,2},{2,3},{3,4},{4,5},{5,6},{6,7},{7,8},{8,9},{9,10},{10,1... | collective-permute-start | bytes 12296 | tf_op jit(solution)/shard_map/ppermute | solution.py:34
  97.7 8.9 %collective-permute-start.15 = (f32[4,16,16,1]{3,2,1,0:T(8,128)S(1)}, f32[4,16,16,1]{3,2,1,0:T(8,128)S(1)}, u32[]{:S(2)}, u32[]{:S(2)}) collective-permute-start(f32[4,16,16,1]{3,2,1,0:T(8,128)S(1)} %get-tuple-element.13), channel_id=1, source_target_pairs={{1,0},{2,1},{3,2},{4,3},{5,4},{6,5},{7,6},{8,7},{9,8},{10,9},{11,1... | collective-permute-start | bytes 12296 | tf_op jit(solution)/shard_map/ppermute | solution.py:35
  107.1 3.1 copy-start.1
  107.1 0.7 copy-start.6
  107.1 0.7 copy-start.8
  107.9 0.7 copy-start.9
Sparse Core Ops, SparseCore 0:
  110.4 219.5 reduce-scatter.1
where the time goes:
time: 372 us; the launch traced here: 371 us
  waiting for transfers between devices  260 us (70%)
  starting transfers between devices  33.5 us (9%)
  matrix products  26.1 us (7%)
  blocking collectives  24.5 us (7%)
  between operations  14.6 us (4%)
  local copies, waits for them, and re-layouts  8.51 us (2%)
  other arithmetic  3.92 us (1%)
    reduce_scatter x1, waiting for transfers between devices, body(): lax.psum_scatter(jnp.einsum('kr,kca->rca', select, probe_values, precisio...  220 us
    ppermute x8, waiting for transfers between devices, with_halo(): after = lax.ppermute(initial, axis, down)  25.5 us
    all_gather x1, blocking collectives, body(): piece = lax.all_gather(probe_rows, 'girth', axis=2, tiled=True)  24.5 us
    ppermute x8, starting transfers between devices, with_halo(): before = lax.ppermute(last, axis, up)  23.5 us
    ppermute x8, waiting for transfers between devices, with_halo(): before = lax.ppermute(last, axis, up)  14.8 us
    ppermute x8, starting transfers between devices, with_halo(): after = lax.ppermute(initial, axis, down)  10 us
    dot_general x16, matrix products, apply_matrix(): jnp.tensordot(blocks, matrix, axes=[[dimension + 1], [1]], precision=HIGH...  9.87 us
  transfers between devices with their start and end apart: 17, of which 13 were waited for; matrix products, arithmetic and copies ran while one was open for 0% of the time, Pallas kernels for 0%

commit v1 on v0

v1 whole, which is shorter than its diff:
```python
import math

import jax
import jax.numpy as jnp
import ml_dtypes
import numpy as np
from jax import lax
from jax.experimental import pallas as pl
from jax.experimental.pallas import tpu as pltpu
from jax.sharding import PartitionSpec as P

C = 4
P_SIZE = 8
LANES = 128
HALO = 32
NODES = 256
WIDE = 6 * LANES
ROWS_DEV = 16
F32 = jnp.float32
BF16 = jnp.bfloat16

LOBATTO = (
    -1.0,
    -0.8717401485096066,
    -0.5917001814331423,
    -0.2092992179024789,
    0.2092992179024789,
    0.5917001814331423,
    0.8717401485096066,
    1.0,
)


def derivative_table():
    node_count = len(LOBATTO)
    barycentric = []
    for row_index in range(node_count):
        product = 1.0
        for col_index in range(node_count):
            if col_index != row_index:
                product = product * (LOBATTO[row_index] - LOBATTO[col_index])
        barycentric.append(1.0 / product)
    table_rows = []
    for row_index in range(node_count):
        entries = []
        for col_index in range(node_count):
            if col_index != row_index:
                entries.append(
                    barycentric[col_index]
                    / barycentric[row_index]
                    / (LOBATTO[row_index] - LOBATTO[col_index])
                )
            else:
                entries.append(0.0)
        entries[row_index] = -sum(entries)
        table_rows.append(entries)
    return np.asarray(table_rows, np.float32)


def np_split(table):
    table = np.asarray(table, np.float32)
    high = table.astype(ml_dtypes.bfloat16)
    low = (table - high.astype(np.float32)).astype(ml_dtypes.bfloat16)
    return high, low


def left_operand(table):
    high, low = np_split(table)
    return np.concatenate([high, high, low], axis=1)


def right_operand(table):
    high, low = np_split(table)
    return np.concatenate([high, high, low], axis=0)


def stiffness_tables():
    d = derivative_table()
    eye = lambda n: np.eye(n, dtype=np.float32)
    radial = np.kron(np.kron(eye(2), d), eye(16))
    axial = np.kron(eye(32), d)
    slope = np.concatenate([radial, axial], axis=0)
    return (
        left_operand(slope),
        left_operand(slope.T),
        right_operand(axial.T),
        right_operand(axial),
    )


def dft_tables():
    a = np.arange(2048)[:, None]
    m = np.arange(LANES)[None, :]
    angle = 2.0 * np.pi * ((a * m) % 2048) / 2048.0
    table = np.concatenate([np.cos(angle), np.sin(angle)], axis=1)
    high, low = np_split(table)
    k = np.arange(16)[:, None]
    lane = np.arange(LANES)[None, :]
    turn = 2.0 * np.pi * ((k * lane) % 16) / 16.0
    phase = np.stack([np.cos(turn), -np.sin(turn)], axis=1) / math.sqrt(2048.0)
    return high, low, phase.astype(np.float32)


def split(x):
    high = x.astype(BF16)
    return high, (x - high.astype(F32)).astype(BF16)


def dot(a, b):
    return jnp.dot(a, b, preferred_element_type=F32)


def left_mul(table, x):
    high, low = split(x)
    return dot(table, jnp.concatenate([high, low, high], axis=0))


def right_mul(x, table):
    high, low = split(x)
    return dot(jnp.concatenate([high, low, high], axis=1), table)


def stiff(u, gr, ga, gg, tables):
    slope_l, slope_t, girth, girth_t = tables
    ra = left_mul(slope_l[...], u)
    g = right_mul(u, girth[...])
    y = jnp.concatenate([ra[:NODES] * gr, ra[NODES:] * ga], axis=0)
    return left_mul(slope_t[...], y) + right_mul(g * gg, girth_t[...])


def twice(x):
    return jnp.concatenate([x, x], axis=1)


def sum_nodes(t):
    width = t.shape[1]
    v = t.reshape(16, 16, width)
    mid = v[7:8] + v[8:9]
    v = jnp.concatenate([v[:7], mid, mid, v[9:]], axis=0)
    pair = v[:, 7:8, :] + v[:, 8:9, :]
    node = lax.broadcasted_iota(jnp.int32, v.shape, 1)
    return jnp.where((node == 7) | (node == 8), pair, v)


def sum_girth(own, left, right, owners):
    lane = lax.broadcasted_iota(jnp.int32, left.shape, 1)
    first = lane % P_SIZE == 0
    last = lane % P_SIZE == P_SIZE - 1

    def inner(x):
        return jnp.where(
            first, pltpu.roll(x, 1, 1), jnp.where(last, pltpu.roll(x, LANES - 1, 1), 0.0)
        )

    sums = []
    for c, x in enumerate(own):
        p = inner(x)
        p = jnp.where(lane == 0, pltpu.roll(left, (LANES - HALO * c - HALO + 1) % LANES, 1), p)
        p = jnp.where(lane == LANES - 1, pltpu.roll(right, (LANES - 1 - HALO * c) % LANES, 1), p)
        sums.append(x + p)
    p = inner(left)
    q = inner(right)
    for c, x in enumerate(owners):
        p = jnp.where(lane == HALO * c + HALO - 1, pltpu.roll(x, HALO * c + HALO - 1, 1), p)
        q = jnp.where(lane == HALO * c, pltpu.roll(x, (HALO * c + 1) % LANES, 1), q)
    return sums + [left + p, right + q]


def shared_local(parts):
    return jnp.concatenate(sum_girth(parts[:4], parts[4], parts[5], parts[:4]), axis=1)


def lanes_of(x, k):
    return x[:, k * LANES : (k + 1) * LANES]


def pack_kernel(field, geom, mass, to_right, to_left):
    lane = lax.broadcasted_iota(jnp.int32, (NODES, LANES), 1)

    def pack(arrays, start):
        out = None
        for k, x in enumerate(arrays):
            moved = pltpu.roll(x, (HALO * k - start) % LANES, 1) if (HALO * k - start) else x
            out = moved if out is None else jnp.where(lane // HALO == k, moved, out)
        return out

    fields = [field[c] for c in range(C)]
    others = [geom[k] for k in range(3)] + [mass[...]]
    to_right[0] = pack(fields, LANES - HALO)
    to_right[1] = pack(others, LANES - HALO)
    to_left[0] = pack(fields, 0)
    to_left[1] = pack(others, 0)


def own_kernel(field, geom, *refs):
    tables, out = refs[:4], refs[4]
    gr, ga, gg = [twice(geom[k]) for k in range(3)]
    for pair in range(2):
        u = jnp.concatenate([field[2 * pair], field[2 * pair + 1]], axis=1)
        out[:, 2 * pair * LANES : (2 * pair + 2) * LANES] = stiff(u, gr, ga, gg, tables)


def faces(total, low, high, offset):
    width = total.shape[2]
    low[:, offset : offset + width] = total[:, 0, :]
    high[:, offset : offset + width] = total[:, 15, :]


def halo_kernel(left, right, own_total, mass, *refs):
    tables = refs[:4]
    halo_geom, total_out, mass_out, low, high = refs[4:]
    lane = lax.broadcasted_iota(jnp.int32, (NODES, LANES), 1)

    def spread(x, k):
        y = jnp.where(lane // HALO == k, x, 0.0)
        y = y + pltpu.roll(y, HALO, 1)
        return y + pltpu.roll(y, 2 * HALO, 1)

    left_others, right_others = left[1], right[1]
    geoms = []
    for k in range(3):
        g = jnp.concatenate([spread(left_others, k), spread(right_others, k)], axis=1)
        halo_geom[k] = g
        geoms.append(g)
    u = jnp.concatenate([left[0], right[0]], axis=1)
    t = stiff(u, *geoms, tables)
    parts = [own_total[:, c * LANES : (c + 1) * LANES] for c in range(C)]
    total = sum_nodes(shared_local(parts + [lanes_of(t, 0), lanes_of(t, 1)]))
    total_out[...] = total.reshape(NODES, WIDE)
    faces(total, low, high, 0)
    m = mass[...]
    masses = sum_girth([m], spread(left_others, 3), spread(right_others, 3), [m] * C)
    lumped = sum_nodes(jnp.concatenate(masses, axis=1))
    mass_out[...] = lumped.reshape(NODES, 3 * LANES)
    faces(lumped, low, high, WIDE)


def received(low, high):
    shape = (16, 16, low.shape[1])
    node = lax.broadcasted_iota(jnp.int32, shape, 1)
    both = jnp.where(
        node == 0, low[:, None, :], jnp.where(node == 15, high[:, None, :], 0.0)
    )
    return both.reshape(NODES, low.shape[1])


def wide(x):
    own = lanes_of(x, 0)
    return jnp.concatenate([own] * C + [x[:, LANES:]], axis=1)


def advance(u, inverse, geom, halo_geom, tables, out, low, high):
    gr, ga, gg = [twice(geom[k]) for k in range(3)]
    parts = []
    for tile in range(3):
        if tile == 2:
            gr, ga, gg = [halo_geom[k] for k in range(3)]
        t = stiff(u[:, 2 * tile * LANES : (2 * tile + 2) * LANES], gr, ga, gg, tables)
        parts += [lanes_of(t, 0), lanes_of(t, 1)]
    total = sum_nodes(shared_local(parts))
    faces(total, low, high, 0)
    out[...] = u - total.reshape(NODES, WIDE) * wide(inverse)


def first_kernel(field, left, right, total, lumped, got_low, got_high, geom, halo_geom, *refs):
    tables = refs[:4]
    out, inverse_out, low, high = refs[4:]
    arrived = received(got_low[...], got_high[...])
    inverse = 1.0 / (lumped[...] + arrived[:, WIDE:])
    inverse_out[...] = inverse
    u = jnp.concatenate([field[c] for c in range(C)] + [left[0], right[0]], axis=1)
    u = u - (total[...] + arrived[:, :WIDE]) * wide(inverse)
    advance(u, inverse, geom, halo_geom, tables, out, low, high)


def step_kernel(state, inverse_ref, got_low, got_high, geom, halo_geom, *refs):
    tables = refs[:4]
    out, low, high = refs[4:]
    inverse = inverse_ref[...]
    u = state[...] - received(got_low[...], got_high[...]) * wide(inverse)
    advance(u, inverse, geom, halo_geom, tables, out, low, high)


def last_kernel(state, inverse_ref, got_low, got_high, slab, girth_weight, select, out, dense):
    own = C * LANES
    inverse = jnp.concatenate([inverse_ref[:, :LANES]] * C, axis=1)
    u = state[:, :own] - received(got_low[:, :own], got_high[:, :own]) * inverse
    for c in range(C):
        out[c] = lanes_of(u, c)
    slab_high, slab_low = split(slab[...])
    values = left_mul(jnp.concatenate([slab_high, slab_high, slab_low], axis=1), u)
    stacked = jnp.concatenate([lanes_of(values, c) for c in range(C)], axis=0)
    weight_high, weight_low = split(girth_weight[...])
    weights = jnp.concatenate([weight_high, weight_high, weight_low], axis=0)
    probes = right_mul(stacked, weights)
    slots = slab.shape[0]
    spread = jnp.concatenate([probes[c * slots : (c + 1) * slots] for c in range(C)], axis=1)
    high, low = split(spread)
    chosen = select[...].astype(BF16)
    rows = dot(jnp.concatenate([chosen, chosen], axis=1), jnp.concatenate([high, low], axis=0))
    for c in range(C):
        dense[:, c * ROWS_DEV : (c + 1) * ROWS_DEV, :] = lanes_of(rows, c).reshape(
            -1, ROWS_DEV, LANES
        )


def dft_kernel(rows, phase, table_high, table_low, out):
    turn_re = phase[0:1, :]
    turn_im = phase[1:2, :]
    total = None
    for pair in range(8):
        x = jnp.concatenate([rows[2 * pair], rows[2 * pair + 1]], axis=1)
        z = jnp.concatenate([x * twice(turn_re), x * twice(turn_im)], axis=0)
        high, low = split(z)
        block = pl.ds(pair * 256, 256)
        th, tl = table_high[block, :], table_low[block, :]
        part = dot(high, th) + dot(low, th) + dot(high, tl)
        total = part if total is None else total + part
    n = C * ROWS_DEV
    re = total[:n, :LANES] + total[n:, LANES:]
    im = total[n:, :LANES] - total[:n, LANES:]
    for c in range(C):
        out[0, :, c, :] = re[c * ROWS_DEV : (c + 1) * ROWS_DEV]
        out[1, :, c, :] = im[c * ROWS_DEV : (c + 1) * ROWS_DEV]


def call(kernel, shapes, flops, *args):
    vmem = pl.BlockSpec(memory_space=pltpu.VMEM)
    out_shape = [jax.ShapeDtypeStruct(s, F32) for s in shapes]
    return pl.pallas_call(
        kernel,
        out_shape=out_shape,
        in_specs=[vmem] * len(args),
        out_specs=[vmem] * len(shapes),
        compiler_params=pltpu.CompilerParams(vmem_limit_bytes=40 * 1024 * 1024),
        cost_estimate=pl.CostEstimate(flops=flops, bytes_accessed=2000000, transcendentals=0),
    )(*args)


def body(
    field, geometry, mass, cycle_id, cycle_radial, cycle_axial, cycle_weights, az_elem, az_weights
):
    axial_count, girth_count = lax.axis_size("axial"), lax.axis_size("girth")
    up = [(i, i + 1) for i in range(axial_count - 1)]
    down = [(j, i) for i, j in up]
    around = [(i, (i + 1) % girth_count) for i in range(girth_count)]
    back = [(j, i) for i, j in around]
    tables = [jnp.asarray(t) for t in stiffness_tables()]
    field = field.reshape(C, NODES, LANES)
    geom = geometry.reshape(3, NODES, LANES)
    mass = mass.reshape(NODES, LANES)
    tile_flops = 18 * 2 * 256**3

    to_right, to_left = call(pack_kernel, [(2, NODES, LANES)] * 2, 1000000, field, geom, mass)
    left = lax.ppermute(to_right, "girth", around)
    right = lax.ppermute(to_left, "girth", back)
    (own_total,) = call(own_kernel, [(NODES, C * LANES)], 2 * tile_flops, field, geom, *tables)

    def exchange(low, high):
        return lax.ppermute(high, "axial", up), lax.ppermute(low, "axial", down)

    face_wide = (16, WIDE + 3 * LANES)
    halo_geom, total, lumped, low, high = call(
        halo_kernel,
        [(3, NODES, 2 * LANES), (NODES, WIDE), (NODES, 3 * LANES), face_wide, face_wide],
        tile_flops,
        left,
        right,
        own_total,
        mass,
        *tables,
    )
    got_low, got_high = exchange(low, high)
    face = (16, WIDE)
    state, inverse, low, high = call(
        first_kernel,
        [(NODES, WIDE), (NODES, 3 * LANES), face, face],
        3 * tile_flops,
        field,
        left,
        right,
        total,
        lumped,
        got_low,
        got_high,
        geom,
        halo_geom,
        *tables,
    )
    for _ in range(2):
        got_low, got_high = exchange(low, high)
        state, low, high = call(
            step_kernel,
            [(NODES, WIDE), face, face],
            3 * tile_flops,
            state,
            inverse,
            got_low,
            got_high,
            geom,
            halo_geom,
            *tables,
        )
    got_low, got_high = exchange(low, high)

    slot_count = cycle_id.shape[0]
    node = jnp.arange(NODES, dtype=jnp.int32)
    radial_node, axial_node = node // 16, node % 16
    radial_weight = jnp.where(
        radial_node[None, :] // P_SIZE == cycle_radial[:, None],
        jnp.tile(jnp.repeat(cycle_weights[0].T, 16, axis=1), (1, 2)),
        0.0,
    )
    axial_weight = jnp.where(
        axial_node[None, :] // P_SIZE == cycle_axial[:, None],
        jnp.tile(cycle_weights[1].T, (1, NODES // P_SIZE)),
        0.0,
    )
    slab = radial_weight * axial_weight
    girth_node = jnp.arange(LANES, dtype=jnp.int32)
    girth_weight = jnp.where(
        girth_node[:, None] // P_SIZE == az_elem[None, :],
        jnp.tile(az_weights, (LANES // P_SIZE, 1)),
        0.0,
    )
    wanted = jnp.arange(ROWS_DEV * axial_count, dtype=jnp.int32)
    select = (wanted[:, None] == cycle_id[None, :]).astype(F32)

    final, dense = call(
        last_kernel,
        [(C, NODES, LANES), (axial_count, C * ROWS_DEV, LANES)],
        tile_flops,
        state,
        inverse,
        got_low,
        got_high,
        slab,
        girth_weight,
        select,
    )
    pieces = lax.all_to_all(dense, "axial", 0, 0)
    rows = lax.all_gather(jnp.sum(pieces, axis=0), "girth")
    table_high, table_low, phases = dft_tables()
    phase = lax.dynamic_index_in_dim(
        jnp.asarray(phases), lax.axis_index("girth"), 0, keepdims=False
    )
    (spectrum,) = call(
        dft_kernel,
        [(2, ROWS_DEV, C, LANES)],
        tile_flops,
        rows,
        phase,
        jnp.asarray(table_high),
        jnp.asarray(table_low),
    )
    return final.reshape(C, 16, 16, LANES), spectrum


def solution(mesh):
    return jax.shard_map(
        body,
        mesh=mesh,
        in_specs=(
            P(None, None, "axial", "girth"),
            P(None, None, "axial", "girth"),
            P(None, "axial", "girth"),
            P("axial"),
            P("axial"),
            P("axial"),
            P(None, None, "axial"),
            P("girth"),
            P(None, "girth"),
        ),
        out_specs=(P(None, None, "axial", "girth"), P(None, "axial", None, "girth")),
        check_vma=False,
    )
```

time: 372 us -> 127 us (0.34)
  waiting for transfers between devices: 260 us -> 33.5 us
  matrix products: 26.1 us -> 0 us
  Pallas kernels: 0 us -> 17.4 us
  between operations: 14.6 us -> 1 us
  blocking collectives: 24.5 us -> 29.4 us
    reduce_scatter x1 -> x0, waiting for transfers between devices: 220 us -> none  [body(): lax.psum_scatter(jnp.einsum('kr,kca->rca', select, probe_values, precisio...]
    dot_general x29 -> x0, matrix products: 26.1 us -> none  [the longest x16 9.87 us: apply_matrix(): jnp.tensordot(blocks, matrix, axes=[[dimension + 1], [1]], precision=HIGH...]
    ppermute x16 -> x10, waiting for transfers between devices: 40.3 us -> 14.9 us  [the longest x8 14.9 us: exchange(): return (lax.ppermute(high, 'axial', up), lax.ppermute(low, 'axial', down))]
    all_to_all x0 -> x1, waiting for transfers between devices: none -> 18.6 us  [body(): pieces = lax.all_to_all(dense, 'axial', 0, 0)]
    pallas_call x0 -> x8, Pallas kernels: none -> 17.4 us  [call(): pl.pallas_call(kernel, out_shape=out_shape, in_specs=[vmem] * len(args),...]
    all_to_all x0 -> x1, starting transfers between devices: none -> 10.7 us  [body(): pieces = lax.all_to_all(dense, 'axial', 0, 0)]
    ppermute x16 -> x10, starting transfers between devices: 33.5 us -> 25 us  [the longest x8 18.2 us: exchange(): return (lax.ppermute(high, 'axial', up), lax.ppermute(low, 'axial', down))]
    all_gather x1, blocking collectives: 24.5 us -> 29.4 us  [body(): rows = lax.all_gather(jnp.sum(pieces, axis=0), 'girth')]
  transfers between devices with their start and end apart: 17 -> 11, of which waited for: 13 -> 6; matrix products, arithmetic and copies ran while one was open for 0% -> 2% of each run, Pallas kernels for 0% -> 2%
where the time goes in v1:
time: 127 us; the launch traced here: 126 us
  starting transfers between devices  35.7 us (28%)
  waiting for transfers between devices  33.5 us (26%)
  blocking collectives  29.4 us (23%)
  Pallas kernels  17.4 us (14%)
  local copies, waits for them, and re-layouts  8.98 us (7%)
    all_gather x1, blocking collectives, body(): rows = lax.all_gather(jnp.sum(pieces, axis=0), 'girth')  29.4 us
    all_to_all x1, waiting for transfers between devices, body(): pieces = lax.all_to_all(dense, 'axial', 0, 0)  18.6 us
    ppermute x8, starting transfers between devices, exchange(): return (lax.ppermute(high, 'axial', up), lax.ppermute(low, 'axial', down))  18.2 us
    pallas_call x8, Pallas kernels, call(): pl.pallas_call(kernel, out_shape=out_shape, in_specs=[vmem] * len(args),...  17.4 us
    ppermute x8, waiting for transfers between devices, exchange(): return (lax.ppermute(high, 'axial', up), lax.ppermute(low, 'axial', down))  14.9 us
    all_to_all x1, starting transfers between devices, body(): pieces = lax.all_to_all(dense, 'axial', 0, 0)  10.7 us
    unnamed x40, local copies, waits for them, and re-layouts  6.69 us
    ppermute x1, starting transfers between devices, body(): right = lax.ppermute(to_left, 'girth', back)  4.19 us
  transfers between devices with their start and end apart: 11, of which 6 were waited for; matrix products, arithmetic and copies ran while one was open for 2% of the time, Pallas kernels for 2%

profile of v1, /device:TPU:1, one launch (start us, length us, event | category | flops | bytes accessed | tf_op | source)
XLA Modules:
  0.0 126.3 jit_solution(7474098800899972126)
XLA Ops:
  0.6 0.0 copy-start.2
  0.7 1.0 copy-done.5
  1.6 1.0 copy-done.7
  2.7 1.0 copy-done.12
  3.7 1.2 shard_map.167
  4.8 2.7 %collective-permute-start = (f32[2,256,128]{2,1,0:T(8,128)}, f32[2,256,128]{2,1,0:T(8,128)S(1)}, u32[]{:S(2)}, u32[]{:S(2)}) collective-permute-start(f32[2,256,128]{2,1,0:T(8,128)} %get-tuple-element.21), channel_id=1, source_target_pairs={{0,1},{1,2},{2,3},{3,4},{4,5},{5,6},{6,7},{7,8},{8,9},{9,10},{10,1... | collective-permute-start | bytes 786440 | tf_op jit(solution)/shard_map/ppermute | solution.py:355
  7.5 4.2 %collective-permute-start.1 = (f32[2,256,128]{2,1,0:T(8,128)}, f32[2,256,128]{2,1,0:T(8,128)S(1)}, u32[]{:S(2)}, u32[]{:S(2)}) collective-permute-start(f32[2,256,128]{2,1,0:T(8,128)} %get-tuple-element.22), channel_id=1, source_target_pairs={{1,0},{2,1},{3,2},{4,3},{5,4},{6,5},{7,6},{8,7},{9,8},{10,9},{11,1... | collective-permute-start | bytes 786440 | tf_op jit(solution)/shard_map/ppermute | solution.py:356
  11.7 0.7 slice_bitcast_fusion
  12.4 0.0 copy-start.3
  12.5 1.1 copy-done.3
  13.6 1.0 copy-done.10
  14.6 2.0 %shard_map.168.own_total = f32[256,512]{1,0:T(8,128)S(1)} custom-call(f32[4,256,128]{2,1,0:T(8,128)S(1)} %bitcast.29, f32[3,256,128]{2,1,0:T(8,128)S(1)} %bitcast.32, bf16[512,768]{1,0:T(8,128)(2,1)S(1)} %copy-done.2, bf16[256,1536]{1,0:T(8,128)(2,1)S(1)} %copy-done.3, bf16[768,256]{1,0:T(8,128)(2,1)S(1)} %copy-done.9, bf16[768,256]{1,0:T(8,128)(2,1)S(1)} %copy-done.10), custom_call_target="tpu_custom_call" | custom-call | flops 1207959552 | bytes 2000000 | tf_op jit(solution)/shard_map/pallas_call | solution.py:330
  16.6 0.0 copy-start.11
  16.6 0.7 copy.21
  17.3 0.1 copy.20
  17.4 0.0 copy-done.16
  17.4 0.0 copy-start.6
  17.5 0.1 copy-done.11
  17.6 0.7 copy-done.6
  18.4 2.2 %shard_map.169 = (f32[3,256,256]{2,1,0:T(8,128)S(1)}, f32[256,768]{1,0:T(8,128)S(1)}, f32[256,384]{1,0:T(8,128)S(1)}, f32[16,1152]{1,0:T(8,128)S(1)}, f32[16,1152]{1,0:T(8,128)S(1)}) custom-call(f32[2,256,128]{2,1,0:T(8,128)S(1)} %collective-permute-done.left, f32[2,256,128]{2,1,0:T(8,128)S(1)} %collective-permute-done.1.right, ...), custom_call_target="tpu_custom_call" | custom-call | flops 603979776 | bytes 2000000 | tf_op jit(solution)/shard_map/pallas_call | solution.py:330
  20.5 1.3 %collective-permute-start.2 = (f32[16,1152]{1,0:T(8,128)S(1)}, f32[16,1152]{1,0:T(8,128)S(1)}, u32[]{:S(2)}, u32[]{:S(2)}) collective-permute-start(f32[16,1152]{1,0:T(8,128)S(1)} %get-tuple-element.25), channel_id=1, source_target_pairs={{0,16},{16,32},{32,48},{48,64},{64,80},{80,96},{96,112},{112,128},... | collective-permute-start | bytes 221192 | tf_op jit(solution)/shard_map/ppermute | solution.py:360
  21.8 1.3 %collective-permute-start.3 = (f32[16,1152]{1,0:T(8,128)S(1)}, f32[16,1152]{1,0:T(8,128)S(1)}, u32[]{:S(2)}, u32[]{:S(2)}) collective-permute-start(f32[16,1152]{1,0:T(8,128)S(1)} %get-tuple-element.26), channel_id=1, source_target_pairs={{16,0},{32,16},{48,32},{64,48},{80,64},{96,80},{112,96},{128,112},... | collective-permute-start | bytes 221192 | tf_op jit(solution)/shard_map/ppermute | solution.py:360
  23.2 0.1 collective-permute-done.2.got_low
  23.2 3.7 %collective-permute-done.3.got_high = f32[16,1152]{1,0:T(8,128)S(1)} collective-permute-done((f32[16,1152]{1,0:T(8,128)S(1)}, f32[16,1152]{1,0:T(8,128)S(1)}, u32[]{:S(2)}, u32[]{:S(2)}) %collective-permute-start.3) | collective-permute-done | bytes 73760 | tf_op jit(solution)/shard_map/ppermute | solution.py:360
  26.9 3.1 %shard_map.170 = (f32[256,768]{1,0:T(8,128)S(1)}, f32[256,384]{1,0:T(8,128)S(1)}, f32[16,768]{1,0:T(8,128)S(1)}, f32[16,768]{1,0:T(8,128)S(1)}) custom-call(f32[4,256,128]{2,1,0:T(8,128)S(1)} %bitcast.30, f32[2,256,128]{2,1,0:T(8,128)S(1)} %collective-permute-done.left, f32[2,256,128]{2,1,0:T(8,128)S(1)} %collective-permute-done.1.right, ...), custom_call_target="tpu_custom_call" | custom-call | flops 1811939328 | bytes 2000000 | tf_op jit(solution)/shard_map/pallas_call | solution.py:330
  30.0 3.5 %collective-permute-start.4 = (f32[16,768]{1,0:T(8,128)S(1)}, f32[16,768]{1,0:T(8,128)S(1)}, u32[]{:S(2)}, u32[]{:S(2)}) collective-permute-start(f32[16,768]{1,0:T(8,128)S(1)} %get-tuple-element.30), channel_id=1, source_target_pairs={{0,16},{16,32},{32,48},{48,64},{64,80},{80,96},{96,112},{112,128},... | collective-permute-start | bytes 147464 | tf_op jit(solution)/shard_map/ppermute | solution.py:360
  33.6 1.3 %collective-permute-start.5 = (f32[16,768]{1,0:T(8,128)S(1)}, f32[16,768]{1,0:T(8,128)S(1)}, u32[]{:S(2)}, u32[]{:S(2)}) collective-permute-start(f32[16,768]{1,0:T(8,128)S(1)} %get-tuple-element.31), channel_id=1, source_target_pairs={{16,0},{32,16},{48,32},{64,48},{80,64},{96,80},{112,96},{128,112},... | collective-permute-start | bytes 147464 | tf_op jit(solution)/shard_map/ppermute | solution.py:360
  35.0 0.6 copy-done.17
  35.6 0.0 copy-done.18
  35.6 0.1 fusion.1.slab
  35.7 4.3 %collective-permute-done.5.got_high = f32[16,768]{1,0:T(8,128)S(1)} collective-permute-done((f32[16,768]{1,0:T(8,128)S(1)}, f32[16,768]{1,0:T(8,128)S(1)}, u32[]{:S(2)}, u32[]{:S(2)}) %collective-permute-start.5) | collective-permute-done | bytes 49184 | tf_op jit(solution)/shard_map/ppermute | solution.py:360
  40.0 3.0 %shard_map.171 = (f32[256,768]{1,0:T(8,128)S(1)}, f32[16,768]{1,0:T(8,128)S(1)}, f32[16,768]{1,0:T(8,128)S(1)}) custom-call(f32[256,768]{1,0:T(8,128)S(1)} %get-tuple-element.28.state, f32[256,384]{1,0:T(8,128)S(1)} %get-tuple-element.29.inverse_ref, f32[16,768]{1,0:T(8,128)S(1)} %collective-permute-done.4.got_low, ...), custom_call_target="tpu_custom_call" | custom-call | flops 1811939328 | bytes 2000000 | tf_op jit(solution)/shard_map/pallas_call | solution.py:330
  43.0 4.6 %collective-permute-start.6 = (f32[16,768]{1,0:T(8,128)S(1)}, f32[16,768]{1,0:T(8,128)S(1)}, u32[]{:S(2)}, u32[]{:S(2)}) collective-permute-start(f32[16,768]{1,0:T(8,128)S(1)} %get-tuple-element.33), channel_id=1, source_target_pairs={{0,16},{16,32},{32,48},{48,64},{64,80},{80,96},{96,112},{112,128},... | collective-permute-start | bytes 147464 | tf_op jit(solution)/shard_map/ppermute | solution.py:360
  47.6 1.5 %collective-permute-start.7 = (f32[16,768]{1,0:T(8,128)S(1)}, f32[16,768]{1,0:T(8,128)S(1)}, u32[]{:S(2)}, u32[]{:S(2)}) collective-permute-start(f32[16,768]{1,0:T(8,128)S(1)} %get-tuple-element.34), channel_id=1, source_target_pairs={{16,0},{32,16},{48,32},{64,48},{80,64},{96,80},{112,96},{128,112},... | collective-permute-start | bytes 147464 | tf_op jit(solution)/shard_map/ppermute | solution.py:360
  49.1 3.3 %collective-permute-done.7.got_high = f32[16,768]{1,0:T(8,128)S(1)} collective-permute-done((f32[16,768]{1,0:T(8,128)S(1)}, f32[16,768]{1,0:T(8,128)S(1)}, u32[]{:S(2)}, u32[]{:S(2)}) %collective-permute-start.7) | collective-permute-done | bytes 49184 | tf_op jit(solution)/shard_map/ppermute | solution.py:360
  52.5 3.0 %shard_map.172 = (f32[256,768]{1,0:T(8,128)S(1)}, f32[16,768]{1,0:T(8,128)S(1)}, f32[16,768]{1,0:T(8,128)S(1)}) custom-call(f32[256,768]{1,0:T(8,128)S(1)} %get-tuple-element.32.state, f32[256,384]{1,0:T(8,128)S(1)} %get-tuple-element.29.inverse_ref, f32[16,768]{1,0:T(8,128)S(1)} %collective-permute-done.6.got_low, ...), custom_call_target="tpu_custom_call" | custom-call | flops 1811939328 | bytes 2000000 | tf_op jit(solution)/shard_map/pallas_call | solution.py:330
  55.5 3.4 %collective-permute-start.8 = (f32[16,768]{1,0:T(8,128)S(1)}, f32[16,768]{1,0:T(8,128)S(1)}, u32[]{:S(2)}, u32[]{:S(2)}) collective-permute-start(f32[16,768]{1,0:T(8,128)S(1)} %get-tuple-element.36), channel_id=1, source_target_pairs={{0,16},{16,32},{32,48},{48,64},{64,80},{80,96},{96,112},{112,128},... | collective-permute-start | bytes 147464 | tf_op jit(solution)/shard_map/ppermute | solution.py:360
  58.9 1.3 %collective-permute-start.9 = (f32[16,768]{1,0:T(8,128)S(1)}, f32[16,768]{1,0:T(8,128)S(1)}, u32[]{:S(2)}, u32[]{:S(2)}) collective-permute-start(f32[16,768]{1,0:T(8,128)S(1)} %get-tuple-element.37), channel_id=1, source_target_pairs={{16,0},{32,16},{48,32},{64,48},{80,64},{96,80},{112,96},{128,112},... | collective-permute-start | bytes 147464 | tf_op jit(solution)/shard_map/ppermute | solution.py:360
  60.2 0.1 bitcast_select_fusion.1.girth_weight
  60.3 3.4 %collective-permute-done.9.got_high = f32[16,768]{1,0:T(8,128)S(1)} collective-permute-done((f32[16,768]{1,0:T(8,128)S(1)}, f32[16,768]{1,0:T(8,128)S(1)}, u32[]{:S(2)}, u32[]{:S(2)}) %collective-permute-start.9) | collective-permute-done | bytes 49184 | tf_op jit(solution)/shard_map/ppermute | solution.py:360
  63.8 1.7 %shard_map.173 = (f32[4,256,128]{2,1,0:T(8,128)}, f32[32,64,128]{2,1,0:T(8,128)}) custom-call(f32[256,768]{1,0:T(8,128)S(1)} %get-tuple-element.35.state, f32[256,384]{1,0:T(8,128)S(1)} %get-tuple-element.29.inverse_ref, f32[16,768]{1,0:T(8,128)S(1)} %collective-permute-done.8.got_low, f32[16,768]{1,0:T(8,128)S(1)} %collective-permute-done.9.got_high, ...), custom_call_target="tpu_custom_call" | custom-call | flops 603979776 | bytes 2000000 | tf_op jit(solution)/shard_map/pallas_call | solution.py:330
  65.5 10.7 %all-to-all-start = ((f32[32,64,128]{2,1,0:T(8,128)}), f32[32,64,128]{2,1,0:T(8,128)S(1)}, u32[]{:S(2)}, u32[]{:S(2)}) async-start(f32[32,64,128]{2,1,0:T(8,128)} %get-tuple-element.39), calls=%async_computation | async-start | bytes 2097152 | tf_op jit(solution)/shard_map/all_to_all | solution.py:441
  76.2 0.0 copy-start
  76.2 0.8 dynamic-slice_bitcast_fusion.phase
  77.0 18.6 %all-to-all-done = f32[32,64,128]{2,1,0:T(8,128)S(1)} async-done(((f32[32,64,128]{2,1,0:T(8,128)}), f32[32,64,128]{2,1,0:T(8,128)S(1)}, u32[]{:S(2)}, u32[]{:S(2)}) %all-to-all-start) | async-done | bytes 1048608 | tf_op jit(solution)/shard_map/all_to_all | solution.py:441
  95.6 0.1 reduce_sum.9
  95.7 29.4 %all-gather = f32[1024,128]{1,0:T(8,128)S(1)} all-gather(f32[64,128]{1,0:T(8,128)S(1)} %reduce_sum.9), channel_id=2, replica_groups=mesh['axial'=32,'girth'=16] {'girth'}, dimensions={0}, use_global_device_ids=true | all-gather | bytes 557056 | tf_op jit(solution)/shard_map/all_gather | solution.py:442
  125.0 1.2 shard_map.174
  (36 shorter events, 0.2 us)
Async XLA Ops:
  0.6 11.8 %copy-start.2 = (bf16[512,768]{1,0:T(8,128)(2,1)S(1)}, bf16[512,768]{1,0:T(8,128)(2,1)}, u32[]{:S(2)}) copy-start(bf16[512,768]{1,0:T(8,128)(2,1)} %constant.86.clone.refs_0_) | copy-start | bytes 2359300
  0.6 1.0 copy-start.5
  1.6 1.0 copy-start.7
  2.7 1.0 copy-start.12
  3.7 8.8 %copy-start.9 = (bf16[768,256]{1,0:T(8,128)(2,1)S(1)}, bf16[768,256]{1,0:T(8,128)(2,1)}, u32[]{:S(2)}) copy-start(bf16[768,256]{1,0:T(8,128)(2,1)} %constant.88.clone.refs_2_) | copy-start | bytes 1179652
  4.8 12.7 %collective-permute-start = (f32[2,256,128]{2,1,0:T(8,128)}, f32[2,256,128]{2,1,0:T(8,128)S(1)}, u32[]{:S(2)}, u32[]{:S(2)}) collective-permute-start(f32[2,256,128]{2,1,0:T(8,128)} %get-tuple-element.21), channel_id=1, source_target_pairs={{0,1},{1,2},{2,3},{3,4},{4,5},{5,6},{6,7},{7,8},{8,9},{9,10},{10,1... | collective-permute-start | bytes 786440 | tf_op jit(solution)/shard_map/ppermute | solution.py:355
  7.5 10.0 %collective-permute-start.1 = (f32[2,256,128]{2,1,0:T(8,128)}, f32[2,256,128]{2,1,0:T(8,128)S(1)}, u32[]{:S(2)}, u32[]{:S(2)}) collective-permute-start(f32[2,256,128]{2,1,0:T(8,128)} %get-tuple-element.22), channel_id=1, source_target_pairs={{1,0},{2,1},{3,2},{4,3},{5,4},{6,5},{7,6},{8,7},{9,8},{10,9},{11,1... | collective-permute-start | bytes 786440 | tf_op jit(solution)/shard_map/ppermute | solution.py:356
  12.4 1.1 copy-start.3
  13.6 1.0 copy-start.10
  14.6 2.8 %copy-start.16 = (s32[64]{0:T(128)S(1)}, s32[64]{0:T(128)}, u32[]{:S(2)}) copy-start(s32[64]{0:T(128)} %param.19) | copy-start | bytes 772
  14.6 2.9 %copy-start.4 = (bf16[256,1536]{1,0:T(8,128)(2,1)S(1)}, bf16[256,1536]{1,0:T(8,128)(2,1)}, u32[]{:S(2)}) copy-start(bf16[256,1536]{1,0:T(8,128)(2,1)} %constant.87.clone.refs_1_) | copy-start | bytes 2359300
  16.6 1.0 copy-start.11
  17.4 0.9 copy-start.6
  17.5 9.5 %copy-start.8 = (f32[4,16,16,128]{3,2,1,0:T(8,128)S(1)}, f32[4,16,16,128]{3,2,1,0:T(8,128)}, u32[]{:S(2)}) copy-start(f32[4,16,16,128]{3,2,1,0:T(8,128)} %param.16) | copy-start | bytes 1572868
  17.5 9.5 %copy-start.13 = (f32[3,16,16,128]{3,2,1,0:T(8,128)S(1)}, f32[3,16,16,128]{3,2,1,0:T(8,128)}, u32[]{:S(2)}) copy-start(f32[3,16,16,128]{3,2,1,0:T(8,128)} %param.17) | copy-start | bytes 1179652
  20.5 2.7 %collective-permute-start.2 = (f32[16,1152]{1,0:T(8,128)S(1)}, f32[16,1152]{1,0:T(8,128)S(1)}, u32[]{:S(2)}, u32[]{:S(2)}) collective-permute-start(f32[16,1152]{1,0:T(8,128)S(1)} %get-tuple-element.25), channel_id=1, source_target_pairs={{0,16},{16,32},{32,48},{48,64},{64,80},{80,96},{96,112},{112,128},... | collective-permute-start | bytes 221192 | tf_op jit(solution)/shard_map/ppermute | solution.py:360
  21.8 5.1 %collective-permute-start.3 = (f32[16,1152]{1,0:T(8,128)S(1)}, f32[16,1152]{1,0:T(8,128)S(1)}, u32[]{:S(2)}, u32[]{:S(2)}) collective-permute-start(f32[16,1152]{1,0:T(8,128)S(1)} %get-tuple-element.26), channel_id=1, source_target_pairs={{16,0},{32,16},{48,32},{64,48},{80,64},{96,80},{112,96},{128,112},... | collective-permute-start | bytes 221192 | tf_op jit(solution)/shard_map/ppermute | solution.py:360
  30.0 4.9 %copy-start.14 = (f32[64,256]{1,0:T(8,128)S(1)}, f32[64,256]{1,0:T(8,128)}, u32[]{:S(2)}) copy-start(f32[64,256]{1,0:T(8,128)} %copy.21) | copy-start | bytes 196612
  30.0 5.7 %collective-permute-start.4 = (f32[16,768]{1,0:T(8,128)S(1)}, f32[16,768]{1,0:T(8,128)S(1)}, u32[]{:S(2)}, u32[]{:S(2)}) collective-permute-start(f32[16,768]{1,0:T(8,128)S(1)} %get-tuple-element.30), channel_id=1, source_target_pairs={{0,16},{16,32},{32,48},{48,64},{64,80},{80,96},{96,112},{112,128},... | collective-permute-start | bytes 147464 | tf_op jit(solution)/shard_map/ppermute | solution.py:360
  33.6 6.4 %collective-permute-start.5 = (f32[16,768]{1,0:T(8,128)S(1)}, f32[16,768]{1,0:T(8,128)S(1)}, u32[]{:S(2)}, u32[]{:S(2)}) collective-permute-start(f32[16,768]{1,0:T(8,128)S(1)} %get-tuple-element.31), channel_id=1, source_target_pairs={{16,0},{32,16},{48,32},{64,48},{80,64},{96,80},{112,96},{128,112},... | collective-permute-start | bytes 147464 | tf_op jit(solution)/shard_map/ppermute | solution.py:360
  34.9 0.7 copy-start.17
  34.9 0.7 copy-start.18
  43.0 6.1 %collective-permute-start.6 = (f32[16,768]{1,0:T(8,128)S(1)}, f32[16,768]{1,0:T(8,128)S(1)}, u32[]{:S(2)}, u32[]{:S(2)}) collective-permute-start(f32[16,768]{1,0:T(8,128)S(1)} %get-tuple-element.33), channel_id=1, source_target_pairs={{0,16},{16,32},{32,48},{48,64},{64,80},{80,96},{96,112},{112,128},... | collective-permute-start | bytes 147464 | tf_op jit(solution)/shard_map/ppermute | solution.py:360
  47.6 4.8 %collective-permute-start.7 = (f32[16,768]{1,0:T(8,128)S(1)}, f32[16,768]{1,0:T(8,128)S(1)}, u32[]{:S(2)}, u32[]{:S(2)}) collective-permute-start(f32[16,768]{1,0:T(8,128)S(1)} %get-tuple-element.34), channel_id=1, source_target_pairs={{16,0},{32,16},{48,32},{64,48},{80,64},{96,80},{112,96},{128,112},... | collective-permute-start | bytes 147464 | tf_op jit(solution)/shard_map/ppermute | solution.py:360
  52.5 7.8 %copy-start.15 = (f32[8,128]{1,0:T(8,128)S(1)}, f32[8,128]{1,0:T(8,128)}, u32[]{:S(2)}) copy-start(f32[8,128]{1,0:T(8,128)} %param.24) | copy-start | bytes 12292
  55.5 4.7 %copy-start.19 = (s32[128]{0:T(128)S(1)}, s32[128]{0:T(128)}, u32[]{:S(2)}) copy-start(s32[128]{0:T(128)} %param.23) | copy-start | bytes 1540
  55.5 4.8 %collective-permute-start.8 = (f32[16,768]{1,0:T(8,128)S(1)}, f32[16,768]{1,0:T(8,128)S(1)}, u32[]{:S(2)}, u32[]{:S(2)}) collective-permute-start(f32[16,768]{1,0:T(8,128)S(1)} %get-tuple-element.36), channel_id=1, source_target_pairs={{0,16},{16,32},{32,48},{48,64},{64,80},{80,96},{96,112},{112,128},... | collective-permute-start | bytes 147464 | tf_op jit(solution)/shard_map/ppermute | solution.py:360
  58.9 4.8 %collective-permute-start.9 = (f32[16,768]{1,0:T(8,128)S(1)}, f32[16,768]{1,0:T(8,128)S(1)}, u32[]{:S(2)}, u32[]{:S(2)}) collective-permute-start(f32[16,768]{1,0:T(8,128)S(1)} %get-tuple-element.37), channel_id=1, source_target_pairs={{16,0},{32,16},{48,32},{64,48},{80,64},{96,80},{112,96},{128,112},... | collective-permute-start | bytes 147464 | tf_op jit(solution)/shard_map/ppermute | solution.py:360
  65.5 59.6 %copy-start.1 = (bf16[2048,256]{1,0:T(8,128)(2,1)S(1)}, bf16[2048,256]{1,0:T(8,128)(2,1)}, u32[]{:S(2)}) copy-start(bf16[2048,256]{1,0:T(8,128)(2,1)} %constant.92.clone.table_low) | copy-start | bytes 3145732
  65.5 30.1 %all-to-all-start = ((f32[32,64,128]{2,1,0:T(8,128)}), f32[32,64,128]{2,1,0:T(8,128)S(1)}, u32[]{:S(2)}, u32[]{:S(2)}) async-start(f32[32,64,128]{2,1,0:T(8,128)} %get-tuple-element.39), calls=%async_computation | async-start | bytes 2097152 | tf_op jit(solution)/shard_map/all_to_all | solution.py:441
  76.2 48.9 %copy-start = (bf16[2048,256]{1,0:T(8,128)(2,1)S(1)}, bf16[2048,256]{1,0:T(8,128)(2,1)}, u32[]{:S(2)}) copy-start(bf16[2048,256]{1,0:T(8,128)(2,1)} %constant.91.clone.table_high) | copy-start | bytes 3145732

commit v2 on v1

--- a/solution.py
+++ b/solution.py
@@ -16,6 +16,7 @@
 NODES = 256
 WIDE = 6 * LANES
 ROWS_DEV = 16
+SLOTS = 8
 F32 = jnp.float32
 BF16 = jnp.bfloat16
 
@@ -80,11 +81,16 @@
     radial = np.kron(np.kron(eye(2), d), eye(16))
     axial = np.kron(eye(32), d)
     slope = np.concatenate([radial, axial], axis=0)
+    ends = np.tile(np.concatenate([d[:, 0], d[:, 7]]), 16)[:, None]
     return (
         left_operand(slope),
         left_operand(slope.T),
         right_operand(axial.T),
         right_operand(axial),
+        left_operand(axial.T),
+        left_operand(np.kron(eye(4), d)),
+        left_operand(np.kron(eye(8), d.T)),
+        np.ascontiguousarray(np.broadcast_to(ends, (NODES, LANES))),
     )
 
 
@@ -121,7 +127,7 @@
 
 
 def stiff(u, gr, ga, gg, tables):
-    slope_l, slope_t, girth, girth_t = tables
+    slope_l, slope_t, girth, girth_t = tables[:4]
     ra = left_mul(slope_l[...], u)
     g = right_mul(u, girth[...])
     y = jnp.concatenate([ra[:NODES] * gr, ra[NODES:] * ga], axis=0)
@@ -174,7 +180,17 @@
     return x[:, k * LANES : (k + 1) * LANES]
 
 
-def pack_kernel(field, geom, mass, to_right, to_left):
+def load_kernel(count, *refs):
+    sources, targets = refs[:count], refs[count : 2 * count]
+    to_right, to_left, sems = refs[2 * count :]
+    copies = []
+    for k in range(count):
+        copy = pltpu.make_async_copy(sources[k], targets[k], sems.at[k])
+        copy.start()
+        copies.append(copy)
+    for copy in copies[:3]:
+        copy.wait()
+    field, geom, mass = targets[:3]
     lane = lax.broadcasted_iota(jnp.int32, (NODES, LANES), 1)
 
     def pack(arrays, start):
@@ -190,25 +206,71 @@
     to_right[1] = pack(others, LANES - HALO)
     to_left[0] = pack(fields, 0)
     to_left[1] = pack(others, 0)
+    for copy in copies[3:]:
+        copy.wait()
 
 
 def own_kernel(field, geom, *refs):
-    tables, out = refs[:4], refs[4]
+    tables, out = refs[:-1], refs[-1]
     gr, ga, gg = [twice(geom[k]) for k in range(3)]
     for pair in range(2):
         u = jnp.concatenate([field[2 * pair], field[2 * pair + 1]], axis=1)
         out[:, 2 * pair * LANES : (2 * pair + 2) * LANES] = stiff(u, gr, ga, gg, tables)
 
 
-def faces(total, low, high, offset):
-    width = total.shape[2]
-    low[:, offset : offset + width] = total[:, 0, :]
-    high[:, offset : offset + width] = total[:, 15, :]
-
-
-def halo_kernel(left, right, own_total, mass, *refs):
-    tables = refs[:4]
-    halo_geom, total_out, mass_out, low, high = refs[4:]
+def at_faces(low, high, width):
+    shape = (16, 16, width)
+    node = lax.broadcasted_iota(jnp.int32, shape, 1)
+    both = jnp.where(
+        node == 0, low[:, None, :], jnp.where(node == 15, high[:, None, :], 0.0)
+    )
+    return both.reshape(NODES, width)
+
+
+def wide(x):
+    own = lanes_of(x, 0)
+    return jnp.concatenate([own] * C + [x[:, LANES:]], axis=1)
+
+
+def put_faces(x, low, high, offset):
+    width = x.shape[1]
+    v = x.reshape(16, 16, width)
+    low[:, offset : offset + width] = v[:, 0, :]
+    high[:, offset : offset + width] = v[:, 15, :]
+
+
+def action(u, geom, halo_geom, tables):
+    gr, ga, gg = [twice(geom[k]) for k in range(3)]
+    parts = []
+    for tile in range(3):
+        if tile == 2:
+            gr, ga, gg = [halo_geom[k] for k in range(3)]
+        t = stiff(u[:, 2 * tile * LANES : (2 * tile + 2) * LANES], gr, ga, gg, tables)
+        parts += [lanes_of(t, 0), lanes_of(t, 1)]
+    return sum_nodes(shared_local(parts)).reshape(NODES, WIDE)
+
+
+def inner_update(u, total, inverse):
+    row = lax.broadcasted_iota(jnp.int32, u.shape, 0) % 16
+    return jnp.where((row == 0) | (row == 15), u, u - total * wide(inverse))
+
+
+def two_steps(u, geom, halo_geom, inverse, first, tables, state, second, low, high):
+    v = inner_update(u, first, inverse)
+    state[...] = v
+    total = action(v, geom, halo_geom, tables)
+    second[...] = total
+    put_faces(first, low, high, 0)
+    put_faces(total, low, high, WIDE)
+
+
+STATIC = 2 * WIDE
+NARROW = 3 * LANES
+
+
+def halo_kernel(left, right, own_total, field, mass, geom, *refs):
+    tables = refs[:8]
+    halo_geom, state, second, mass_out, ends_out, low, high = refs[8:]
     lane = lax.broadcasted_iota(jnp.int32, (NODES, LANES), 1)
 
     def spread(x, k):
@@ -225,66 +287,112 @@
     u = jnp.concatenate([left[0], right[0]], axis=1)
     t = stiff(u, *geoms, tables)
     parts = [own_total[:, c * LANES : (c + 1) * LANES] for c in range(C)]
-    total = sum_nodes(shared_local(parts + [lanes_of(t, 0), lanes_of(t, 1)]))
-    total_out[...] = total.reshape(NODES, WIDE)
-    faces(total, low, high, 0)
+    first = sum_nodes(shared_local(parts + [lanes_of(t, 0), lanes_of(t, 1)]))
+    first = first.reshape(NODES, WIDE)
     m = mass[...]
     masses = sum_girth([m], spread(left_others, 3), spread(right_others, 3), [m] * C)
-    lumped = sum_nodes(jnp.concatenate(masses, axis=1))
-    mass_out[...] = lumped.reshape(NODES, 3 * LANES)
-    faces(lumped, low, high, WIDE)
-
-
-def received(low, high):
-    shape = (16, 16, low.shape[1])
-    node = lax.broadcasted_iota(jnp.int32, shape, 1)
-    both = jnp.where(
-        node == 0, low[:, None, :], jnp.where(node == 15, high[:, None, :], 0.0)
-    )
-    return both.reshape(NODES, low.shape[1])
-
-
-def wide(x):
-    own = lanes_of(x, 0)
-    return jnp.concatenate([own] * C + [x[:, LANES:]], axis=1)
-
-
-def advance(u, inverse, geom, halo_geom, tables, out, low, high):
-    gr, ga, gg = [twice(geom[k]) for k in range(3)]
-    parts = []
+    lumped = sum_nodes(jnp.concatenate(masses, axis=1)).reshape(NODES, NARROW)
+    mass_out[...] = lumped
+    whole = [jnp.concatenate([geom[k], geoms[k]], axis=1) for k in range(3)]
+    end = tables[7][...]
+    ends = left_mul(tables[4][...], whole[1] * jnp.concatenate([end] * 3, axis=1))
+    ends_out[...] = ends
+    for k, x in enumerate([lumped, whole[0], whole[2], ends]):
+        put_faces(x, low, high, STATIC + k * NARROW)
+    start = jnp.concatenate([field[c] for c in range(C)] + [u], axis=1)
+    two_steps(start, geom, halo_geom, 1.0 / lumped, first, tables, state, second, low, high)
+
+
+def static_part(ref, k):
+    return ref[:, STATIC + k * NARROW : STATIC + (k + 1) * NARROW]
+
+
+def finish_pair(state, second, inverse, ends, statics, own, got, tables):
+    low, high, got_low, got_high = statics
+    own_low, own_high = own
+    new_low, new_high = got
+    w_low = -(own_low[:, :WIDE] + new_low[:, :WIDE]) * wide(
+        1.0 / (static_part(low, 0) + static_part(got_low, 0))
+    )
+    w_high = -(own_high[:, :WIDE] + new_high[:, :WIDE]) * wide(
+        1.0 / (static_part(high, 0) + static_part(got_high, 0))
+    )
+    w = jnp.concatenate([w_low, w_high], axis=0)
+    radial, girthwise = [
+        wide(jnp.concatenate([static_part(ref, k) for ref in statics], axis=0)) for k in (1, 2)
+    ]
+    slope = left_mul(tables[5][...], w)
+    face = left_mul(tables[6][...], jnp.concatenate([slope, slope], axis=0) * radial)
+    pieces = []
     for tile in range(3):
-        if tile == 2:
-            gr, ga, gg = [halo_geom[k] for k in range(3)]
-        t = stiff(u[:, 2 * tile * LANES : (2 * tile + 2) * LANES], gr, ga, gg, tables)
-        parts += [lanes_of(t, 0), lanes_of(t, 1)]
-    total = sum_nodes(shared_local(parts))
-    faces(total, low, high, 0)
-    out[...] = u - total.reshape(NODES, WIDE) * wide(inverse)
-
-
-def first_kernel(field, left, right, total, lumped, got_low, got_high, geom, halo_geom, *refs):
-    tables = refs[:4]
-    out, inverse_out, low, high = refs[4:]
-    arrived = received(got_low[...], got_high[...])
-    inverse = 1.0 / (lumped[...] + arrived[:, WIDE:])
+        span = slice(2 * tile * LANES, (2 * tile + 2) * LANES)
+        g = right_mul(w[:, span], tables[2][...])
+        y = jnp.concatenate([g, g], axis=0) * girthwise[:, span]
+        pieces.append(right_mul(y, tables[3][...]))
+    face = face + jnp.concatenate(pieces, axis=1)
+    other = jnp.concatenate([static_part(got_low, 3), static_part(got_high, 3)], axis=0)
+    beyond = face[32:] + wide(other) * w
+    beyond = shared_local([lanes_of(beyond, k) for k in range(6)]).reshape(2, 16, WIDE)
+    pair = beyond[:, 7:8, :] + beyond[:, 8:9, :]
+    node = lax.broadcasted_iota(jnp.int32, beyond.shape, 1)
+    beyond = jnp.where((node == 7) | (node == 8), pair, beyond)
+    beyond_low = beyond[0] + new_low[:, WIDE : 2 * WIDE]
+    beyond_high = beyond[1] + new_high[:, WIDE : 2 * WIDE]
+    node = lax.broadcasted_iota(jnp.int32, (16, 16, WIDE), 1)
+    along = jnp.where(node < P_SIZE, w_low[:, None, :], w_high[:, None, :])
+    change = wide(ends) * along.reshape(NODES, WIDE) + at_faces(face[:16], face[16:32], WIDE)
+    change = sum_nodes(shared_local([lanes_of(change, k) for k in range(6)]))
+    total = second + change.reshape(NODES, WIDE) + at_faces(beyond_low, beyond_high, WIDE)
+    return state + at_faces(w_low, w_high, WIDE) - total * wide(inverse)
+
+
+def middle_kernel(state, second, lumped, ends, low, high, got_low, got_high, geom, halo_geom, *refs):
+    tables = refs[:8]
+    state_out, second_out, inverse_out, next_low, next_high = refs[8:]
+    inverse = 1.0 / (
+        lumped[...] + at_faces(static_part(got_low, 0), static_part(got_high, 0), NARROW)
+    )
     inverse_out[...] = inverse
-    u = jnp.concatenate([field[c] for c in range(C)] + [left[0], right[0]], axis=1)
-    u = u - (total[...] + arrived[:, :WIDE]) * wide(inverse)
-    advance(u, inverse, geom, halo_geom, tables, out, low, high)
-
-
-def step_kernel(state, inverse_ref, got_low, got_high, geom, halo_geom, *refs):
-    tables = refs[:4]
-    out, low, high = refs[4:]
-    inverse = inverse_ref[...]
-    u = state[...] - received(got_low[...], got_high[...]) * wide(inverse)
-    advance(u, inverse, geom, halo_geom, tables, out, low, high)
-
-
-def last_kernel(state, inverse_ref, got_low, got_high, slab, girth_weight, select, out, dense):
-    own = C * LANES
-    inverse = jnp.concatenate([inverse_ref[:, :LANES]] * C, axis=1)
-    u = state[:, :own] - received(got_low[:, :own], got_high[:, :own]) * inverse
+    statics = (low, high, got_low, got_high)
+    u = finish_pair(
+        state[...], second[...], inverse, ends[...], statics, (low, high), (got_low, got_high), tables
+    )
+    first = action(u, geom, halo_geom, tables)
+    two_steps(u, geom, halo_geom, inverse, first, tables, state_out, second_out, next_low, next_high)
+
+
+def last_kernel(
+    state,
+    second,
+    inverse,
+    ends,
+    low,
+    high,
+    got_low,
+    got_high,
+    own_low,
+    own_high,
+    new_low,
+    new_high,
+    slab,
+    girth_weight,
+    select,
+    header,
+    *refs,
+):
+    tables = refs[:8]
+    out, packed, probes_out = refs[8:]
+    u = finish_pair(
+        state[...],
+        second[...],
+        inverse[...],
+        ends[...],
+        (low, high, got_low, got_high),
+        (own_low, own_high),
+        (new_low, new_high),
+        tables,
+    )
+    u = u[:, : C * LANES]
     for c in range(C):
         out[c] = lanes_of(u, c)
     slab_high, slab_low = split(slab[...])
@@ -295,12 +403,37 @@
     probes = right_mul(stacked, weights)
     slots = slab.shape[0]
     spread = jnp.concatenate([probes[c * slots : (c + 1) * slots] for c in range(C)], axis=1)
-    high, low = split(spread)
+    probes_out[...] = spread
+    high_part, low_part = split(spread)
     chosen = select[...].astype(BF16)
-    rows = dot(jnp.concatenate([chosen, chosen], axis=1), jnp.concatenate([high, low], axis=0))
+    rows = dot(
+        jnp.concatenate([chosen, chosen], axis=1),
+        jnp.concatenate([high_part, low_part], axis=0),
+    )
     for c in range(C):
-        dense[:, c * ROWS_DEV : (c + 1) * ROWS_DEV, :] = lanes_of(rows, c).reshape(
-            -1, ROWS_DEV, LANES
+        block = lanes_of(rows, c).reshape(-1, SLOTS, LANES)
+        if c == 0:
+            place = lax.broadcasted_iota(jnp.int32, block.shape, 1)
+            block = jnp.where(place == SLOTS - 1, header[...][:, None, :], block)
+        packed[:, c * SLOTS : (c + 1) * SLOTS, :] = block
+
+
+def unpack_kernel(pieces, out):
+    sources = pieces.shape[0]
+    heads = pieces[:, 0:SLOTS, :]
+    head = jnp.broadcast_to(heads[:, SLOTS - 1 : SLOTS, :], heads.shape)
+    place = lax.broadcasted_iota(jnp.int32, heads.shape, 1)
+    lane = lax.broadcasted_iota(jnp.int32, heads.shape, 2)
+    mine = jnp.where((lane == place) & (place < SLOTS - 1), head, 0.0)
+    row = jnp.sum(mine.reshape(sources * SLOTS, LANES), axis=1, keepdims=True)
+    column = lax.broadcasted_iota(jnp.int32, (sources * SLOTS, LANES), 1).astype(F32)
+    chosen = jnp.transpose(jnp.where(row == column + 1.0, 1.0, 0.0))[:ROWS_DEV].astype(BF16)
+    both = jnp.concatenate([chosen, chosen], axis=1)
+    for c in range(C):
+        x = pieces[:, c * SLOTS : (c + 1) * SLOTS, :].reshape(sources * SLOTS, LANES)
+        high, low = split(x)
+        out[c * ROWS_DEV : (c + 1) * ROWS_DEV, :] = dot(
+            both, jnp.concatenate([high, low], axis=0)
         )
 
 
@@ -337,6 +470,20 @@
     )(*args)
 
 
+def load(*args):
+    halo = jax.ShapeDtypeStruct((2, NODES, LANES), F32)
+    outs = [jax.ShapeDtypeStruct(x.shape, x.dtype) for x in args] + [halo] * 2
+    got = pl.pallas_call(
+        lambda *refs: load_kernel(len(args), *refs),
+        out_shape=outs,
+        in_specs=[pl.BlockSpec(memory_space=pltpu.HBM)] * len(args),
+        out_specs=[pl.BlockSpec(memory_space=pltpu.VMEM)] * len(outs),
+        scratch_shapes=[pltpu.SemaphoreType.DMA((len(args),))],
+        compiler_params=pltpu.CompilerParams(vmem_limit_bytes=40 * 1024 * 1024),
+    )(*args)
+    return got[: len(args)], got[len(args)], got[len(args) + 1]
+
+
 def body(
     field, geometry, mass, cycle_id, cycle_radial, cycle_axial, cycle_weights, az_elem, az_weights
 ):
@@ -345,63 +492,55 @@
     down = [(j, i) for i, j in up]
     around = [(i, (i + 1) % girth_count) for i in range(girth_count)]
     back = [(j, i) for i, j in around]
-    tables = [jnp.asarray(t) for t in stiffness_tables()]
-    field = field.reshape(C, NODES, LANES)
-    geom = geometry.reshape(3, NODES, LANES)
-    mass = mass.reshape(NODES, LANES)
+    loaded, to_right, to_left = load(
+        field.reshape(C, NODES, LANES),
+        geometry.reshape(3, NODES, LANES),
+        mass.reshape(NODES, LANES),
+        *[jnp.asarray(t) for t in stiffness_tables()],
+    )
+    field, geom, mass = loaded[:3]
+    tables = loaded[3:]
     tile_flops = 18 * 2 * 256**3
 
-    to_right, to_left = call(pack_kernel, [(2, NODES, LANES)] * 2, 1000000, field, geom, mass)
     left = lax.ppermute(to_right, "girth", around)
     right = lax.ppermute(to_left, "girth", back)
-    (own_total,) = call(own_kernel, [(NODES, C * LANES)], 2 * tile_flops, field, geom, *tables)
+    (own_total,) = call(own_kernel, [(NODES, C * LANES)], 2 * tile_flops, field, geom, *tables[:4])
 
     def exchange(low, high):
         return lax.ppermute(high, "axial", up), lax.ppermute(low, "axial", down)
 
-    face_wide = (16, WIDE + 3 * LANES)
-    halo_geom, total, lumped, low, high = call(
+    whole, narrow = (NODES, WIDE), (NODES, NARROW)
+    face_static = (16, STATIC + 4 * NARROW)
+    halo_geom, state, second, lumped, ends, low, high = call(
         halo_kernel,
-        [(3, NODES, 2 * LANES), (NODES, WIDE), (NODES, 3 * LANES), face_wide, face_wide],
-        tile_flops,
+        [(3, NODES, 2 * LANES), whole, whole, narrow, narrow, face_static, face_static],
+        4 * tile_flops,
         left,
         right,
         own_total,
+        field,
         mass,
+        geom,
         *tables,
     )
     got_low, got_high = exchange(low, high)
-    face = (16, WIDE)
-    state, inverse, low, high = call(
-        first_kernel,
-        [(NODES, WIDE), (NODES, 3 * LANES), face, face],
-        3 * tile_flops,
-        field,
-        left,
-        right,
-        total,
+    state, second, inverse, own_low, own_high = call(
+        middle_kernel,
+        [whole, whole, narrow, (16, STATIC), (16, STATIC)],
+        6 * tile_flops,
+        state,
+        second,
         lumped,
+        ends,
+        low,
+        high,
         got_low,
         got_high,
         geom,
         halo_geom,
         *tables,
     )
-    for _ in range(2):
-        got_low, got_high = exchange(low, high)
-        state, low, high = call(
-            step_kernel,
-            [(NODES, WIDE), face, face],
-            3 * tile_flops,
-            state,
-            inverse,
-            got_low,
-            got_high,
-            geom,
-            halo_geom,
-            *tables,
-        )
-    got_low, got_high = exchange(low, high)
+    new_low, new_high = exchange(own_low, own_high)
 
     slot_count = cycle_id.shape[0]
     node = jnp.arange(NODES, dtype=jnp.int32)
@@ -423,23 +562,62 @@
         jnp.tile(az_weights, (LANES // P_SIZE, 1)),
         0.0,
     )
-    wanted = jnp.arange(ROWS_DEV * axial_count, dtype=jnp.int32)
-    select = (wanted[:, None] == cycle_id[None, :]).astype(F32)
-
-    final, dense = call(
+    target = jnp.where(cycle_id >= 0, cycle_id // ROWS_DEV, -1)
+    order = jnp.arange(slot_count, dtype=jnp.int32)
+    earlier = (target[:, None] == target[None, :]) & (order[None, :] < order[:, None])
+    rank = jnp.sum(earlier.astype(jnp.int32), axis=1)
+    fits = (cycle_id >= 0) & (rank < SLOTS - 1)
+    position = jnp.where(fits, target * SLOTS + rank, -1)
+    wanted = jnp.arange(SLOTS * axial_count, dtype=jnp.int32)
+    select = (wanted[:, None] == position[None, :]).astype(F32)
+    number = jnp.sum(select * (cycle_id % ROWS_DEV + 1).astype(F32)[None, :], axis=1)
+    overflow = jnp.any((cycle_id >= 0) & (rank >= SLOTS - 1)).astype(F32)
+    header = jnp.concatenate(
+        [
+            number.reshape(axial_count, SLOTS),
+            jnp.broadcast_to(overflow, (axial_count, LANES - SLOTS)),
+        ],
+        axis=1,
+    )
+
+    final, packed, probes = call(
         last_kernel,
-        [(C, NODES, LANES), (axial_count, C * ROWS_DEV, LANES)],
+        [(C, NODES, LANES), (axial_count, C * SLOTS, LANES), (slot_count, C * LANES)],
         tile_flops,
         state,
+        second,
         inverse,
+        ends,
+        low,
+        high,
         got_low,
         got_high,
+        own_low,
+        own_high,
+        new_low,
+        new_high,
         slab,
         girth_weight,
         select,
-    )
-    pieces = lax.all_to_all(dense, "axial", 0, 0)
-    rows = lax.all_gather(jnp.sum(pieces, axis=0), "girth")
+        header,
+        *tables,
+    )
+    pieces = lax.all_to_all(packed, "axial", 0, 0)
+
+    def compact(pieces, probes, cycle_id):
+        return call(unpack_kernel, [(C * ROWS_DEV, LANES)], tile_flops, pieces)[0]
+
+    def dense(pieces, probes, cycle_id):
+        wanted = jnp.arange(ROWS_DEV * axial_count, dtype=jnp.int32)
+        chosen = (wanted[:, None] == cycle_id[None, :]).astype(F32)
+        rows = jnp.dot(chosen, probes, precision=lax.Precision.HIGHEST)
+        rows = rows.reshape(axial_count, ROWS_DEV, C * LANES)
+        rows = jnp.sum(lax.all_to_all(rows, "axial", 0, 0), axis=0)
+        return rows.reshape(ROWS_DEV, C, LANES).swapaxes(0, 1).reshape(C * ROWS_DEV, LANES)
+
+    crowded = jnp.max(pieces[:, SLOTS - 1, SLOTS]) > 0.5
+    rows = lax.cond(crowded, dense, compact, pieces, probes, cycle_id)
+    rows = lax.all_gather(rows, "girth")
     table_high, table_low, phases = dft_tables()
     phase = lax.dynamic_index_in_dim(
         jnp.asarray(phases), lax.axis_index("girth"), 0, keepdims=False

time: 127 us -> 135 us (1.063)
  local copies, waits for them, and re-layouts: 8.98 us -> 33.3 us
  waiting for transfers between devices: 33.5 us -> 19.4 us
  starting transfers between devices: 35.7 us -> 27 us
  Pallas kernels: 17.4 us -> 23.4 us
  blocking collectives: 29.4 us -> 25.9 us
  other arithmetic: 0.27 us -> 2.38 us
  between operations: 1 us -> 2.43 us
    unnamed x40 -> x118, local copies, waits for them, and re-layouts: 6.69 us -> 28.8 us
    ppermute x8 -> x4, starting transfers between devices: 18.2 us -> 9.44 us  [exchange(): return (lax.ppermute(high, 'axial', up), lax.ppermute(low, 'axial', down))]
    all_to_all x1, waiting for transfers between devices: 18.6 us -> 11.1 us  [body(): pieces = lax.all_to_all(packed, 'axial', 0, 0)]
    ppermute x8 -> x4, waiting for transfers between devices: 14.9 us -> 8.36 us  [exchange(): return (lax.ppermute(high, 'axial', up), lax.ppermute(low, 'axial', down))]
    all_gather x1, blocking collectives: 29.4 us -> 25.9 us  [body(): rows = lax.all_gather(rows, 'girth')]
    pallas_call x8 -> x6, Pallas kernels: 17.4 us -> 20.6 us  [call(): pl.pallas_call(kernel, out_shape=out_shape, in_specs=[vmem] * len(args),...]
    pallas_call x0 -> x1, Pallas kernels: none -> 2.83 us  [load(): pl.pallas_call(lambda *refs: load_kernel(len(args), *refs), out_shape=out...]
    another operation x2, local copies, waits for them, and re-layouts: 0.73 us -> 2.26 us  [body(): jnp.tile(cycle_weights[1].T, (1, NODES // P_SIZE))]
  transfers between devices with their start and end apart: 11 -> 7, of which waited for: 6 -> 4; matrix products, arithmetic and copies ran while one was open for 2% -> 5% of each run, Pallas kernels for 2% -> 2%
where the time goes in v2:
time: 135 us; the launch traced here: 134 us
  local copies, waits for them, and re-layouts  33.3 us (25%)
  starting transfers between devices  27 us (20%)
  blocking collectives  25.9 us (19%)
  Pallas kernels  23.4 us (17%)
  waiting for transfers between devices  19.4 us (14%)
  between operations  2.43 us (2%)
  other arithmetic  2.38 us (2%)
    unnamed x118, local copies, waits for them, and re-layouts  28.8 us
    all_gather x1, blocking collectives, body(): rows = lax.all_gather(rows, 'girth')  25.9 us
    pallas_call x6, Pallas kernels, call(): pl.pallas_call(kernel, out_shape=out_shape, in_specs=[vmem] * len(args),...  20.6 us
    all_to_all x1, waiting for transfers between devices, body(): pieces = lax.all_to_all(packed, 'axial', 0, 0)  11.1 us
    all_to_all x1, starting transfers between devices, body(): pieces = lax.all_to_all(packed, 'axial', 0, 0)  10.6 us
    ppermute x4, starting transfers between devices, exchange(): return (lax.ppermute(high, 'axial', up), lax.ppermute(low, 'axial', down))  9.44 us
    ppermute x4, waiting for transfers between devices, exchange(): return (lax.ppermute(high, 'axial', up), lax.ppermute(low, 'axial', down))  8.36 us
    ppermute x1, starting transfers between devices, body(): right = lax.ppermute(to_left, 'girth', back)  4.23 us
  transfers between devices with their start and end apart: 7, of which 4 were waited for; matrix products, arithmetic and copies ran while one was open for 5% of the time, Pallas kernels for 2%

profile of v2, /device:TPU:1, one launch (start us, length us, event | category | flops | bytes accessed | tf_op | source)
XLA Modules:
  0.0 133.8 jit_solution(446536080746484328)
XLA Ops:
  1.3 1.1 copy-done.2
  2.5 1.1 copy-done.3
  3.6 1.0 copy-done.4
  4.6 1.0 copy-done.19
  5.6 1.0 copy-done.20
  6.6 1.0 copy-done.21
  7.6 1.0 copy-done.22
  8.6 0.9 copy-done.31
  9.5 0.9 copy-done.32
  10.4 0.8 copy-done.36
  11.2 2.8 %shard_map.203 = (f32[4,256,128]{2,1,0:T(8,128)S(1)}, f32[3,256,128]{2,1,0:T(8,128)S(1)}, f32[256,128]{1,0:T(8,128)S(1)}, bf16[512,768]{1,0:T(8,128)(2,1)S(1)}, ...) custom-call(f32[4,256,128]{2,1,0:T(8,128)S(1)} %bitcast.30, ...), custom_call_target="tpu_custom_call" | custom-call | tf_op jit(solution)/shard_map/pallas_call | solution.py:476
  14.7 2.7 %collective-permute-start = (f32[2,256,128]{2,1,0:T(8,128)}, f32[2,256,128]{2,1,0:T(8,128)}, u32[]{:S(2)}, u32[]{:S(2)}) collective-permute-start(f32[2,256,128]{2,1,0:T(8,128)} %get-tuple-element.40), channel_id=1, source_target_pairs={{0,1},{1,2},{2,3},{3,4},{4,5},{5,6},{6,7},{7,8},{8,9},{9,10},{10,1... | collective-permute-start | bytes 786440 | tf_op jit(solution)/shard_map/ppermute | solution.py:505
  17.4 4.2 %collective-permute-start.1 = (f32[2,256,128]{2,1,0:T(8,128)}, f32[2,256,128]{2,1,0:T(8,128)}, u32[]{:S(2)}, u32[]{:S(2)}) collective-permute-start(f32[2,256,128]{2,1,0:T(8,128)} %get-tuple-element.41), channel_id=1, source_target_pairs={{1,0},{2,1},{3,2},{4,3},{5,4},{6,5},{7,6},{8,7},{9,8},{10,9},{11,1... | collective-permute-start | bytes 786440 | tf_op jit(solution)/shard_map/ppermute | solution.py:506
  23.2 2.0 %shard_map.204.own_total = f32[256,512]{1,0:T(8,128)S(1)} custom-call(f32[4,256,128]{2,1,0:T(8,128)S(1)} %get-tuple-element.42.field, f32[3,256,128]{2,1,0:T(8,128)S(1)} %get-tuple-element.43.geom, bf16[512,768]{1,0:T(8,128)(2,1)S(1)} %get-tuple-element.44.refs_0_, bf16[256,1536]{1,0:T(8,128)(2,1)S(1)} %get-tuple-element.45.refs_1_, ...), custom_call_target="tpu_custom_call" | custom-call | flops 1207959552 | bytes 2000000 | tf_op jit(solution)/shard_map/pallas_call | solution.py:463
  25.3 0.8 copy-done.45
  27.3 1.6 %copy.31 = f32[64,256]{1,0:T(8,128)} copy(f32[64,256]{0,1:T(8,128)} %broadcast_bitcast_fusion) | data formatting | bytes 131072 | tf_op jit(solution)/shard_map/tile | solution.py:555
  29.1 0.8 copy-done.47
  30.1 1.0 copy-done.39
  31.1 1.0 copy-done.46
  32.1 5.6 %shard_map.205 = (f32[3,256,256]{2,1,0:T(8,128)S(1)}, f32[256,768]{1,0:T(8,128)S(1)}, f32[256,768]{1,0:T(8,128)S(1)}, f32[256,384]{1,0:T(8,128)S(1)}, f32[256,38...) custom-call(f32[2,256,128]{2,1,0:T(8,128)} %collective-permute-done.left, ...), custom_call_target="tpu_custom_call" | custom-call | flops 2415919104 | bytes 2000000 | tf_op jit(solution)/shard_map/pallas_call | solution.py:463
  37.8 1.4 %collective-permute-start.2 = (f32[16,3072]{1,0:T(8,128)S(1)}, f32[16,3072]{1,0:T(8,128)S(1)}, u32[]{:S(2)}, u32[]{:S(2)}) collective-permute-start(f32[16,3072]{1,0:T(8,128)S(1)} %get-tuple-element.58.high), channel_id=1, source_target_pairs={{0,16},{16,32},{32,48},{48,64},{64,80},{80,96},{96,112},{112,128},... | collective-permute-start | bytes 589832 | tf_op jit(solution)/shard_map/ppermute | solution.py:510
  39.2 1.5 %collective-permute-start.3 = (f32[16,3072]{1,0:T(8,128)S(1)}, f32[16,3072]{1,0:T(8,128)S(1)}, u32[]{:S(2)}, u32[]{:S(2)}) collective-permute-start(f32[16,3072]{1,0:T(8,128)S(1)} %get-tuple-element.57.low), channel_id=1, source_target_pairs={{16,0},{32,16},{48,32},{64,48},{80,64},{96,80},{112,96},{128,112},... | collective-permute-start | bytes 589832 | tf_op jit(solution)/shard_map/ppermute | solution.py:510
  40.8 1.0 collective-permute-done.2.got_low
  41.8 3.8 %collective-permute-done.3.got_high = f32[16,3072]{1,0:T(8,128)S(1)} collective-permute-done((f32[16,3072]{1,0:T(8,128)S(1)}, f32[16,3072]{1,0:T(8,128)S(1)}, u32[]{:S(2)}, u32[]{:S(2)}) %collective-permute-start.3) | collective-permute-done | bytes 196640 | tf_op jit(solution)/shard_map/ppermute | solution.py:510
  45.6 1.1 copy-done.7
  46.7 1.0 copy-done.10
  47.7 1.0 copy-done.13
  48.7 7.8 %shard_map.206 = (f32[256,768]{1,0:T(8,128)S(1)}, f32[256,768]{1,0:T(8,128)S(1)}, f32[256,384]{1,0:T(8,128)S(1)}, f32[16,1536]{1,0:T(8,128)}, f32[16,1536]{1,0:T(8,128)}) custom-call(f32[256,768]{1,0:T(8,128)S(1)} %get-tuple-element.53.state, f32[256,768]{1,0:T(8,128)S(1)} %get-tuple-element.54.second, f32[256,384]{1,0:T(8,128)S(1)} %get-tuple-element.55.lumped, ...), custom_call_target="tpu_custom_call" | custom-call | flops 3623878656 | bytes 2000000 | tf_op jit(solution)/shard_map/pallas_call | solution.py:463
  56.6 0.7 copy-done.17
  57.3 5.3 %collective-permute-start.4 = (f32[16,1536]{1,0:T(8,128)}, f32[16,1536]{1,0:T(8,128)}, u32[]{:S(2)}, u32[]{:S(2)}) collective-permute-start(f32[16,1536]{1,0:T(8,128)} %get-tuple-element.64.own_high), channel_id=1, source_target_pairs={{0,16},{16,32},{32,48},{48,64},{64,80},{80,96},{96,112},{112,128},... | collective-permute-start | bytes 294920 | tf_op jit(solution)/shard_map/ppermute | solution.py:510
  62.5 1.3 collective-permute-start.5
  65.2 0.7 concatenate.3.header
  65.9 3.5 %collective-permute-done.5.new_high = f32[16,1536]{1,0:T(8,128)} collective-permute-done((f32[16,1536]{1,0:T(8,128)}, f32[16,1536]{1,0:T(8,128)}, u32[]{:S(2)}, u32[]{:S(2)}) %collective-permute-start.5) | collective-permute-done | bytes 98336 | tf_op jit(solution)/shard_map/ppermute | solution.py:510
  69.4 1.0 copy-done.8
  70.4 1.0 copy-done.11
  71.4 1.0 copy-done.14
  72.4 1.0 copy-done.16
  73.4 1.0 copy-done.18
  74.4 0.9 copy-done.24
  75.3 0.9 copy-done.26
  76.3 0.9 copy-done.28
  77.2 0.9 copy-done.30
  78.1 3.6 %shard_map.207 = (f32[4,256,128]{2,1,0:T(8,128)}, f32[32,32,128]{2,1,0:T(8,128)S(1)}, f32[64,512]{1,0:T(8,128)}) custom-call(f32[256,768]{1,0:T(8,128)S(1)} %get-tuple-element.60.state, f32[256,768]{1,0:T(8,128)S(1)} %get-tuple-element.61.second, f32[256,384]{1,0:T(8,128)S(1)} %copy-done.18, f32[256,384]{1,0:T(8,128)S(1)} %copy-done.16, ...), custom_call_target="tpu_custom_call" | custom-call | flops 603979776 | bytes 2000000 | tf_op jit(solution)/shard_map/pallas_call | solution.py:463
  81.8 0.8 copy-done.5
  82.6 10.6 %all-to-all-start.1 = ((f32[32,32,128]{2,1,0:T(8,128)}), f32[32,32,128]{2,1,0:T(8,128)S(1)}, u32[]{:S(2)}, u32[]{:S(2)}) async-start(f32[32,32,128]{2,1,0:T(8,128)} %copy-done.5), calls=%async_computation.1 | async-start | bytes 1048576 | tf_op jit(solution)/shard_map/all_to_all | solution.py:605
  93.9 11.1 %all-to-all-done.1 = f32[32,32,128]{2,1,0:T(8,128)S(1)} async-done(((f32[32,32,128]{2,1,0:T(8,128)}), f32[32,32,128]{2,1,0:T(8,128)S(1)}, u32[]{:S(2)}, u32[]{:S(2)}) %all-to-all-start.1) | async-done | bytes 524320 | tf_op jit(solution)/shard_map/all_to_all | solution.py:605
  106.7 25.9 %all-gather = f32[1024,128]{1,0:T(8,128)S(1)} all-gather(f32[64,128]{1,0:T(8,128)S(1)} %get-tuple-element.74), channel_id=2, replica_groups=mesh['axial'=32,'girth'=16] {'girth'}, dimensions={0}, use_global_device_ids=true | all-gather | bytes 557056 | tf_op jit(solution)/shard_map/all_gather | solution.py:620
  132.6 1.2 shard_map.208
  (113 shorter events, 7.2 us)
Async XLA Ops:
  1.3 1.1 copy-start.2
  2.5 1.1 copy-start.3
  3.6 1.0 copy-start.4
  4.6 1.0 copy-start.19
  5.6 1.0 copy-start.20
  6.6 1.0 copy-start.21
  7.6 1.0 copy-start.22
  14.7 10.6 %copy-start.38 = (f32[4,256,128]{2,1,0:T(8,128)}, f32[4,256,128]{2,1,0:T(8,128)S(1)}, u32[]{:S(2)}) copy-start(f32[4,256,128]{2,1,0:T(8,128)S(1)} %get-tuple-element.42.field) | copy-start | bytes 1572868
  14.7 10.6 %copy-start.40 = (f32[3,256,128]{2,1,0:T(8,128)}, f32[3,256,128]{2,1,0:T(8,128)S(1)}, u32[]{:S(2)}) copy-start(f32[3,256,128]{2,1,0:T(8,128)S(1)} %get-tuple-element.43.geom) | copy-start | bytes 1179652
  14.7 15.3 %copy-start.6 = (bf16[768,256]{1,0:T(8,128)(2,1)}, bf16[768,256]{1,0:T(8,128)(2,1)S(1)}, u32[]{:S(2)}) copy-start(bf16[768,256]{1,0:T(8,128)(2,1)S(1)} %get-tuple-element.46.refs_2_) | copy-start | bytes 1179652
  14.7 15.3 %copy-start.9 = (bf16[768,256]{1,0:T(8,128)(2,1)}, bf16[768,256]{1,0:T(8,128)(2,1)S(1)}, u32[]{:S(2)}) copy-start(bf16[768,256]{1,0:T(8,128)(2,1)S(1)} %get-tuple-element.47.refs_3_) | copy-start | bytes 1179652
  14.7 15.3 %copy-start.12 = (bf16[256,768]{1,0:T(8,128)(2,1)}, bf16[256,768]{1,0:T(8,128)(2,1)S(1)}, u32[]{:S(2)}) copy-start(bf16[256,768]{1,0:T(8,128)(2,1)S(1)} %get-tuple-element.49.refs_4_) | copy-start | bytes 1179652
  14.7 15.3 %copy-start.33 = (bf16[64,192]{1,0:T(8,128)(2,1)}, bf16[64,192]{1,0:T(8,128)(2,1)S(1)}, u32[]{:S(2)}) copy-start(bf16[64,192]{1,0:T(8,128)(2,1)S(1)} %get-tuple-element.51.refs_6_) | copy-start | bytes 73732
  14.7 15.3 %collective-permute-start = (f32[2,256,128]{2,1,0:T(8,128)}, f32[2,256,128]{2,1,0:T(8,128)}, u32[]{:S(2)}, u32[]{:S(2)}) collective-permute-start(f32[2,256,128]{2,1,0:T(8,128)} %get-tuple-element.40), channel_id=1, source_target_pairs={{0,1},{1,2},{2,3},{3,4},{4,5},{5,6},{6,7},{7,8},{8,9},{9,10},{10,1... | collective-permute-start | bytes 786440 | tf_op jit(solution)/shard_map/ppermute | solution.py:505
  17.4 4.2 %copy-start.51 = (s32[64]{0:T(128)S(1)}, s32[64]{0:T(128)}, u32[]{:S(2)}) copy-start(s32[64]{0:T(128)} %param.25) | copy-start | bytes 772
  17.4 12.6 %collective-permute-start.1 = (f32[2,256,128]{2,1,0:T(8,128)}, f32[2,256,128]{2,1,0:T(8,128)}, u32[]{:S(2)}, u32[]{:S(2)}) collective-permute-start(f32[2,256,128]{2,1,0:T(8,128)} %get-tuple-element.41), channel_id=1, source_target_pairs={{1,0},{2,1},{3,2},{4,3},{5,4},{6,5},{7,6},{8,7},{9,8},{10,9},{11,1... | collective-permute-start | bytes 786440 | tf_op jit(solution)/shard_map/ppermute | solution.py:506
  26.6 3.4 %copy-start.41 = (f32[3,256,128]{2,1,0:T(8,128)S(1)}, f32[3,256,128]{2,1,0:T(8,128)}, u32[]{:S(2)}) copy-start(f32[3,256,128]{2,1,0:T(8,128)} %copy-done.40) | copy-start | bytes 1179652
  30.0 1.0 copy-start.39
  31.1 1.0 copy-start.46
  32.1 8.6 %copy-start.50 = (f32[8,128]{1,0:T(8,128)S(1)}, f32[8,128]{1,0:T(8,128)}, u32[]{:S(2)}) copy-start(f32[8,128]{1,0:T(8,128)} %param.30) | copy-start | bytes 12292
  32.1 13.5 %copy-start.42 = (f32[3,256,128]{2,1,0:T(8,128)S(1)}, f32[3,256,128]{2,1,0:T(8,128)}, u32[]{:S(2)}) copy-start(f32[3,256,128]{2,1,0:T(8,128)} %copy-done.40) | copy-start | bytes 1179652
  37.7 18.8 %copy-start.15 = (f32[256,384]{1,0:T(8,128)}, f32[256,384]{1,0:T(8,128)S(1)}, u32[]{:S(2)}) copy-start(f32[256,384]{1,0:T(8,128)S(1)} %get-tuple-element.56.ends) | copy-start | bytes 1179652
  37.7 18.8 %copy-start.23 = (f32[16,3072]{1,0:T(8,128)}, f32[16,3072]{1,0:T(8,128)S(1)}, u32[]{:S(2)}) copy-start(f32[16,3072]{1,0:T(8,128)S(1)} %get-tuple-element.57.low) | copy-start | bytes 589828
  37.7 18.8 %copy-start.25 = (f32[16,3072]{1,0:T(8,128)}, f32[16,3072]{1,0:T(8,128)S(1)}, u32[]{:S(2)}) copy-start(f32[16,3072]{1,0:T(8,128)S(1)} %get-tuple-element.58.high) | copy-start | bytes 589828
  37.7 3.0 %copy-start.55 = (s32[128]{0:T(128)S(1)}, s32[128]{0:T(128)}, u32[]{:S(2)}) copy-start(s32[128]{0:T(128)} %param.29) | copy-start | bytes 1540
  37.8 3.0 %copy-start.56 = (s32[128]{0:T(128)S(1)}, s32[128]{0:T(128)}, u32[]{:S(2)}) copy-start(s32[128]{0:T(128)} %and_select_fusion.3) | copy-start | bytes 1540
  37.8 4.0 %collective-permute-start.2 = (f32[16,3072]{1,0:T(8,128)S(1)}, f32[16,3072]{1,0:T(8,128)S(1)}, u32[]{:S(2)}, u32[]{:S(2)}) collective-permute-start(f32[16,3072]{1,0:T(8,128)S(1)} %get-tuple-element.58.high), channel_id=1, source_target_pairs={{0,16},{16,32},{32,48},{48,64},{64,80},{80,96},{96,112},{112,128},... | collective-permute-start | bytes 589832 | tf_op jit(solution)/shard_map/ppermute | solution.py:510
  39.2 6.4 %copy-start.34 = (bf16[64,192]{1,0:T(8,128)(2,1)S(1)}, bf16[64,192]{1,0:T(8,128)(2,1)}, u32[]{:S(2)}) copy-start(bf16[64,192]{1,0:T(8,128)(2,1)} %copy-done.33) | copy-start | bytes 73732
  39.2 6.4 %collective-permute-start.3 = (f32[16,3072]{1,0:T(8,128)S(1)}, f32[16,3072]{1,0:T(8,128)S(1)}, u32[]{:S(2)}, u32[]{:S(2)}) collective-permute-start(f32[16,3072]{1,0:T(8,128)S(1)} %get-tuple-element.57.low), channel_id=1, source_target_pairs={{16,0},{32,16},{48,32},{64,48},{80,64},{96,80},{112,96},{128,112},... | collective-permute-start | bytes 589832 | tf_op jit(solution)/shard_map/ppermute | solution.py:510
  41.8 14.7 %copy-start.27 = (f32[16,3072]{1,0:T(8,128)}, f32[16,3072]{1,0:T(8,128)S(1)}, u32[]{:S(2)}) copy-start(f32[16,3072]{1,0:T(8,128)S(1)} %collective-permute-done.2.got_low) | copy-start | bytes 589828
  45.6 10.9 %copy-start.29 = (f32[16,3072]{1,0:T(8,128)}, f32[16,3072]{1,0:T(8,128)S(1)}, u32[]{:S(2)}) copy-start(f32[16,3072]{1,0:T(8,128)S(1)} %collective-permute-done.3.got_high) | copy-start | bytes 589828
  45.6 1.1 copy-start.7
  46.7 1.0 copy-start.10
  47.7 1.0 copy-start.13
  57.3 6.5 %copy-start.52 = (s32[64]{0:T(128)S(1)}, s32[64]{0:T(128)}, u32[]{:S(2)}) copy-start(s32[64]{0:T(128)} %param.25) | copy-start | bytes 772
  57.3 6.6 %copy-start.58 = (s32[64]{0:T(128)S(1)}, s32[64]{0:T(128)}, u32[]{:S(2)}) copy-start(s32[64]{0:T(128)} %copy-done.57) | copy-start | bytes 772
  57.3 8.6 %collective-permute-start.4 = (f32[16,1536]{1,0:T(8,128)}, f32[16,1536]{1,0:T(8,128)}, u32[]{:S(2)}, u32[]{:S(2)}) collective-permute-start(f32[16,1536]{1,0:T(8,128)} %get-tuple-element.64.own_high), channel_id=1, source_target_pairs={{0,16},{16,32},{32,48},{48,64},{64,80},{80,96},{96,112},{112,128},... | collective-permute-start | bytes 294920 | tf_op jit(solution)/shard_map/ppermute | solution.py:510
  62.5 6.9 %collective-permute-start.5 = (f32[16,1536]{1,0:T(8,128)}, f32[16,1536]{1,0:T(8,128)}, u32[]{:S(2)}, u32[]{:S(2)}) collective-permute-start(f32[16,1536]{1,0:T(8,128)} %get-tuple-element.63.own_low), channel_id=1, source_target_pairs={{16,0},{32,16},{48,32},{64,48},{80,64},{96,80},{112,96},{128,112},... | collective-permute-start | bytes 294920 | tf_op jit(solution)/shard_map/ppermute | solution.py:510
  65.1 4.3 %copy-start.35 = (bf16[64,192]{1,0:T(8,128)(2,1)S(1)}, bf16[64,192]{1,0:T(8,128)(2,1)}, u32[]{:S(2)}) copy-start(bf16[64,192]{1,0:T(8,128)(2,1)} %copy-done.33) | copy-start | bytes 73732
  69.4 1.0 copy-start.8
  70.4 1.0 copy-start.11
  71.4 1.0 copy-start.14
  72.4 1.0 copy-start.16
  73.4 1.0 copy-start.18
  82.6 23.7 %copy-start.48 = (f32[64,512]{1,0:T(8,128)S(1)}, f32[64,512]{1,0:T(8,128)}, u32[]{:S(2)}) copy-start(f32[64,512]{1,0:T(8,128)} %get-tuple-element.67) | copy-start | bytes 393220
  82.6 22.4 %all-to-all-start.1 = ((f32[32,32,128]{2,1,0:T(8,128)}), f32[32,32,128]{2,1,0:T(8,128)S(1)}, u32[]{:S(2)}, u32[]{:S(2)}) async-start(f32[32,32,128]{2,1,0:T(8,128)} %copy-done.5), calls=%async_computation.1 | async-start | bytes 1048576 | tf_op jit(solution)/shard_map/all_to_all | solution.py:605
  106.3 26.2 %copy-start = (bf16[2048,256]{1,0:T(8,128)(2,1)S(1)}, bf16[2048,256]{1,0:T(8,128)(2,1)}, u32[]{:S(2)}) copy-start(bf16[2048,256]{1,0:T(8,128)(2,1)} %constant.136.clone.table_high) | copy-start | bytes 3145732
  106.3 26.2 %copy-start.1 = (bf16[2048,256]{1,0:T(8,128)(2,1)S(1)}, bf16[2048,256]{1,0:T(8,128)(2,1)}, u32[]{:S(2)}) copy-start(bf16[2048,256]{1,0:T(8,128)(2,1)} %constant.137.clone.table_low) | copy-start | bytes 3145732
  (18 other events, 14.8 us)

commit v3 on v2

--- a/solution.py
+++ b/solution.py
@@ -17,6 +17,8 @@
 WIDE = 6 * LANES
 ROWS_DEV = 16
 SLOTS = 8
+VMEM_LIMIT = 32 * 1024 * 1024
+LOAD_LIMIT = 60000000
 F32 = jnp.float32
 BF16 = jnp.bfloat16
 
@@ -65,33 +67,16 @@
     return high, low
 
 
-def left_operand(table):
-    high, low = np_split(table)
-    return np.concatenate([high, high, low], axis=1)
-
-
-def right_operand(table):
-    high, low = np_split(table)
-    return np.concatenate([high, high, low], axis=0)
-
-
-def stiffness_tables():
+def stiffness_table():
     d = derivative_table()
     eye = lambda n: np.eye(n, dtype=np.float32)
-    radial = np.kron(np.kron(eye(2), d), eye(16))
     axial = np.kron(eye(32), d)
-    slope = np.concatenate([radial, axial], axis=0)
-    ends = np.tile(np.concatenate([d[:, 0], d[:, 7]]), 16)[:, None]
-    return (
-        left_operand(slope),
-        left_operand(slope.T),
-        right_operand(axial.T),
-        right_operand(axial),
-        left_operand(axial.T),
-        left_operand(np.kron(eye(4), d)),
-        left_operand(np.kron(eye(8), d.T)),
-        np.ascontiguousarray(np.broadcast_to(ends, (NODES, LANES))),
-    )
+    blocks = list(np_split(axial)) + list(np_split(axial.T))
+    for small in (np.kron(eye(4), d), np.kron(eye(8), d.T)):
+        high, low = np_split(small)
+        row = np.concatenate([high, high, low], axis=1)
+        blocks.append(np.pad(row, ((0, 0), (0, NODES - row.shape[1]))))
+    return np.concatenate(blocks, axis=0)
 
 
 def dft_tables():
@@ -126,12 +111,83 @@
     return dot(jnp.concatenate([high, low, high], axis=1), table)
 
 
-def stiff(u, gr, ga, gg, tables):
-    slope_l, slope_t, girth, girth_t = tables[:4]
-    ra = left_mul(slope_l[...], u)
-    g = right_mul(u, girth[...])
-    y = jnp.concatenate([ra[:NODES] * gr, ra[NODES:] * ga], axis=0)
-    return left_mul(slope_t[...], y) + right_mul(g * gg, girth_t[...])
+def square(table, k):
+    return table[k * NODES : (k + 1) * NODES, :]
+
+
+def axial_left(table):
+    return jnp.concatenate([square(table, 0), square(table, 0), square(table, 1)], axis=1)
+
+
+def axial_left_t(table):
+    return jnp.concatenate([square(table, 2), square(table, 2), square(table, 3)], axis=1)
+
+
+def girth_right(table):
+    return jnp.concatenate([square(table, 2), square(table, 2), square(table, 3)], axis=0)
+
+
+def girth_right_t(table):
+    return jnp.concatenate([square(table, 0), square(table, 0), square(table, 1)], axis=0)
+
+
+def radial_small(table):
+    return table[4 * NODES : 4 * NODES + 32, :96]
+
+
+def radial_small_t(table):
+    return table[4 * NODES + 32 : 4 * NODES + 96, :192]
+
+
+def radial_apply(x, matrix):
+    half = P_SIZE // 2
+    odd_rows = 0.5 * (matrix[:half, :half] - matrix[:half, : half - 1 : -1])
+    even_rows = 0.5 * (matrix[:half, :half] + matrix[:half, : half - 1 : -1])
+    outs = {}
+    for element in range(2):
+        for part in range(2):
+            for tile in range(x.shape[1] // LANES):
+                nodes = []
+                for i in range(P_SIZE):
+                    row = (element * P_SIZE + i) * 16 + part * 8
+                    nodes.append(x[row : row + 8, tile * LANES : (tile + 1) * LANES])
+                even = [nodes[j] + nodes[P_SIZE - 1 - j] for j in range(half)]
+                odd = [nodes[j] - nodes[P_SIZE - 1 - j] for j in range(half)]
+                for i in range(half):
+                    p = float(odd_rows[i, 0]) * odd[0]
+                    q = float(even_rows[i, 0]) * even[0]
+                    for j in range(1, half):
+                        p = p + float(odd_rows[i, j]) * odd[j]
+                        q = q + float(even_rows[i, j]) * even[j]
+                    outs[element * P_SIZE + i, part, tile] = p + q
+                    outs[element * P_SIZE + P_SIZE - 1 - i, part, tile] = p - q
+    columns = []
+    for tile in range(x.shape[1] // LANES):
+        columns.append(
+            jnp.concatenate([outs[i, part, tile] for i in range(16) for part in range(2)], axis=0)
+        )
+    return jnp.concatenate(columns, axis=1)
+
+
+def end_columns(rows):
+    d = derivative_table()
+    values = [float(x) for x in np.concatenate([d[:, 0], d[:, 7]])]
+    node = lax.broadcasted_iota(jnp.int32, (16, LANES), 0)
+    column = jnp.full((16, LANES), values[0], F32)
+    for k in range(1, 16):
+        column = jnp.where(node == k, values[k], column)
+    return jnp.broadcast_to(column[None], (16, 16, LANES)).reshape(rows, LANES)
+
+
+def stiff(u, gr, ga, gg, table):
+    d = derivative_table()
+    high, low = split(u)
+    axial = dot(axial_left(table), jnp.concatenate([high, low, high], axis=0)) * ga
+    girth = dot(jnp.concatenate([high, low, high], axis=1), girth_right(table)) * gg
+    radial = radial_apply(radial_apply(u, d) * gr, d.T)
+    return (
+        left_mul(axial_left_t(table), axial) + right_mul(girth, girth_right_t(table)) + radial
+    )
 
 
 def twice(x):
@@ -180,17 +236,14 @@
     return x[:, k * LANES : (k + 1) * LANES]
 
 
-def load_kernel(count, *refs):
-    sources, targets = refs[:count], refs[count : 2 * count]
-    to_right, to_left, sems = refs[2 * count :]
-    copies = []
-    for k in range(count):
-        copy = pltpu.make_async_copy(sources[k], targets[k], sems.at[k])
+def pack_kernel(field_in, geom_in, mass_in, to_right, to_left, field, geom, mass, sems):
+    copies = [
+        pltpu.make_async_copy(field_in, field, sems.at[0]),
+        pltpu.make_async_copy(geom_in, geom, sems.at[1]),
+        pltpu.make_async_copy(mass_in, mass, sems.at[2]),
+    ]
+    for copy in copies:
         copy.start()
-        copies.append(copy)
-    for copy in copies[:3]:
-        copy.wait()
-    field, geom, mass = targets[:3]
     lane = lax.broadcasted_iota(jnp.int32, (NODES, LANES), 1)
 
     def pack(arrays, start):
@@ -200,22 +253,22 @@
             out = moved if out is None else jnp.where(lane // HALO == k, moved, out)
         return out
 
+    copies[0].wait()
     fields = [field[c] for c in range(C)]
+    to_right[0] = pack(fields, LANES - HALO)
+    to_left[0] = pack(fields, 0)
+    copies[1].wait()
+    copies[2].wait()
     others = [geom[k] for k in range(3)] + [mass[...]]
-    to_right[0] = pack(fields, LANES - HALO)
     to_right[1] = pack(others, LANES - HALO)
-    to_left[0] = pack(fields, 0)
     to_left[1] = pack(others, 0)
-    for copy in copies[3:]:
-        copy.wait()
-
-
-def own_kernel(field, geom, *refs):
-    tables, out = refs[:-1], refs[-1]
+
+
+def own_kernel(field, geom, table, out):
     gr, ga, gg = [twice(geom[k]) for k in range(3)]
     for pair in range(2):
         u = jnp.concatenate([field[2 * pair], field[2 * pair + 1]], axis=1)
-        out[:, 2 * pair * LANES : (2 * pair + 2) * LANES] = stiff(u, gr, ga, gg, tables)
+        out[:, 2 * pair * LANES : (2 * pair + 2) * LANES] = stiff(u, gr, ga, gg, table)
 
 
 def at_faces(low, high, width):
@@ -268,9 +321,9 @@
 NARROW = 3 * LANES
 
 
-def halo_kernel(left, right, own_total, field, mass, geom, *refs):
-    tables = refs[:8]
-    halo_geom, state, second, mass_out, ends_out, low, high = refs[8:]
+def halo_kernel(
+    left, right, own_total, field, mass, geom, tables, halo_geom, state, second, mass_out, ends_out, low, high
+):
     lane = lax.broadcasted_iota(jnp.int32, (NODES, LANES), 1)
 
     def spread(x, k):
@@ -294,8 +347,8 @@
     lumped = sum_nodes(jnp.concatenate(masses, axis=1)).reshape(NODES, NARROW)
     mass_out[...] = lumped
     whole = [jnp.concatenate([geom[k], geoms[k]], axis=1) for k in range(3)]
-    end = tables[7][...]
-    ends = left_mul(tables[4][...], whole[1] * jnp.concatenate([end] * 3, axis=1))
+    end = end_columns(NODES)
+    ends = left_mul(axial_left_t(tables), whole[1] * jnp.concatenate([end] * 3, axis=1))
     ends_out[...] = ends
     for k, x in enumerate([lumped, whole[0], whole[2], ends]):
         put_faces(x, low, high, STATIC + k * NARROW)
@@ -321,14 +374,14 @@
     radial, girthwise = [
         wide(jnp.concatenate([static_part(ref, k) for ref in statics], axis=0)) for k in (1, 2)
     ]
-    slope = left_mul(tables[5][...], w)
-    face = left_mul(tables[6][...], jnp.concatenate([slope, slope], axis=0) * radial)
+    slope = left_mul(radial_small(tables), w)
+    face = left_mul(radial_small_t(tables), jnp.concatenate([slope, slope], axis=0) * radial)
     pieces = []
     for tile in range(3):
         span = slice(2 * tile * LANES, (2 * tile + 2) * LANES)
-        g = right_mul(w[:, span], tables[2][...])
+        g = right_mul(w[:, span], girth_right(tables))
         y = jnp.concatenate([g, g], axis=0) * girthwise[:, span]
-        pieces.append(right_mul(y, tables[3][...]))
+        pieces.append(right_mul(y, girth_right_t(tables)))
     face = face + jnp.concatenate(pieces, axis=1)
     other = jnp.concatenate([static_part(got_low, 3), static_part(got_high, 3)], axis=0)
     beyond = face[32:] + wide(other) * w
@@ -347,8 +400,7 @@
 
 
 def middle_kernel(state, second, lumped, ends, low, high, got_low, got_high, geom, halo_geom, *refs):
-    tables = refs[:8]
-    state_out, second_out, inverse_out, next_low, next_high = refs[8:]
+    tables, state_out, second_out, inverse_out, next_low, next_high = refs
     inverse = 1.0 / (
         lumped[...] + at_faces(static_part(got_low, 0), static_part(got_high, 0), NARROW)
     )
@@ -378,10 +430,11 @@
     girth_weight,
     select,
     header,
-    *refs,
+    tables,
+    out,
+    packed,
+    probes_out,
 ):
-    tables = refs[:8]
-    out, packed, probes_out = refs[8:]
     u = finish_pair(
         state[...],
         second[...],
@@ -418,13 +471,56 @@
         packed[:, c * SLOTS : (c + 1) * SLOTS, :] = block
 
 
-def unpack_kernel(pieces, out):
+def weights_kernel(
+    cycle_id, cycle_radial, cycle_axial, cycle_weights, az_elem, az_weights, slab, girth, select, header
+):
+    slots = cycle_id.shape[0]
+    ids = cycle_id[...].reshape(1, slots)
+    in_radial, in_axial = [x[...].reshape(1, slots) for x in (cycle_radial, cycle_axial)]
+    radial, axial = [
+        jnp.concatenate(
+            [jnp.where(owner == e, cycle_weights[k], 0.0) for e in range(2)], axis=0
+        )
+        for k, owner in enumerate((in_radial, in_axial))
+    ]
+    slab[...] = jnp.transpose((radial[:, None, :] * axial[None, :, :]).reshape(NODES, slots))
+    places = az_elem[...].reshape(1, 1, LANES)
+    element = lax.broadcasted_iota(jnp.int32, (LANES // P_SIZE, P_SIZE, LANES), 0)
+    girth[...] = jnp.where(element == places, az_weights[...][None], 0.0).reshape(LANES, LANES)
+    used = ids >= 0
+    target = jnp.where(used, lax.shift_right_logical(ids, 4), -1).astype(F32)
+    across = jnp.broadcast_to(target, (slots, slots))
+    down = jnp.transpose(across)
+    before = lax.broadcasted_iota(jnp.int32, across.shape, 0) < lax.broadcasted_iota(
+        jnp.int32, across.shape, 1
+    )
+    rank = jnp.sum(jnp.where((across == down) & before, 1.0, 0.0), axis=0, keepdims=True)
+    position = jnp.where(used & (rank < SLOTS - 1.5), target * SLOTS + rank, -1.0)
+    wanted = lax.broadcasted_iota(jnp.int32, select.shape, 0).astype(F32)
+    select[...] = jnp.where(wanted == position, 1.0, 0.0)
+    number = (ids & (ROWS_DEV - 1)).astype(F32) + 1.0
+    owners = lax.broadcasted_iota(jnp.int32, (header.shape[0], slots), 0).astype(F32)
+    named = jnp.where(owners == target, number, 0.0).astype(BF16)
+    ranks = lax.broadcasted_iota(jnp.int32, (LANES, slots), 0).astype(F32)
+    placed = jnp.where(ranks == rank, 1.0, 0.0).astype(BF16)
+    numbers = lax.dot_general(
+        named, placed, (((1,), (1,)), ((), ())), preferred_element_type=F32
+    )
+    overflow = jnp.max(jnp.where(used & (rank > SLOTS - 1.5), 1.0, 0.0), axis=1, keepdims=True)
+    lane = lax.broadcasted_iota(jnp.int32, header.shape, 1)
+    header[...] = jnp.where(
+        lane >= SLOTS, overflow, jnp.where(lane < SLOTS - 1, numbers, 0.0)
+    )
+
+
+def unpack_kernel(pieces, out, crowded):
     sources = pieces.shape[0]
     heads = pieces[:, 0:SLOTS, :]
     head = jnp.broadcast_to(heads[:, SLOTS - 1 : SLOTS, :], heads.shape)
     place = lax.broadcasted_iota(jnp.int32, heads.shape, 1)
     lane = lax.broadcasted_iota(jnp.int32, heads.shape, 2)
     mine = jnp.where((lane == place) & (place < SLOTS - 1), head, 0.0)
+    crowded[0, 0] = jnp.max(jnp.where(lane >= SLOTS, head, 0.0)).astype(jnp.int32)
     row = jnp.sum(mine.reshape(sources * SLOTS, LANES), axis=1, keepdims=True)
     column = lax.broadcasted_iota(jnp.int32, (sources * SLOTS, LANES), 1).astype(F32)
     chosen = jnp.transpose(jnp.where(row == column + 1.0, 1.0, 0.0))[:ROWS_DEV].astype(BF16)
@@ -465,23 +561,22 @@
         out_shape=out_shape,
         in_specs=[vmem] * len(args),
         out_specs=[vmem] * len(shapes),
-        compiler_params=pltpu.CompilerParams(vmem_limit_bytes=40 * 1024 * 1024),
+        compiler_params=pltpu.CompilerParams(vmem_limit_bytes=VMEM_LIMIT),
         cost_estimate=pl.CostEstimate(flops=flops, bytes_accessed=2000000, transcendentals=0),
     )(*args)
 
 
-def load(*args):
-    halo = jax.ShapeDtypeStruct((2, NODES, LANES), F32)
-    outs = [jax.ShapeDtypeStruct(x.shape, x.dtype) for x in args] + [halo] * 2
-    got = pl.pallas_call(
-        lambda *refs: load_kernel(len(args), *refs),
-        out_shape=outs,
-        in_specs=[pl.BlockSpec(memory_space=pltpu.HBM)] * len(args),
-        out_specs=[pl.BlockSpec(memory_space=pltpu.VMEM)] * len(outs),
-        scratch_shapes=[pltpu.SemaphoreType.DMA((len(args),))],
-        compiler_params=pltpu.CompilerParams(vmem_limit_bytes=40 * 1024 * 1024),
+def pack_halos(*args):
+    hbm, vmem = [pl.BlockSpec(memory_space=m) for m in (pltpu.HBM, pltpu.VMEM)]
+    return pl.pallas_call(
+        pack_kernel,
+        out_shape=[jax.ShapeDtypeStruct((2, NODES, LANES), F32)] * 2,
+        in_specs=[hbm] * len(args),
+        out_specs=[vmem] * 2,
+        scratch_shapes=[pltpu.VMEM(x.shape, F32) for x in args]
+        + [pltpu.SemaphoreType.DMA((len(args),))],
+        compiler_params=pltpu.CompilerParams(vmem_limit_bytes=LOAD_LIMIT),
     )(*args)
-    return got[: len(args)], got[len(args)], got[len(args) + 1]
 
 
 def body(
@@ -492,19 +587,16 @@
     down = [(j, i) for i, j in up]
     around = [(i, (i + 1) % girth_count) for i in range(girth_count)]
     back = [(j, i) for i, j in around]
-    loaded, to_right, to_left = load(
-        field.reshape(C, NODES, LANES),
-        geometry.reshape(3, NODES, LANES),
-        mass.reshape(NODES, LANES),
-        *[jnp.asarray(t) for t in stiffness_tables()],
-    )
-    field, geom, mass = loaded[:3]
-    tables = loaded[3:]
+    field = field.reshape(C, NODES, LANES)
+    geom = geometry.reshape(3, NODES, LANES)
+    mass = mass.reshape(NODES, LANES)
+    table = jnp.asarray(stiffness_table())
+    to_right, to_left = pack_halos(field, geom, mass)
     tile_flops = 18 * 2 * 256**3
 
     left = lax.ppermute(to_right, "girth", around)
     right = lax.ppermute(to_left, "girth", back)
-    (own_total,) = call(own_kernel, [(NODES, C * LANES)], 2 * tile_flops, field, geom, *tables[:4])
+    (own_total,) = call(own_kernel, [(NODES, C * LANES)], 2 * tile_flops, field, geom, table)
 
     def exchange(low, high):
         return lax.ppermute(high, "axial", up), lax.ppermute(low, "axial", down)
@@ -521,7 +613,7 @@
         field,
         mass,
         geom,
-        *tables,
+        table,
     )
     got_low, got_high = exchange(low, high)
     state, second, inverse, own_low, own_high = call(
@@ -538,46 +630,26 @@
         got_high,
         geom,
         halo_geom,
-        *tables,
+        table,
     )
     new_low, new_high = exchange(own_low, own_high)
 
     slot_count = cycle_id.shape[0]
-    node = jnp.arange(NODES, dtype=jnp.int32)
-    radial_node, axial_node = node // 16, node % 16
-    radial_weight = jnp.where(
-        radial_node[None, :] // P_SIZE == cycle_radial[:, None],
-        jnp.tile(jnp.repeat(cycle_weights[0].T, 16, axis=1), (1, 2)),
-        0.0,
-    )
-    axial_weight = jnp.where(
-        axial_node[None, :] // P_SIZE == cycle_axial[:, None],
-        jnp.tile(cycle_weights[1].T, (1, NODES // P_SIZE)),
-        0.0,
-    )
-    slab = radial_weight * axial_weight
-    girth_node = jnp.arange(LANES, dtype=jnp.int32)
-    girth_weight = jnp.where(
-        girth_node[:, None] // P_SIZE == az_elem[None, :],
-        jnp.tile(az_weights, (LANES // P_SIZE, 1)),
-        0.0,
-    )
-    target = jnp.where(cycle_id >= 0, cycle_id // ROWS_DEV, -1)
-    order = jnp.arange(slot_count, dtype=jnp.int32)
-    earlier = (target[:, None] == target[None, :]) & (order[None, :] < order[:, None])
-    rank = jnp.sum(earlier.astype(jnp.int32), axis=1)
-    fits = (cycle_id >= 0) & (rank < SLOTS - 1)
-    position = jnp.where(fits, target * SLOTS + rank, -1)
-    wanted = jnp.arange(SLOTS * axial_count, dtype=jnp.int32)
-    select = (wanted[:, None] == position[None, :]).astype(F32)
-    number = jnp.sum(select * (cycle_id % ROWS_DEV + 1).astype(F32)[None, :], axis=1)
-    overflow = jnp.any((cycle_id >= 0) & (rank >= SLOTS - 1)).astype(F32)
-    header = jnp.concatenate(
+    slab, girth_weight, select, header = call(
+        weights_kernel,
         [
-            number.reshape(axial_count, SLOTS),
-            jnp.broadcast_to(overflow, (axial_count, LANES - SLOTS)),
+            (slot_count, NODES),
+            (LANES, LANES),
+            (SLOTS * axial_count, slot_count),
+            (axial_count, LANES),
         ],
-        axis=1,
+        1000000,
+        cycle_id,
+        cycle_radial,
+        cycle_axial,
+        cycle_weights,
+        az_elem,
+        az_weights,
     )
 
     final, packed, probes = call(
@@ -600,14 +672,23 @@
         girth_weight,
         select,
         header,
-        *tables,
+        table,
     )
     pieces = lax.all_to_all(packed, "axial", 0, 0)
 
-    def compact(pieces, probes, cycle_id):
-        return call(unpack_kernel, [(C * ROWS_DEV, LANES)], tile_flops, pieces)[0]
-
-    def dense(pieces, probes, cycle_id):
+    vmem = pl.BlockSpec(memory_space=pltpu.VMEM)
+    rows, crowded = pl.pallas_call(
+        unpack_kernel,
+        out_shape=[
+            jax.ShapeDtypeStruct((C * ROWS_DEV, LANES), F32),
+            jax.ShapeDtypeStruct((1, 1), jnp.int32),
+        ],
+        in_specs=[vmem],
+        out_specs=[vmem, pl.BlockSpec(memory_space=pltpu.SMEM)],
+        compiler_params=pltpu.CompilerParams(vmem_limit_bytes=VMEM_LIMIT),
+    )(pieces)
+
+    def dense(rows, probes, cycle_id):
         wanted = jnp.arange(ROWS_DEV * axial_count, dtype=jnp.int32)
         chosen = (wanted[:, None] == cycle_id[None, :]).astype(F32)
         rows = jnp.dot(chosen, probes, precision=lax.Precision.HIGHEST)
@@ -615,8 +696,9 @@
         rows = jnp.sum(lax.all_to_all(rows, "axial", 0, 0), axis=0)
         return rows.reshape(ROWS_DEV, C, LANES).swapaxes(0, 1).reshape(C * ROWS_DEV, LANES)
 
-    crowded = jnp.max(pieces[:, SLOTS - 1, SLOTS]) > 0.5
-    rows = lax.cond(crowded, dense, compact, pieces, probes, cycle_id)
+    rows = lax.cond(
+        crowded[0, 0] > 0, dense, lambda rows, *_: rows, rows, probes, cycle_id
+    )
     rows = lax.all_gather(rows, "girth")
     table_high, table_low, phases = dft_tables()
     phase = lax.dynamic_index_in_dim(

time: 135 us -> 100 us (0.74)
  local copies, waits for them, and re-layouts: 33.3 us -> 1.79 us
  Pallas kernels: 23.4 us -> 19.1 us
  waiting for transfers between devices: 19.4 us -> 23.3 us
  starting transfers between devices: 27 us -> 29.4 us
  other arithmetic: 2.38 us -> 0 us
    unnamed x118 -> x24, local copies, waits for them, and re-layouts: 28.8 us -> 1.1 us
    pallas_call x6, Pallas kernels: 20.6 us -> 16 us  [call(): pl.pallas_call(kernel, out_shape=out_shape, in_specs=[vmem] * len(args),...]
    ppermute x4, waiting for transfers between devices: 8.36 us -> 11.2 us  [exchange(): return (lax.ppermute(high, 'axial', up), lax.ppermute(low, 'axial', down))]
    ppermute x4, starting transfers between devices: 9.44 us -> 12 us  [exchange(): return (lax.ppermute(high, 'axial', up), lax.ppermute(low, 'axial', down))]
    another operation x4 -> x0, local copies, waits for them, and re-layouts: 2.35 us -> none  [the longest x2 2.26 us: body(): jnp.tile(cycle_weights[1].T, (1, NODES // P_SIZE))]
    pallas_call x1 -> x2, Pallas kernels: 2.83 us -> 3.14 us  [the longest x1 2.39 us: pack_halos(): pl.pallas_call(pack_kernel, out_shape=[jax.ShapeDtypeStruct((2, NODES, LA...]
  transfers between devices with their start and end apart: 7 -> 7, of which waited for: 4 -> 4; matrix products, arithmetic and copies ran while one was open for 5% -> 1% of each run, Pallas kernels for 2% -> 2%
where the time goes in v3:
time: 100 us; the launch traced here: 99.7 us
  starting transfers between devices  29.4 us (29%)
  blocking collectives  24.6 us (25%)
  waiting for transfers between devices  23.3 us (23%)
  Pallas kernels  19.1 us (19%)
  local copies, waits for them, and re-layouts  1.79 us (2%)
  between operations  1.51 us (2%)
    all_gather x1, blocking collectives, body(): rows = lax.all_gather(rows, 'girth')  24.6 us
    pallas_call x6, Pallas kernels, call(): pl.pallas_call(kernel, out_shape=out_shape, in_specs=[vmem] * len(args),...  16 us
    all_to_all x1, waiting for transfers between devices, body(): pieces = lax.all_to_all(packed, 'axial', 0, 0)  12.1 us
    ppermute x4, starting transfers between devices, exchange(): return (lax.ppermute(high, 'axial', up), lax.ppermute(low, 'axial', down))  12 us
    ppermute x4, waiting for transfers between devices, exchange(): return (lax.ppermute(high, 'axial', up), lax.ppermute(low, 'axial', down))  11.2 us
    all_to_all x1, starting transfers between devices, body(): pieces = lax.all_to_all(packed, 'axial', 0, 0)  10.5 us
    ppermute x1, starting transfers between devices, body(): right = lax.ppermute(to_left, 'girth', back)  4.22 us
    ppermute x1, starting transfers between devices, body(): left = lax.ppermute(to_right, 'girth', around)  2.7 us
  transfers between devices with their start and end apart: 7, of which 4 were waited for; matrix products, arithmetic and copies ran while one was open for 1% of the time, Pallas kernels for 2%

profile of v3, /device:TPU:1, one launch (start us, length us, event | category | flops | bytes accessed | tf_op | source)
XLA Modules:
  0.0 99.7 jit_solution(8205821753777194770)
XLA Ops:
  0.6 0.0 copy-start.2
  0.6 0.0 copy-start.4
  0.7 2.4 %shard_map.140 = (f32[2,256,128]{2,1,0:T(8,128)}, f32[2,256,128]{2,1,0:T(8,128)}) custom-call(f32[4,256,128]{2,1,0:T(8,128)} %bitcast.13, f32[3,256,128]{2,1,0:T(8,128)} %bitcast.16, f32[256,128]{1,0:T(8,128)} %bitcast.20), custom_call_target="tpu_custom_call" | custom-call | tf_op jit(solution)/shard_map/pallas_call | solution.py:571
  3.1 2.7 %collective-permute-start = (f32[2,256,128]{2,1,0:T(8,128)}, f32[2,256,128]{2,1,0:T(8,128)S(1)}, u32[]{:S(2)}, u32[]{:S(2)}) collective-permute-start(f32[2,256,128]{2,1,0:T(8,128)} %get-tuple-element.35), channel_id=1, source_target_pairs={{0,1},{1,2},{2,3},{3,4},{4,5},{5,6},{6,7},{7,8},{8,9},{9,10},{10,1... | collective-permute-start | bytes 786440 | tf_op jit(solution)/shard_map/ppermute | solution.py:597
  5.8 4.2 %collective-permute-start.1 = (f32[2,256,128]{2,1,0:T(8,128)}, f32[2,256,128]{2,1,0:T(8,128)S(1)}, u32[]{:S(2)}, u32[]{:S(2)}) collective-permute-start(f32[2,256,128]{2,1,0:T(8,128)} %get-tuple-element.36), channel_id=1, source_target_pairs={{1,0},{2,1},{3,2},{4,3},{5,4},{6,5},{7,6},{8,7},{9,8},{10,9},{11,1... | collective-permute-start | bytes 786440 | tf_op jit(solution)/shard_map/ppermute | solution.py:598
  10.0 0.0 copy-done.2
  10.0 0.0 copy-done.4
  10.0 0.0 copy-start.3
  10.0 1.0 %copy-done.3 = f32[4,16,16,128]{3,2,1,0:T(8,128)S(1)} copy-done((f32[4,16,16,128]{3,2,1,0:T(8,128)S(1)}, f32[4,16,16,128]{3,2,1,0:T(8,128)}, u32[]{:S(2)}) %copy-start.3) | copy-done | bytes 524312
  11.0 0.0 copy-start.5
  11.0 1.5 %shard_map.141.own_total = f32[256,512]{1,0:T(8,128)S(1)} custom-call(f32[4,256,128]{2,1,0:T(8,128)S(1)} %bitcast.14, f32[3,256,128]{2,1,0:T(8,128)S(1)} %bitcast.17, bf16[1120,256]{1,0:T(8,128)(2,1)S(1)} %copy-done.2), custom_call_target="tpu_custom_call" | custom-call | flops 1207959552 | bytes 2000000 | tf_op jit(solution)/shard_map/pallas_call | solution.py:559
  12.6 0.0 collective-permute-done.left
  12.6 0.0 collective-permute-done.1.right
  12.6 0.0 copy-done.5
  12.6 4.0 %shard_map.142 = (f32[3,256,256]{2,1,0:T(8,128)S(1)}, f32[256,768]{1,0:T(8,128)S(1)}, f32[256,768]{1,0:T(8,128)S(1)}, f32[256,384]{1,0:T(8,128)S(1)}, f32[256,38...) custom-call(f32[2,256,128]{2,1,0:T(8,128)S(1)} %collective-permute-done.left, ...), custom_call_target="tpu_custom_call" | custom-call | flops 2415919104 | bytes 2000000 | tf_op jit(solution)/shard_map/pallas_call | solution.py:559
  16.6 3.2 %collective-permute-start.2 = (f32[16,3072]{1,0:T(8,128)S(1)}, f32[16,3072]{1,0:T(8,128)S(1)}, u32[]{:S(2)}, u32[]{:S(2)}) collective-permute-start(f32[16,3072]{1,0:T(8,128)S(1)} %get-tuple-element.42.high), channel_id=1, source_target_pairs={{0,16},{16,32},{32,48},{48,64},{64,80},{80,96},{96,112},{112,128},... | collective-permute-start | bytes 589832 | tf_op jit(solution)/shard_map/ppermute | solution.py:602
  19.8 1.3 %collective-permute-start.3 = (f32[16,3072]{1,0:T(8,128)S(1)}, f32[16,3072]{1,0:T(8,128)S(1)}, u32[]{:S(2)}, u32[]{:S(2)}) collective-permute-start(f32[16,3072]{1,0:T(8,128)S(1)} %get-tuple-element.41.low), channel_id=1, source_target_pairs={{16,0},{32,16},{48,32},{64,48},{80,64},{96,80},{112,96},{128,112},... | collective-permute-start | bytes 589832 | tf_op jit(solution)/shard_map/ppermute | solution.py:602
  21.1 1.3 %collective-permute-done.2.got_low = f32[16,3072]{1,0:T(8,128)S(1)} collective-permute-done((f32[16,3072]{1,0:T(8,128)S(1)}, f32[16,3072]{1,0:T(8,128)S(1)}, u32[]{:S(2)}, u32[]{:S(2)}) %collective-permute-start.2) | collective-permute-done | bytes 196640 | tf_op jit(solution)/shard_map/ppermute | solution.py:602
  22.4 4.5 %collective-permute-done.3.got_high = f32[16,3072]{1,0:T(8,128)S(1)} collective-permute-done((f32[16,3072]{1,0:T(8,128)S(1)}, f32[16,3072]{1,0:T(8,128)S(1)}, u32[]{:S(2)}, u32[]{:S(2)}) %collective-permute-start.3) | collective-permute-done | bytes 196640 | tf_op jit(solution)/shard_map/ppermute | solution.py:602
  26.9 0.0 copy-start.6
  26.9 0.0 copy-start.7
  26.9 6.0 %shard_map.143 = (f32[256,768]{1,0:T(8,128)S(1)}, f32[256,768]{1,0:T(8,128)S(1)}, f32[256,384]{1,0:T(8,128)S(1)}, f32[16,1536]{1,0:T(8,128)S(1)}, f32[16,1536]{1,0:T(8,128)S(1)}) custom-call(f32[256,768]{1,0:T(8,128)S(1)} %get-tuple-element.37.state, f32[256,768]{1,0:T(8,128)S(1)} %get-tuple-element.38.second, f32[256,384]{1,0:T(8,128)S(1)} %get-tuple-element.39.lumped, ...), custom_call_target="tpu_custom_call" | custom-call | flops 3623878656 | bytes 2000000 | tf_op jit(solution)/shard_map/pallas_call | solution.py:559
  32.9 0.0 copy-start.11
  32.9 0.0 copy-start.8
  32.9 0.0 copy-start.9
  32.9 0.0 copy-start.10
  32.9 6.1 %collective-permute-start.4 = (f32[16,1536]{1,0:T(8,128)S(1)}, f32[16,1536]{1,0:T(8,128)S(1)}, u32[]{:S(2)}, u32[]{:S(2)}) collective-permute-start(f32[16,1536]{1,0:T(8,128)S(1)} %get-tuple-element.48.own_high), channel_id=1, source_target_pairs={{0,16},{16,32},{32,48},{48,64},{64,80},{80,96},{96,112},{112,128},... | collective-permute-start | bytes 294920 | tf_op jit(solution)/shard_map/ppermute | solution.py:602
  39.0 1.5 %collective-permute-start.5 = (f32[16,1536]{1,0:T(8,128)S(1)}, f32[16,1536]{1,0:T(8,128)S(1)}, u32[]{:S(2)}, u32[]{:S(2)}) collective-permute-start(f32[16,1536]{1,0:T(8,128)S(1)} %get-tuple-element.47.own_low), channel_id=1, source_target_pairs={{16,0},{32,16},{48,32},{64,48},{80,64},{96,80},{112,96},{128,112},... | collective-permute-start | bytes 294920 | tf_op jit(solution)/shard_map/ppermute | solution.py:602
  40.5 0.0 copy-done.6
  40.5 0.0 copy-done.7
  40.5 0.0 copy-done.11
  40.5 0.0 copy-done.8
  40.6 0.0 copy-done.9
  40.6 0.0 copy-done.10
  40.6 0.2 shard_map.144
  40.8 0.0 collective-permute-done.4.new_low
  40.8 5.4 %collective-permute-done.5.new_high = f32[16,1536]{1,0:T(8,128)S(1)} collective-permute-done((f32[16,1536]{1,0:T(8,128)S(1)}, f32[16,1536]{1,0:T(8,128)S(1)}, u32[]{:S(2)}, u32[]{:S(2)}) %collective-permute-start.5) | collective-permute-done | bytes 98336 | tf_op jit(solution)/shard_map/ppermute | solution.py:602
  46.2 2.9 %shard_map.145 = (f32[4,256,128]{2,1,0:T(8,128)}, f32[32,32,128]{2,1,0:T(8,128)}, f32[64,512]{1,0:T(8,128)S(1)}) custom-call(f32[256,768]{1,0:T(8,128)S(1)} %get-tuple-element.44.state, f32[256,768]{1,0:T(8,128)S(1)} %get-tuple-element.45.second, f32[256,384]{1,0:T(8,128)S(1)} %get-tuple-element.46.inverse, f32[256,384]{1,0:T(8,128)S(1)} %get-tuple-element.40.ends, ...), custom_call_target="tpu_custom_call" | custom-call | flops 603979776 | bytes 2000000 | tf_op jit(solution)/shard_map/pallas_call | solution.py:559
  49.2 10.5 %all-to-all-start.1 = ((f32[32,32,128]{2,1,0:T(8,128)}), f32[32,32,128]{2,1,0:T(8,128)S(1)}, u32[]{:S(2)}, u32[]{:S(2)}) async-start(f32[32,32,128]{2,1,0:T(8,128)} %get-tuple-element.54), calls=%async_computation.1 | async-start | bytes 1048576 | tf_op jit(solution)/shard_map/all_to_all | solution.py:677
  59.6 0.7 dynamic-slice_bitcast_fusion.phase
  60.3 12.1 %all-to-all-done.1.pieces = f32[32,32,128]{2,1,0:T(8,128)S(1)} async-done(((f32[32,32,128]{2,1,0:T(8,128)}), f32[32,32,128]{2,1,0:T(8,128)S(1)}, u32[]{:S(2)}, u32[]{:S(2)}) %all-to-all-start.1) | async-done | bytes 524320 | tf_op jit(solution)/shard_map/all_to_all | solution.py:677
  72.4 0.8 shard_map.146
  73.8 0.0 copy-start
  73.8 0.0 copy-start.1
  73.8 24.6 %all-gather = f32[1024,128]{1,0:T(8,128)S(1)} all-gather(f32[64,128]{1,0:T(8,128)S(1)} %get-tuple-element.58), channel_id=2, replica_groups=mesh['axial'=32,'girth'=16] {'girth'}, dimensions={0}, use_global_device_ids=true | all-gather | bytes 557056 | tf_op jit(solution)/shard_map/all_gather | solution.py:702
  98.4 0.0 copy-done
  98.4 0.0 copy-done.1
  98.4 1.2 %shard_map.147 = f32[2,16,4,128]{3,2,1,0:T(4,128)} custom-call(f32[16,64,128]{2,1,0:T(8,128)S(1)} %bitcast.12, f32[2,128]{1,0:T(2,128)S(1)} %dynamic-slice_bitcast_fusion.phase, bf16[2048,256]{1,0:T(8,128)(2,1)S(1)} %copy-done, bf16[2048,256]{1,0:T(8,128)(2,1)S(1)} %copy-done.1), custom_call_target="tpu_custom_call" | custom-call | flops 603979776 | bytes 2000000 | tf_op jit(solution)/shard_map/pallas_call | solution.py:559
  (1 shorter events, 0.0 us)
Async XLA Ops:
  0.6 9.3 %copy-start.2 = (bf16[1120,256]{1,0:T(8,128)(2,1)S(1)}, bf16[1120,256]{1,0:T(8,128)(2,1)}, u32[]{:S(2)}) copy-start(bf16[1120,256]{1,0:T(8,128)(2,1)} %constant.23.clone.table.tables.refs_0_) | copy-start | bytes 1720324
  0.6 9.3 %copy-start.4 = (f32[3,16,16,128]{3,2,1,0:T(8,128)S(1)}, f32[3,16,16,128]{3,2,1,0:T(8,128)}, u32[]{:S(2)}) copy-start(f32[3,16,16,128]{3,2,1,0:T(8,128)} %param.16) | copy-start | bytes 1179652
  3.1 9.5 %collective-permute-start = (f32[2,256,128]{2,1,0:T(8,128)}, f32[2,256,128]{2,1,0:T(8,128)S(1)}, u32[]{:S(2)}, u32[]{:S(2)}) collective-permute-start(f32[2,256,128]{2,1,0:T(8,128)} %get-tuple-element.35), channel_id=1, source_target_pairs={{0,1},{1,2},{2,3},{3,4},{4,5},{5,6},{6,7},{7,8},{8,9},{9,10},{10,1... | collective-permute-start | bytes 786440 | tf_op jit(solution)/shard_map/ppermute | solution.py:597
  5.8 6.8 %collective-permute-start.1 = (f32[2,256,128]{2,1,0:T(8,128)}, f32[2,256,128]{2,1,0:T(8,128)S(1)}, u32[]{:S(2)}, u32[]{:S(2)}) collective-permute-start(f32[2,256,128]{2,1,0:T(8,128)} %get-tuple-element.36), channel_id=1, source_target_pairs={{1,0},{2,1},{3,2},{4,3},{5,4},{6,5},{7,6},{8,7},{9,8},{10,9},{11,1... | collective-permute-start | bytes 786440 | tf_op jit(solution)/shard_map/ppermute | solution.py:598
  10.0 1.0 %copy-start.3 = (f32[4,16,16,128]{3,2,1,0:T(8,128)S(1)}, f32[4,16,16,128]{3,2,1,0:T(8,128)}, u32[]{:S(2)}) copy-start(f32[4,16,16,128]{3,2,1,0:T(8,128)} %param.15) | copy-start | bytes 1572868
  11.0 1.6 %copy-start.5 = (f32[16,16,128]{2,1,0:T(8,128)S(1)}, f32[16,16,128]{2,1,0:T(8,128)}, u32[]{:S(2)}) copy-start(f32[16,16,128]{2,1,0:T(8,128)} %param.17) | copy-start | bytes 393220
  16.6 5.8 %collective-permute-start.2 = (f32[16,3072]{1,0:T(8,128)S(1)}, f32[16,3072]{1,0:T(8,128)S(1)}, u32[]{:S(2)}, u32[]{:S(2)}) collective-permute-start(f32[16,3072]{1,0:T(8,128)S(1)} %get-tuple-element.42.high), channel_id=1, source_target_pairs={{0,16},{16,32},{32,48},{48,64},{64,80},{80,96},{96,112},{112,128},... | collective-permute-start | bytes 589832 | tf_op jit(solution)/shard_map/ppermute | solution.py:602
  19.8 7.0 %collective-permute-start.3 = (f32[16,3072]{1,0:T(8,128)S(1)}, f32[16,3072]{1,0:T(8,128)S(1)}, u32[]{:S(2)}, u32[]{:S(2)}) collective-permute-start(f32[16,3072]{1,0:T(8,128)S(1)} %get-tuple-element.41.low), channel_id=1, source_target_pairs={{16,0},{32,16},{48,32},{64,48},{80,64},{96,80},{112,96},{128,112},... | collective-permute-start | bytes 589832 | tf_op jit(solution)/shard_map/ppermute | solution.py:602
  26.9 13.7 %copy-start.6 = (f32[2,8,64]{2,1,0:T(8,128)S(1)}, f32[2,8,64]{2,1,0:T(8,128)}, u32[]{:S(2)}) copy-start(f32[2,8,64]{2,1,0:T(8,128)} %cycle_weights.1) | copy-start | bytes 12292
  26.9 13.7 %copy-start.7 = (f32[8,128]{1,0:T(8,128)S(1)}, f32[8,128]{1,0:T(8,128)}, u32[]{:S(2)}) copy-start(f32[8,128]{1,0:T(8,128)} %az_weights.1) | copy-start | bytes 12292
  32.9 7.7 %copy-start.11 = (s32[64]{0:T(128)S(1)}, s32[64]{0:T(128)}, u32[]{:S(2)}) copy-start(s32[64]{0:T(128)} %cycle_id.1) | copy-start | bytes 772
  32.9 7.7 %copy-start.8 = (s32[64]{0:T(128)S(1)}, s32[64]{0:T(128)}, u32[]{:S(2)}) copy-start(s32[64]{0:T(128)} %cycle_radial.1) | copy-start | bytes 772
  32.9 7.7 %copy-start.9 = (s32[64]{0:T(128)S(1)}, s32[64]{0:T(128)}, u32[]{:S(2)}) copy-start(s32[64]{0:T(128)} %cycle_axial.1) | copy-start | bytes 772
  32.9 7.7 %copy-start.10 = (s32[128]{0:T(128)S(1)}, s32[128]{0:T(128)}, u32[]{:S(2)}) copy-start(s32[128]{0:T(128)} %az_elem.1) | copy-start | bytes 1540
  32.9 7.9 %collective-permute-start.4 = (f32[16,1536]{1,0:T(8,128)S(1)}, f32[16,1536]{1,0:T(8,128)S(1)}, u32[]{:S(2)}, u32[]{:S(2)}) collective-permute-start(f32[16,1536]{1,0:T(8,128)S(1)} %get-tuple-element.48.own_high), channel_id=1, source_target_pairs={{0,16},{16,32},{32,48},{48,64},{64,80},{80,96},{96,112},{112,128},... | collective-permute-start | bytes 294920 | tf_op jit(solution)/shard_map/ppermute | solution.py:602
  39.0 7.2 %collective-permute-start.5 = (f32[16,1536]{1,0:T(8,128)S(1)}, f32[16,1536]{1,0:T(8,128)S(1)}, u32[]{:S(2)}, u32[]{:S(2)}) collective-permute-start(f32[16,1536]{1,0:T(8,128)S(1)} %get-tuple-element.47.own_low), channel_id=1, source_target_pairs={{16,0},{32,16},{48,32},{64,48},{80,64},{96,80},{112,96},{128,112},... | collective-permute-start | bytes 294920 | tf_op jit(solution)/shard_map/ppermute | solution.py:602
  49.2 23.2 %all-to-all-start.1 = ((f32[32,32,128]{2,1,0:T(8,128)}), f32[32,32,128]{2,1,0:T(8,128)S(1)}, u32[]{:S(2)}, u32[]{:S(2)}) async-start(f32[32,32,128]{2,1,0:T(8,128)} %get-tuple-element.54), calls=%async_computation.1 | async-start | bytes 1048576 | tf_op jit(solution)/shard_map/all_to_all | solution.py:677
  73.8 24.6 %copy-start = (bf16[2048,256]{1,0:T(8,128)(2,1)S(1)}, bf16[2048,256]{1,0:T(8,128)(2,1)}, u32[]{:S(2)}) copy-start(bf16[2048,256]{1,0:T(8,128)(2,1)} %constant.25.clone.table_high) | copy-start | bytes 3145732
  73.8 24.6 %copy-start.1 = (bf16[2048,256]{1,0:T(8,128)(2,1)S(1)}, bf16[2048,256]{1,0:T(8,128)(2,1)}, u32[]{:S(2)}) copy-start(bf16[2048,256]{1,0:T(8,128)(2,1)} %constant.26.clone.table_low) | copy-start | bytes 3145732

commit v4 on v3

--- a/solution.py
+++ b/solution.py
@@ -72,7 +72,9 @@
     eye = lambda n: np.eye(n, dtype=np.float32)
     axial = np.kron(eye(32), d)
     blocks = list(np_split(axial)) + list(np_split(axial.T))
-    for small in (np.kron(eye(4), d), np.kron(eye(8), d.T)):
+    ends = axial.T.reshape(16, 16, NODES)[:, [0, 15]].swapaxes(0, 1).reshape(32, NODES)
+    blocks += list(np_split(ends))
+    for small in (np.kron(eye(4), d), np.kron(eye(8), d.T), np.kron(eye(4), d.T)):
         high, low = np_split(small)
         row = np.concatenate([high, high, low], axis=1)
         blocks.append(np.pad(row, ((0, 0), (0, NODES - row.shape[1]))))
@@ -131,12 +133,24 @@
     return jnp.concatenate([square(table, 0), square(table, 0), square(table, 1)], axis=0)
 
 
+SMALL = 4 * NODES
+
+
+def ends_left(table):
+    high, low = table[SMALL : SMALL + 32, :], table[SMALL + 32 : SMALL + 64, :]
+    return jnp.concatenate([high, high, low], axis=1)
+
+
 def radial_small(table):
-    return table[4 * NODES : 4 * NODES + 32, :96]
+    return table[SMALL + 64 : SMALL + 96, :96]
 
 
 def radial_small_t(table):
-    return table[4 * NODES + 32 : 4 * NODES + 96, :192]
+    return table[SMALL + 96 : SMALL + 160, :192]
+
+
+def radial_faces_t(table):
+    return table[SMALL + 160 : SMALL + 192, :96]
 
 
 def radial_apply(x, matrix):
@@ -308,13 +322,42 @@
     return jnp.where((row == 0) | (row == 15), u, u - total * wide(inverse))
 
 
-def two_steps(u, geom, halo_geom, inverse, first, tables, state, second, low, high):
+def sum_faces(x):
+    summed = shared_local([lanes_of(x, k) for k in range(6)]).reshape(2, 16, WIDE)
+    pair = summed[:, 7:8, :] + summed[:, 8:9, :]
+    node = lax.broadcasted_iota(jnp.int32, summed.shape, 1)
+    return jnp.where((node == 7) | (node == 8), pair, summed)
+
+
+def face_action(v, geom, halo_geom, statics, table):
+    low, high = statics
+    radial, girthwise = [
+        wide(jnp.concatenate([static_part(low, k), static_part(high, k)], axis=0)) for k in (1, 2)
+    ]
+    nodes = v.reshape(16, 16, WIDE)
+    ends = jnp.concatenate([nodes[:, 0, :], nodes[:, 15, :]], axis=0)
+    face = left_mul(radial_faces_t(table), left_mul(radial_small(table), ends) * radial)
+    pieces = []
+    for tile in range(3):
+        span = slice(2 * tile * LANES, (2 * tile + 2) * LANES)
+        ga = halo_geom[1] if tile == 2 else twice(geom[1])
+        slope = left_mul(axial_left(table), v[:, span]) * ga
+        g = right_mul(ends[:, span], girth_right(table)) * girthwise[:, span]
+        pieces.append(left_mul(ends_left(table), slope) + right_mul(g, girth_right_t(table)))
+    return sum_faces(face + jnp.concatenate(pieces, axis=1))
+
+
+def two_steps(u, geom, halo_geom, inverse, first, statics, table, state, low, high):
     v = inner_update(u, first, inverse)
     state[...] = v
-    total = action(v, geom, halo_geom, tables)
-    second[...] = total
     put_faces(first, low, high, 0)
-    put_faces(total, low, high, WIDE)
+    faces = face_action(v, geom, halo_geom, statics, table)
+    low[:, WIDE : 2 * WIDE] = faces[0]
+    high[:, WIDE : 2 * WIDE] = faces[1]
+
+
+def second_kernel(state, geom, halo_geom, table, out):
+    out[...] = action(state[...], geom, halo_geom, table)
 
 
 STATIC = 2 * WIDE
@@ -322,7 +365,7 @@
 
 
 def halo_kernel(
-    left, right, own_total, field, mass, geom, tables, halo_geom, state, second, mass_out, ends_out, low, high
+    left, right, own_total, field, mass, geom, tables, halo_geom, state, mass_out, ends_out, low, high
 ):
     lane = lax.broadcasted_iota(jnp.int32, (NODES, LANES), 1)
 
@@ -353,7 +396,7 @@
     for k, x in enumerate([lumped, whole[0], whole[2], ends]):
         put_faces(x, low, high, STATIC + k * NARROW)
     start = jnp.concatenate([field[c] for c in range(C)] + [u], axis=1)
-    two_steps(start, geom, halo_geom, 1.0 / lumped, first, tables, state, second, low, high)
+    two_steps(start, geom, halo_geom, 1.0 / lumped, first, (low, high), tables, state, low, high)
 
 
 def static_part(ref, k):
@@ -385,10 +428,7 @@
     face = face + jnp.concatenate(pieces, axis=1)
     other = jnp.concatenate([static_part(got_low, 3), static_part(got_high, 3)], axis=0)
     beyond = face[32:] + wide(other) * w
-    beyond = shared_local([lanes_of(beyond, k) for k in range(6)]).reshape(2, 16, WIDE)
-    pair = beyond[:, 7:8, :] + beyond[:, 8:9, :]
-    node = lax.broadcasted_iota(jnp.int32, beyond.shape, 1)
-    beyond = jnp.where((node == 7) | (node == 8), pair, beyond)
+    beyond = sum_faces(beyond)
     beyond_low = beyond[0] + new_low[:, WIDE : 2 * WIDE]
     beyond_high = beyond[1] + new_high[:, WIDE : 2 * WIDE]
     node = lax.broadcasted_iota(jnp.int32, (16, 16, WIDE), 1)
@@ -400,7 +440,7 @@
 
 
 def middle_kernel(state, second, lumped, ends, low, high, got_low, got_high, geom, halo_geom, *refs):
-    tables, state_out, second_out, inverse_out, next_low, next_high = refs
+    tables, state_out, inverse_out, next_low, next_high = refs
     inverse = 1.0 / (
         lumped[...] + at_faces(static_part(got_low, 0), static_part(got_high, 0), NARROW)
     )
@@ -410,7 +450,7 @@
         state[...], second[...], inverse, ends[...], statics, (low, high), (got_low, got_high), tables
     )
     first = action(u, geom, halo_geom, tables)
-    two_steps(u, geom, halo_geom, inverse, first, tables, state_out, second_out, next_low, next_high)
+    two_steps(u, geom, halo_geom, inverse, first, (low, high), tables, state_out, next_low, next_high)
 
 
 def last_kernel(
@@ -603,10 +643,10 @@
 
     whole, narrow = (NODES, WIDE), (NODES, NARROW)
     face_static = (16, STATIC + 4 * NARROW)
-    halo_geom, state, second, lumped, ends, low, high = call(
+    halo_geom, state, lumped, ends, low, high = call(
         halo_kernel,
-        [(3, NODES, 2 * LANES), whole, whole, narrow, narrow, face_static, face_static],
-        4 * tile_flops,
+        [(3, NODES, 2 * LANES), whole, narrow, narrow, face_static, face_static],
+        2 * tile_flops,
         left,
         right,
         own_total,
@@ -616,10 +656,11 @@
         table,
     )
     got_low, got_high = exchange(low, high)
-    state, second, inverse, own_low, own_high = call(
+    (second,) = call(second_kernel, [whole], 3 * tile_flops, state, geom, halo_geom, table)
+    state, inverse, own_low, own_high = call(
         middle_kernel,
-        [whole, whole, narrow, (16, STATIC), (16, STATIC)],
-        6 * tile_flops,
+        [whole, narrow, (16, STATIC), (16, STATIC)],
+        4 * tile_flops,
         state,
         second,
         lumped,
@@ -633,6 +674,7 @@
         table,
     )
     new_low, new_high = exchange(own_low, own_high)
+    (second,) = call(second_kernel, [whole], 3 * tile_flops, state, geom, halo_geom, table)
 
     slot_count = cycle_id.shape[0]
     slab, girth_weight, select, header = call(

time: 100 us -> 99.3 us (level)
  waiting for transfers between devices: 23.3 us -> 18.4 us
  Pallas kernels: 19.1 us -> 23.1 us
    ppermute x4, waiting for transfers between devices: 11.2 us -> 6.34 us  [exchange(): return (lax.ppermute(high, 'axial', up), lax.ppermute(low, 'axial', down))]
    pallas_call x6 -> x8, Pallas kernels: 16 us -> 20 us  [call(): pl.pallas_call(kernel, out_shape=out_shape, in_specs=[vmem] * len(args),...]
  transfers between devices with their start and end apart: 7 -> 7, of which waited for: 4 -> 3; matrix products, arithmetic and copies ran while one was open for 1% -> 1% of each run, Pallas kernels for 2% -> 7%
where the time goes in v4:
time: 99.3 us; the launch traced here: 98.9 us
  starting transfers between devices  29.4 us (30%)
  blocking collectives  24.6 us (25%)
  Pallas kernels  23.1 us (23%)
  waiting for transfers between devices  18.4 us (19%)
  local copies, waits for them, and re-layouts  1.8 us (2%)
  between operations  1.56 us (2%)
    all_gather x1, blocking collectives, body(): rows = lax.all_gather(rows, 'girth')  24.6 us
    pallas_call x8, Pallas kernels, call(): pl.pallas_call(kernel, out_shape=out_shape, in_specs=[vmem] * len(args),...  20 us
    all_to_all x1, waiting for transfers between devices, body(): pieces = lax.all_to_all(packed, 'axial', 0, 0)  12.1 us
    ppermute x4, starting transfers between devices, exchange(): return (lax.ppermute(high, 'axial', up), lax.ppermute(low, 'axial', down))  12 us
    all_to_all x1, starting transfers between devices, body(): pieces = lax.all_to_all(packed, 'axial', 0, 0)  10.5 us
    ppermute x4, waiting for transfers between devices, exchange(): return (lax.ppermute(high, 'axial', up), lax.ppermute(low, 'axial', down))  6.34 us
    ppermute x1, starting transfers between devices, body(): right = lax.ppermute(to_left, 'girth', back)  4.22 us
    ppermute x1, starting transfers between devices, body(): left = lax.ppermute(to_right, 'girth', around)  2.7 us
  transfers between devices with their start and end apart: 7, of which 3 were waited for; matrix products, arithmetic and copies ran while one was open for 1% of the time, Pallas kernels for 7%

profile of v4, /device:TPU:1, one launch (start us, length us, event | category | flops | bytes accessed | tf_op | source)
XLA Modules:
  0.0 98.9 jit_solution(3428271804077799571)
XLA Ops:
  0.6 0.0 copy-start.2
  0.6 0.0 copy-start.4
  0.7 2.4 %shard_map.140 = (f32[2,256,128]{2,1,0:T(8,128)}, f32[2,256,128]{2,1,0:T(8,128)}) custom-call(f32[4,256,128]{2,1,0:T(8,128)} %bitcast.13, f32[3,256,128]{2,1,0:T(8,128)} %bitcast.16, f32[256,128]{1,0:T(8,128)} %bitcast.22), custom_call_target="tpu_custom_call" | custom-call | tf_op jit(solution)/shard_map/pallas_call | solution.py:611
  3.1 2.7 %collective-permute-start = (f32[2,256,128]{2,1,0:T(8,128)}, f32[2,256,128]{2,1,0:T(8,128)S(1)}, u32[]{:S(2)}, u32[]{:S(2)}) collective-permute-start(f32[2,256,128]{2,1,0:T(8,128)} %get-tuple-element.33), channel_id=1, source_target_pairs={{0,1},{1,2},{2,3},{3,4},{4,5},{5,6},{6,7},{7,8},{8,9},{9,10},{10,1... | collective-permute-start | bytes 786440 | tf_op jit(solution)/shard_map/ppermute | solution.py:637
  5.8 4.2 %collective-permute-start.1 = (f32[2,256,128]{2,1,0:T(8,128)}, f32[2,256,128]{2,1,0:T(8,128)S(1)}, u32[]{:S(2)}, u32[]{:S(2)}) collective-permute-start(f32[2,256,128]{2,1,0:T(8,128)} %get-tuple-element.34), channel_id=1, source_target_pairs={{1,0},{2,1},{3,2},{4,3},{5,4},{6,5},{7,6},{8,7},{9,8},{10,9},{11,1... | collective-permute-start | bytes 786440 | tf_op jit(solution)/shard_map/ppermute | solution.py:638
  10.0 0.0 copy-done.2
  10.0 0.0 copy-done.4
  10.0 1.0 %copy-done.3 = f32[4,16,16,128]{3,2,1,0:T(8,128)S(1)} copy-done((f32[4,16,16,128]{3,2,1,0:T(8,128)S(1)}, f32[4,16,16,128]{3,2,1,0:T(8,128)}, u32[]{:S(2)}) %copy-start.3) | copy-done | bytes 524312
  11.0 1.5 %shard_map.141.own_total = f32[256,512]{1,0:T(8,128)S(1)} custom-call(f32[4,256,128]{2,1,0:T(8,128)S(1)} %bitcast.14, f32[3,256,128]{2,1,0:T(8,128)S(1)} %bitcast.17, bf16[1216,256]{1,0:T(8,128)(2,1)S(1)} %copy-done.2), custom_call_target="tpu_custom_call" | custom-call | flops 1207959552 | bytes 2000000 | tf_op jit(solution)/shard_map/pallas_call | solution.py:599
  12.6 0.0 collective-permute-done.left
  12.6 0.0 collective-permute-done.1.right
  12.6 0.0 copy-done.5
  12.6 0.0 copy-start.6
  12.6 0.0 copy-start.7
  12.6 3.8 %shard_map.142 = (f32[3,256,256]{2,1,0:T(8,128)S(1)}, f32[256,768]{1,0:T(8,128)S(1)}, f32[256,384]{1,0:T(8,128)S(1)}, f32[256,384]{1,0:T(8,128)S(1)}, f32[16,3072]{1,0:T(8,128)S(1)}, /*index=5*/f32[16,3072]{1,0:T(8,128)S(1)}) custom-call(f32[2,256,128]{2,1,0:T(8,128)S(1)} %collective-permute-done.left, f32[2,256,128]{2,1,0:T(8,128)S(1)} %collective-permute-done.1.right, ...), custom_call_target="tpu_custom_call" | custom-call | flops 1207959552 | bytes 2000000 | tf_op jit(solution)/shard_map/pallas_call | solution.py:599
  16.4 0.0 copy-start.11
  16.4 0.0 copy-start.8
  16.4 0.0 copy-start.9
  16.4 0.0 copy-start.10
  16.5 3.3 %collective-permute-start.2 = (f32[16,3072]{1,0:T(8,128)S(1)}, f32[16,3072]{1,0:T(8,128)S(1)}, u32[]{:S(2)}, u32[]{:S(2)}) collective-permute-start(f32[16,3072]{1,0:T(8,128)S(1)} %get-tuple-element.40.high), channel_id=1, source_target_pairs={{0,16},{16,32},{32,48},{48,64},{64,80},{80,96},{96,112},{112,128},... | collective-permute-start | bytes 589832 | tf_op jit(solution)/shard_map/ppermute | solution.py:642
  19.7 1.3 %collective-permute-start.3 = (f32[16,3072]{1,0:T(8,128)S(1)}, f32[16,3072]{1,0:T(8,128)S(1)}, u32[]{:S(2)}, u32[]{:S(2)}) collective-permute-start(f32[16,3072]{1,0:T(8,128)S(1)} %get-tuple-element.39.low), channel_id=1, source_target_pairs={{16,0},{32,16},{48,32},{64,48},{80,64},{96,80},{112,96},{128,112},... | collective-permute-start | bytes 589832 | tf_op jit(solution)/shard_map/ppermute | solution.py:642
  21.0 0.0 copy-done.6
  21.1 0.0 copy-done.7
  21.1 0.0 copy-done.11
  21.1 0.0 copy-done.8
  21.1 0.0 copy-done.9
  21.1 0.0 copy-done.10
  21.1 0.2 shard_map.146
  21.3 2.4 %shard_map.143.second = f32[256,768]{1,0:T(8,128)S(1)} custom-call(f32[256,768]{1,0:T(8,128)S(1)} %get-tuple-element.35.state, f32[3,256,128]{2,1,0:T(8,128)S(1)} %bitcast.19, f32[3,256,256]{2,1,0:T(8,128)S(1)} %get-tuple-element.36.halo_geom, bf16[1216,256]{1,0:T(8,128)(2,1)S(1)} %copy-done.2), custom_call_target="tpu_custom_call" | custom-call | flops 1811939328 | bytes 2000000 | tf_op jit(solution)/shard_map/pallas_call | solution.py:599
  23.8 0.0 collective-permute-done.2.got_low
  23.8 3.0 %collective-permute-done.3.got_high = f32[16,3072]{1,0:T(8,128)S(1)} collective-permute-done((f32[16,3072]{1,0:T(8,128)S(1)}, f32[16,3072]{1,0:T(8,128)S(1)}, u32[]{:S(2)}, u32[]{:S(2)}) %collective-permute-start.3) | collective-permute-done | bytes 196640 | tf_op jit(solution)/shard_map/ppermute | solution.py:642
  26.8 5.5 %shard_map.144 = (f32[256,768]{1,0:T(8,128)S(1)}, f32[256,384]{1,0:T(8,128)S(1)}, f32[16,1536]{1,0:T(8,128)S(1)}, f32[16,1536]{1,0:T(8,128)S(1)}) custom-call(f32[256,768]{1,0:T(8,128)S(1)} %get-tuple-element.35.state, f32[256,768]{1,0:T(8,128)S(1)} %shard_map.143.second, f32[256,384]{1,0:T(8,128)S(1)} %get-tuple-element.37.lumped, ...), custom_call_target="tpu_custom_call" | custom-call | flops 2415919104 | bytes 2000000 | tf_op jit(solution)/shard_map/pallas_call | solution.py:599
  32.3 6.0 %collective-permute-start.4 = (f32[16,1536]{1,0:T(8,128)S(1)}, f32[16,1536]{1,0:T(8,128)S(1)}, u32[]{:S(2)}, u32[]{:S(2)}) collective-permute-start(f32[16,1536]{1,0:T(8,128)S(1)} %get-tuple-element.44.own_high), channel_id=1, source_target_pairs={{0,16},{16,32},{32,48},{48,64},{64,80},{80,96},{96,112},{112,128},... | collective-permute-start | bytes 294920 | tf_op jit(solution)/shard_map/ppermute | solution.py:642
  38.2 1.5 %collective-permute-start.5 = (f32[16,1536]{1,0:T(8,128)S(1)}, f32[16,1536]{1,0:T(8,128)S(1)}, u32[]{:S(2)}, u32[]{:S(2)}) collective-permute-start(f32[16,1536]{1,0:T(8,128)S(1)} %get-tuple-element.43.own_low), channel_id=1, source_target_pairs={{16,0},{32,16},{48,32},{64,48},{80,64},{96,80},{112,96},{128,112},... | collective-permute-start | bytes 294920 | tf_op jit(solution)/shard_map/ppermute | solution.py:642
  39.7 2.4 %shard_map.145.second = f32[256,768]{1,0:T(8,128)S(1)} custom-call(f32[256,768]{1,0:T(8,128)S(1)} %get-tuple-element.41.state, f32[3,256,128]{2,1,0:T(8,128)S(1)} %bitcast.21, f32[3,256,256]{2,1,0:T(8,128)S(1)} %get-tuple-element.36.halo_geom, bf16[1216,256]{1,0:T(8,128)(2,1)S(1)} %copy-done.2), custom_call_target="tpu_custom_call" | custom-call | flops 1811939328 | bytes 2000000 | tf_op jit(solution)/shard_map/pallas_call | solution.py:599
  42.1 0.0 collective-permute-done.4.new_low
  42.1 3.3 %collective-permute-done.5.new_high = f32[16,1536]{1,0:T(8,128)S(1)} collective-permute-done((f32[16,1536]{1,0:T(8,128)S(1)}, f32[16,1536]{1,0:T(8,128)S(1)}, u32[]{:S(2)}, u32[]{:S(2)}) %collective-permute-start.5) | collective-permute-done | bytes 98336 | tf_op jit(solution)/shard_map/ppermute | solution.py:642
  45.4 2.9 %shard_map.147 = (f32[4,256,128]{2,1,0:T(8,128)}, f32[32,32,128]{2,1,0:T(8,128)}, f32[64,512]{1,0:T(8,128)S(1)}) custom-call(f32[256,768]{1,0:T(8,128)S(1)} %get-tuple-element.41.state, f32[256,768]{1,0:T(8,128)S(1)} %shard_map.145.second, f32[256,384]{1,0:T(8,128)S(1)} %get-tuple-element.42.inverse, f32[256,384]{1,0:T(8,128)S(1)} %get-tuple-element.38.ends, ...), custom_call_target="tpu_custom_call" | custom-call | flops 603979776 | bytes 2000000 | tf_op jit(solution)/shard_map/pallas_call | solution.py:599
  48.4 10.5 %all-to-all-start.1 = ((f32[32,32,128]{2,1,0:T(8,128)}), f32[32,32,128]{2,1,0:T(8,128)S(1)}, u32[]{:S(2)}, u32[]{:S(2)}) async-start(f32[32,32,128]{2,1,0:T(8,128)} %get-tuple-element.50), calls=%async_computation.1 | async-start | bytes 1048576 | tf_op jit(solution)/shard_map/all_to_all | solution.py:719
  58.8 0.7 dynamic-slice_bitcast_fusion.phase
  59.5 12.1 %all-to-all-done.1.pieces = f32[32,32,128]{2,1,0:T(8,128)S(1)} async-done(((f32[32,32,128]{2,1,0:T(8,128)}), f32[32,32,128]{2,1,0:T(8,128)S(1)}, u32[]{:S(2)}, u32[]{:S(2)}) %all-to-all-start.1) | async-done | bytes 524320 | tf_op jit(solution)/shard_map/all_to_all | solution.py:719
  71.6 0.8 shard_map.148
  73.0 0.0 copy-start
  73.0 0.0 copy-start.1
  73.1 24.6 %all-gather = f32[1024,128]{1,0:T(8,128)S(1)} all-gather(f32[64,128]{1,0:T(8,128)S(1)} %get-tuple-element.54), channel_id=2, replica_groups=mesh['axial'=32,'girth'=16] {'girth'}, dimensions={0}, use_global_device_ids=true | all-gather | bytes 557056 | tf_op jit(solution)/shard_map/all_gather | solution.py:744
  97.7 0.0 copy-done
  97.7 0.0 copy-done.1
  97.7 1.2 %shard_map.149 = f32[2,16,4,128]{3,2,1,0:T(4,128)} custom-call(f32[16,64,128]{2,1,0:T(8,128)S(1)} %bitcast.12, f32[2,128]{1,0:T(2,128)S(1)} %dynamic-slice_bitcast_fusion.phase, bf16[2048,256]{1,0:T(8,128)(2,1)S(1)} %copy-done, bf16[2048,256]{1,0:T(8,128)(2,1)S(1)} %copy-done.1), custom_call_target="tpu_custom_call" | custom-call | flops 603979776 | bytes 2000000 | tf_op jit(solution)/shard_map/pallas_call | solution.py:599
  (3 shorter events, 0.0 us)
Async XLA Ops:
  0.6 9.3 %copy-start.2 = (bf16[1216,256]{1,0:T(8,128)(2,1)S(1)}, bf16[1216,256]{1,0:T(8,128)(2,1)}, u32[]{:S(2)}) copy-start(bf16[1216,256]{1,0:T(8,128)(2,1)} %constant.23.clone.table.tables.refs_0_) | copy-start | bytes 1867780
  0.6 9.3 %copy-start.4 = (f32[3,16,16,128]{3,2,1,0:T(8,128)S(1)}, f32[3,16,16,128]{3,2,1,0:T(8,128)}, u32[]{:S(2)}) copy-start(f32[3,16,16,128]{3,2,1,0:T(8,128)} %param.16) | copy-start | bytes 1179652
  3.1 9.5 %collective-permute-start = (f32[2,256,128]{2,1,0:T(8,128)}, f32[2,256,128]{2,1,0:T(8,128)S(1)}, u32[]{:S(2)}, u32[]{:S(2)}) collective-permute-start(f32[2,256,128]{2,1,0:T(8,128)} %get-tuple-element.33), channel_id=1, source_target_pairs={{0,1},{1,2},{2,3},{3,4},{4,5},{5,6},{6,7},{7,8},{8,9},{9,10},{10,1... | collective-permute-start | bytes 786440 | tf_op jit(solution)/shard_map/ppermute | solution.py:637
  5.8 6.8 %collective-permute-start.1 = (f32[2,256,128]{2,1,0:T(8,128)}, f32[2,256,128]{2,1,0:T(8,128)S(1)}, u32[]{:S(2)}, u32[]{:S(2)}) collective-permute-start(f32[2,256,128]{2,1,0:T(8,128)} %get-tuple-element.34), channel_id=1, source_target_pairs={{1,0},{2,1},{3,2},{4,3},{5,4},{6,5},{7,6},{8,7},{9,8},{10,9},{11,1... | collective-permute-start | bytes 786440 | tf_op jit(solution)/shard_map/ppermute | solution.py:638
  10.0 1.0 %copy-start.3 = (f32[4,16,16,128]{3,2,1,0:T(8,128)S(1)}, f32[4,16,16,128]{3,2,1,0:T(8,128)}, u32[]{:S(2)}) copy-start(f32[4,16,16,128]{3,2,1,0:T(8,128)} %param.15) | copy-start | bytes 1572868
  11.0 1.6 %copy-start.5 = (f32[16,16,128]{2,1,0:T(8,128)S(1)}, f32[16,16,128]{2,1,0:T(8,128)}, u32[]{:S(2)}) copy-start(f32[16,16,128]{2,1,0:T(8,128)} %param.17) | copy-start | bytes 393220
  12.6 8.4 %copy-start.6 = (f32[2,8,64]{2,1,0:T(8,128)S(1)}, f32[2,8,64]{2,1,0:T(8,128)}, u32[]{:S(2)}) copy-start(f32[2,8,64]{2,1,0:T(8,128)} %cycle_weights.1) | copy-start | bytes 12292
  12.6 8.4 %copy-start.7 = (f32[8,128]{1,0:T(8,128)S(1)}, f32[8,128]{1,0:T(8,128)}, u32[]{:S(2)}) copy-start(f32[8,128]{1,0:T(8,128)} %az_weights.1) | copy-start | bytes 12292
  16.4 4.7 %copy-start.11 = (s32[64]{0:T(128)S(1)}, s32[64]{0:T(128)}, u32[]{:S(2)}) copy-start(s32[64]{0:T(128)} %cycle_id.1) | copy-start | bytes 772
  16.4 4.7 %copy-start.8 = (s32[64]{0:T(128)S(1)}, s32[64]{0:T(128)}, u32[]{:S(2)}) copy-start(s32[64]{0:T(128)} %cycle_radial.1) | copy-start | bytes 772
  16.4 4.7 %copy-start.9 = (s32[64]{0:T(128)S(1)}, s32[64]{0:T(128)}, u32[]{:S(2)}) copy-start(s32[64]{0:T(128)} %cycle_axial.1) | copy-start | bytes 772
  16.4 4.7 %copy-start.10 = (s32[128]{0:T(128)S(1)}, s32[128]{0:T(128)}, u32[]{:S(2)}) copy-start(s32[128]{0:T(128)} %az_elem.1) | copy-start | bytes 1540
  16.5 7.3 %collective-permute-start.2 = (f32[16,3072]{1,0:T(8,128)S(1)}, f32[16,3072]{1,0:T(8,128)S(1)}, u32[]{:S(2)}, u32[]{:S(2)}) collective-permute-start(f32[16,3072]{1,0:T(8,128)S(1)} %get-tuple-element.40.high), channel_id=1, source_target_pairs={{0,16},{16,32},{32,48},{48,64},{64,80},{80,96},{96,112},{112,128},... | collective-permute-start | bytes 589832 | tf_op jit(solution)/shard_map/ppermute | solution.py:642
  19.7 7.0 %collective-permute-start.3 = (f32[16,3072]{1,0:T(8,128)S(1)}, f32[16,3072]{1,0:T(8,128)S(1)}, u32[]{:S(2)}, u32[]{:S(2)}) collective-permute-start(f32[16,3072]{1,0:T(8,128)S(1)} %get-tuple-element.39.low), channel_id=1, source_target_pairs={{16,0},{32,16},{48,32},{64,48},{80,64},{96,80},{112,96},{128,112},... | collective-permute-start | bytes 589832 | tf_op jit(solution)/shard_map/ppermute | solution.py:642
  32.3 9.9 %collective-permute-start.4 = (f32[16,1536]{1,0:T(8,128)S(1)}, f32[16,1536]{1,0:T(8,128)S(1)}, u32[]{:S(2)}, u32[]{:S(2)}) collective-permute-start(f32[16,1536]{1,0:T(8,128)S(1)} %get-tuple-element.44.own_high), channel_id=1, source_target_pairs={{0,16},{16,32},{32,48},{48,64},{64,80},{80,96},{96,112},{112,128},... | collective-permute-start | bytes 294920 | tf_op jit(solution)/shard_map/ppermute | solution.py:642
  38.2 7.2 %collective-permute-start.5 = (f32[16,1536]{1,0:T(8,128)S(1)}, f32[16,1536]{1,0:T(8,128)S(1)}, u32[]{:S(2)}, u32[]{:S(2)}) collective-permute-start(f32[16,1536]{1,0:T(8,128)S(1)} %get-tuple-element.43.own_low), channel_id=1, source_target_pairs={{16,0},{32,16},{48,32},{64,48},{80,64},{96,80},{112,96},{128,112},... | collective-permute-start | bytes 294920 | tf_op jit(solution)/shard_map/ppermute | solution.py:642
  48.4 23.2 %all-to-all-start.1 = ((f32[32,32,128]{2,1,0:T(8,128)}), f32[32,32,128]{2,1,0:T(8,128)S(1)}, u32[]{:S(2)}, u32[]{:S(2)}) async-start(f32[32,32,128]{2,1,0:T(8,128)} %get-tuple-element.50), calls=%async_computation.1 | async-start | bytes 1048576 | tf_op jit(solution)/shard_map/all_to_all | solution.py:719
  73.0 24.7 %copy-start = (bf16[2048,256]{1,0:T(8,128)(2,1)S(1)}, bf16[2048,256]{1,0:T(8,128)(2,1)}, u32[]{:S(2)}) copy-start(bf16[2048,256]{1,0:T(8,128)(2,1)} %constant.25.clone.table_high) | copy-start | bytes 3145732
  73.0 24.7 %copy-start.1 = (bf16[2048,256]{1,0:T(8,128)(2,1)S(1)}, bf16[2048,256]{1,0:T(8,128)(2,1)}, u32[]{:S(2)}) copy-start(bf16[2048,256]{1,0:T(8,128)(2,1)} %constant.26.clone.table_low) | copy-start | bytes 3145732

commit v5 on v4

--- a/solution.py
+++ b/solution.py
@@ -136,9 +136,8 @@
 SMALL = 4 * NODES
 
 
-def ends_left(table):
-    high, low = table[SMALL : SMALL + 32, :], table[SMALL + 32 : SMALL + 64, :]
-    return jnp.concatenate([high, high, low], axis=1)
+def ends_pair(table):
+    return table[SMALL : SMALL + 64, :]
 
 
 def radial_small(table):
@@ -193,15 +192,41 @@
     return jnp.broadcast_to(column[None], (16, 16, LANES)).reshape(rows, LANES)
 
 
-def stiff(u, gr, ga, gg, table):
+def stiff_many(us, geoms, table):
     d = derivative_table()
-    high, low = split(u)
-    axial = dot(axial_left(table), jnp.concatenate([high, low, high], axis=0)) * ga
-    girth = dot(jnp.concatenate([high, low, high], axis=1), girth_right(table)) * gg
-    radial = radial_apply(radial_apply(u, d) * gr, d.T)
-    return (
-        left_mul(axial_left_t(table), axial) + right_mul(girth, girth_right_t(table)) + radial
-    )
+    halves = [split(u) for u in us]
+    rows = [jnp.concatenate([high, low, high], axis=1) for high, low in halves]
+    girth = dot(jnp.concatenate(rows, axis=0), girth_right(table))
+    girth = girth * jnp.concatenate([g[2] for g in geoms], axis=0)
+    girth = right_mul(girth, girth_right_t(table))
+    outs = []
+    for k, (u, (high, low), (gr, ga, _)) in enumerate(zip(us, halves, geoms)):
+        axial = dot(axial_left(table), jnp.concatenate([high, low, high], axis=0)) * ga
+        radial = radial_apply(radial_apply(u, d) * gr, d.T)
+        part = girth[k * NODES : (k + 1) * NODES]
+        outs.append(left_mul(axial_left_t(table), axial) + part + radial)
+    return outs
+
+
+def left_pair(both, x):
+    high, low = split(x)
+    rows = both.shape[0] // 2
+    first = dot(both, high)
+    return first[:rows] + first[rows:] + dot(both[:rows], low)
+
+
+def girth_faces(x, factor, repeat, table):
+    rows = x.shape[0]
+    stacked = jnp.concatenate([x[:, k * NODES : (k + 1) * NODES] for k in range(3)], axis=0)
+    slope = right_mul(stacked, girth_right(table))
+    scaled = []
+    for k in range(3):
+        part = slope[k * rows : (k + 1) * rows]
+        part = jnp.concatenate([part] * repeat, axis=0)
+        scaled.append(part * factor[:, k * NODES : (k + 1) * NODES])
+    moved = right_mul(jnp.concatenate(scaled, axis=0), girth_right_t(table))
+    rows = rows * repeat
+    return jnp.concatenate([moved[k * rows : (k + 1) * rows] for k in range(3)], axis=1)
 
 
 def twice(x):
@@ -279,10 +304,9 @@
 
 
 def own_kernel(field, geom, table, out):
-    gr, ga, gg = [twice(geom[k]) for k in range(3)]
-    for pair in range(2):
-        u = jnp.concatenate([field[2 * pair], field[2 * pair + 1]], axis=1)
-        out[:, 2 * pair * LANES : (2 * pair + 2) * LANES] = stiff(u, gr, ga, gg, table)
+    geoms = tuple(twice(geom[k]) for k in range(3))
+    us = [jnp.concatenate([field[2 * k], field[2 * k + 1]], axis=1) for k in range(2)]
+    out[...] = jnp.concatenate(stiff_many(us, [geoms] * 2, table), axis=1)
 
 
 def at_faces(low, high, width):
@@ -307,12 +331,11 @@
 
 
 def action(u, geom, halo_geom, tables):
-    gr, ga, gg = [twice(geom[k]) for k in range(3)]
+    own = tuple(twice(geom[k]) for k in range(3))
+    geoms = [own, own, tuple(halo_geom[k] for k in range(3))]
+    us = [u[:, k * NODES : (k + 1) * NODES] for k in range(3)]
     parts = []
-    for tile in range(3):
-        if tile == 2:
-            gr, ga, gg = [halo_geom[k] for k in range(3)]
-        t = stiff(u[:, 2 * tile * LANES : (2 * tile + 2) * LANES], gr, ga, gg, tables)
+    for t in stiff_many(us, geoms, tables):
         parts += [lanes_of(t, 0), lanes_of(t, 1)]
     return sum_nodes(shared_local(parts)).reshape(NODES, WIDE)
 
@@ -337,13 +360,12 @@
     nodes = v.reshape(16, 16, WIDE)
     ends = jnp.concatenate([nodes[:, 0, :], nodes[:, 15, :]], axis=0)
     face = left_mul(radial_faces_t(table), left_mul(radial_small(table), ends) * radial)
+    face = face + girth_faces(ends, girthwise, 1, table)
     pieces = []
     for tile in range(3):
-        span = slice(2 * tile * LANES, (2 * tile + 2) * LANES)
         ga = halo_geom[1] if tile == 2 else twice(geom[1])
-        slope = left_mul(axial_left(table), v[:, span]) * ga
-        g = right_mul(ends[:, span], girth_right(table)) * girthwise[:, span]
-        pieces.append(left_mul(ends_left(table), slope) + right_mul(g, girth_right_t(table)))
+        slope = left_pair(table[: 2 * NODES, :], v[:, tile * NODES : (tile + 1) * NODES]) * ga
+        pieces.append(left_pair(ends_pair(table), slope))
     return sum_faces(face + jnp.concatenate(pieces, axis=1))
 
 
@@ -381,7 +403,7 @@
         halo_geom[k] = g
         geoms.append(g)
     u = jnp.concatenate([left[0], right[0]], axis=1)
-    t = stiff(u, *geoms, tables)
+    (t,) = stiff_many([u], [tuple(geoms)], tables)
     parts = [own_total[:, c * LANES : (c + 1) * LANES] for c in range(C)]
     first = sum_nodes(shared_local(parts + [lanes_of(t, 0), lanes_of(t, 1)]))
     first = first.reshape(NODES, WIDE)
@@ -419,13 +441,7 @@
     ]
     slope = left_mul(radial_small(tables), w)
     face = left_mul(radial_small_t(tables), jnp.concatenate([slope, slope], axis=0) * radial)
-    pieces = []
-    for tile in range(3):
-        span = slice(2 * tile * LANES, (2 * tile + 2) * LANES)
-        g = right_mul(w[:, span], girth_right(tables))
-        y = jnp.concatenate([g, g], axis=0) * girthwise[:, span]
-        pieces.append(right_mul(y, girth_right_t(tables)))
-    face = face + jnp.concatenate(pieces, axis=1)
+    face = face + girth_faces(w, girthwise, 2, tables)
     other = jnp.concatenate([static_part(got_low, 3), static_part(got_high, 3)], axis=0)
     beyond = face[32:] + wide(other) * w
     beyond = sum_faces(beyond)

time: 99.3 us -> 98.5 us (level)
  no operation moved by 1% of the time
where the time goes in v5:
time: 98.5 us; the launch traced here: 98.1 us
  starting transfers between devices  29.5 us (30%)
  blocking collectives  24.6 us (25%)
  Pallas kernels  22.2 us (23%)
  waiting for transfers between devices  18.4 us (19%)
  local copies, waits for them, and re-layouts  1.8 us (2%)
  between operations  1.56 us (2%)
    all_gather x1, blocking collectives, body(): rows = lax.all_gather(rows, 'girth')  24.6 us
    pallas_call x8, Pallas kernels, call(): pl.pallas_call(kernel, out_shape=out_shape, in_specs=[vmem] * len(args),...  19.1 us
    ppermute x4, starting transfers between devices, exchange(): return (lax.ppermute(high, 'axial', up), lax.ppermute(low, 'axial', down))  12.1 us
    all_to_all x1, waiting for transfers between devices, body(): pieces = lax.all_to_all(packed, 'axial', 0, 0)  12.1 us
    all_to_all x1, starting transfers between devices, body(): pieces = lax.all_to_all(packed, 'axial', 0, 0)  10.5 us
    ppermute x4, waiting for transfers between devices, exchange(): return (lax.ppermute(high, 'axial', up), lax.ppermute(low, 'axial', down))  6.32 us
    ppermute x1, starting transfers between devices, body(): right = lax.ppermute(to_left, 'girth', back)  4.22 us
    ppermute x1, starting transfers between devices, body(): left = lax.ppermute(to_right, 'girth', around)  2.7 us
  transfers between devices with their start and end apart: 7, of which 3 were waited for; matrix products, arithmetic and copies ran while one was open for 1% of the time, Pallas kernels for 7%

profile of v5, /device:TPU:1, one launch (start us, length us, event | category | flops | bytes accessed | tf_op | source)
XLA Modules:
  0.0 98.1 jit_solution(15902129615493947209)
XLA Ops:
  0.6 0.0 copy-start.2
  0.6 0.0 copy-start.4
  0.7 2.4 %shard_map.140 = (f32[2,256,128]{2,1,0:T(8,128)}, f32[2,256,128]{2,1,0:T(8,128)}) custom-call(f32[4,256,128]{2,1,0:T(8,128)} %bitcast.13, f32[3,256,128]{2,1,0:T(8,128)} %bitcast.16, f32[256,128]{1,0:T(8,128)} %bitcast.22), custom_call_target="tpu_custom_call" | custom-call | tf_op jit(solution)/shard_map/pallas_call | solution.py:627
  3.1 2.7 %collective-permute-start = (f32[2,256,128]{2,1,0:T(8,128)}, f32[2,256,128]{2,1,0:T(8,128)S(1)}, u32[]{:S(2)}, u32[]{:S(2)}) collective-permute-start(f32[2,256,128]{2,1,0:T(8,128)} %get-tuple-element.33), channel_id=1, source_target_pairs={{0,1},{1,2},{2,3},{3,4},{4,5},{5,6},{6,7},{7,8},{8,9},{9,10},{10,1... | collective-permute-start | bytes 786440 | tf_op jit(solution)/shard_map/ppermute | solution.py:653
  5.8 4.2 %collective-permute-start.1 = (f32[2,256,128]{2,1,0:T(8,128)}, f32[2,256,128]{2,1,0:T(8,128)S(1)}, u32[]{:S(2)}, u32[]{:S(2)}) collective-permute-start(f32[2,256,128]{2,1,0:T(8,128)} %get-tuple-element.34), channel_id=1, source_target_pairs={{1,0},{2,1},{3,2},{4,3},{5,4},{6,5},{7,6},{8,7},{9,8},{10,9},{11,1... | collective-permute-start | bytes 786440 | tf_op jit(solution)/shard_map/ppermute | solution.py:654
  10.0 0.0 copy-done.2
  10.0 0.0 copy-done.4
  10.0 1.0 %copy-done.3 = f32[4,16,16,128]{3,2,1,0:T(8,128)S(1)} copy-done((f32[4,16,16,128]{3,2,1,0:T(8,128)S(1)}, f32[4,16,16,128]{3,2,1,0:T(8,128)}, u32[]{:S(2)}) %copy-start.3) | copy-done | bytes 524312
  11.0 1.4 %shard_map.141.own_total = f32[256,512]{1,0:T(8,128)S(1)} custom-call(f32[4,256,128]{2,1,0:T(8,128)S(1)} %bitcast.14, f32[3,256,128]{2,1,0:T(8,128)S(1)} %bitcast.17, bf16[1216,256]{1,0:T(8,128)(2,1)S(1)} %copy-done.2), custom_call_target="tpu_custom_call" | custom-call | flops 1207959552 | bytes 2000000 | tf_op jit(solution)/shard_map/pallas_call | solution.py:615
  12.4 0.0 collective-permute-done.left
  12.4 0.0 collective-permute-done.1.right
  12.5 0.0 copy-done.5
  12.5 0.0 copy-start.6
  12.5 0.0 copy-start.7
  12.5 3.4 %shard_map.142 = (f32[3,256,256]{2,1,0:T(8,128)S(1)}, f32[256,768]{1,0:T(8,128)S(1)}, f32[256,384]{1,0:T(8,128)S(1)}, f32[256,384]{1,0:T(8,128)S(1)}, f32[16,3072]{1,0:T(8,128)S(1)}, /*index=5*/f32[16,3072]{1,0:T(8,128)S(1)}) custom-call(f32[2,256,128]{2,1,0:T(8,128)S(1)} %collective-permute-done.left, f32[2,256,128]{2,1,0:T(8,128)S(1)} %collective-permute-done.1.right, ...), custom_call_target="tpu_custom_call" | custom-call | flops 1207959552 | bytes 2000000 | tf_op jit(solution)/shard_map/pallas_call | solution.py:615
  15.9 0.0 copy-start.11
  15.9 0.0 copy-start.8
  15.9 0.0 copy-start.9
  16.0 0.0 copy-start.10
  16.0 3.4 %collective-permute-start.2 = (f32[16,3072]{1,0:T(8,128)S(1)}, f32[16,3072]{1,0:T(8,128)S(1)}, u32[]{:S(2)}, u32[]{:S(2)}) collective-permute-start(f32[16,3072]{1,0:T(8,128)S(1)} %get-tuple-element.40.high), channel_id=1, source_target_pairs={{0,16},{16,32},{32,48},{48,64},{64,80},{80,96},{96,112},{112,128},... | collective-permute-start | bytes 589832 | tf_op jit(solution)/shard_map/ppermute | solution.py:658
  19.4 1.3 %collective-permute-start.3 = (f32[16,3072]{1,0:T(8,128)S(1)}, f32[16,3072]{1,0:T(8,128)S(1)}, u32[]{:S(2)}, u32[]{:S(2)}) collective-permute-start(f32[16,3072]{1,0:T(8,128)S(1)} %get-tuple-element.39.low), channel_id=1, source_target_pairs={{16,0},{32,16},{48,32},{64,48},{80,64},{96,80},{112,96},{128,112},... | collective-permute-start | bytes 589832 | tf_op jit(solution)/shard_map/ppermute | solution.py:658
  20.7 0.0 copy-done.6
  20.7 0.0 copy-done.7
  20.7 0.0 copy-done.11
  20.7 0.0 copy-done.8
  20.7 0.0 copy-done.9
  20.7 0.0 copy-done.10
  20.8 0.2 shard_map.146
  21.0 2.4 %shard_map.143.second = f32[256,768]{1,0:T(8,128)S(1)} custom-call(f32[256,768]{1,0:T(8,128)S(1)} %get-tuple-element.35.state, f32[3,256,128]{2,1,0:T(8,128)S(1)} %bitcast.19, f32[3,256,256]{2,1,0:T(8,128)S(1)} %get-tuple-element.36.halo_geom, bf16[1216,256]{1,0:T(8,128)(2,1)S(1)} %copy-done.2), custom_call_target="tpu_custom_call" | custom-call | flops 1811939328 | bytes 2000000 | tf_op jit(solution)/shard_map/pallas_call | solution.py:615
  23.4 0.0 collective-permute-done.2.got_low
  23.4 3.0 %collective-permute-done.3.got_high = f32[16,3072]{1,0:T(8,128)S(1)} collective-permute-done((f32[16,3072]{1,0:T(8,128)S(1)}, f32[16,3072]{1,0:T(8,128)S(1)}, u32[]{:S(2)}, u32[]{:S(2)}) %collective-permute-start.3) | collective-permute-done | bytes 196640 | tf_op jit(solution)/shard_map/ppermute | solution.py:658
  26.4 5.2 %shard_map.144 = (f32[256,768]{1,0:T(8,128)S(1)}, f32[256,384]{1,0:T(8,128)S(1)}, f32[16,1536]{1,0:T(8,128)S(1)}, f32[16,1536]{1,0:T(8,128)S(1)}) custom-call(f32[256,768]{1,0:T(8,128)S(1)} %get-tuple-element.35.state, f32[256,768]{1,0:T(8,128)S(1)} %shard_map.143.second, f32[256,384]{1,0:T(8,128)S(1)} %get-tuple-element.37.lumped, ...), custom_call_target="tpu_custom_call" | custom-call | flops 2415919104 | bytes 2000000 | tf_op jit(solution)/shard_map/pallas_call | solution.py:615
  31.6 6.0 %collective-permute-start.4 = (f32[16,1536]{1,0:T(8,128)S(1)}, f32[16,1536]{1,0:T(8,128)S(1)}, u32[]{:S(2)}, u32[]{:S(2)}) collective-permute-start(f32[16,1536]{1,0:T(8,128)S(1)} %get-tuple-element.44.own_high), channel_id=1, source_target_pairs={{0,16},{16,32},{32,48},{48,64},{64,80},{80,96},{96,112},{112,128},... | collective-permute-start | bytes 294920 | tf_op jit(solution)/shard_map/ppermute | solution.py:658
  37.6 1.5 %collective-permute-start.5 = (f32[16,1536]{1,0:T(8,128)S(1)}, f32[16,1536]{1,0:T(8,128)S(1)}, u32[]{:S(2)}, u32[]{:S(2)}) collective-permute-start(f32[16,1536]{1,0:T(8,128)S(1)} %get-tuple-element.43.own_low), channel_id=1, source_target_pairs={{16,0},{32,16},{48,32},{64,48},{80,64},{96,80},{112,96},{128,112},... | collective-permute-start | bytes 294920 | tf_op jit(solution)/shard_map/ppermute | solution.py:658
  39.1 2.4 %shard_map.145.second = f32[256,768]{1,0:T(8,128)S(1)} custom-call(f32[256,768]{1,0:T(8,128)S(1)} %get-tuple-element.41.state, f32[3,256,128]{2,1,0:T(8,128)S(1)} %bitcast.21, f32[3,256,256]{2,1,0:T(8,128)S(1)} %get-tuple-element.36.halo_geom, bf16[1216,256]{1,0:T(8,128)(2,1)S(1)} %copy-done.2), custom_call_target="tpu_custom_call" | custom-call | flops 1811939328 | bytes 2000000 | tf_op jit(solution)/shard_map/pallas_call | solution.py:615
  41.5 0.0 collective-permute-done.4.new_low
  41.5 3.3 %collective-permute-done.5.new_high = f32[16,1536]{1,0:T(8,128)S(1)} collective-permute-done((f32[16,1536]{1,0:T(8,128)S(1)}, f32[16,1536]{1,0:T(8,128)S(1)}, u32[]{:S(2)}, u32[]{:S(2)}) %collective-permute-start.5) | collective-permute-done | bytes 98336 | tf_op jit(solution)/shard_map/ppermute | solution.py:658
  44.8 2.7 %shard_map.147 = (f32[4,256,128]{2,1,0:T(8,128)}, f32[32,32,128]{2,1,0:T(8,128)}, f32[64,512]{1,0:T(8,128)S(1)}) custom-call(f32[256,768]{1,0:T(8,128)S(1)} %get-tuple-element.41.state, f32[256,768]{1,0:T(8,128)S(1)} %shard_map.145.second, f32[256,384]{1,0:T(8,128)S(1)} %get-tuple-element.42.inverse, f32[256,384]{1,0:T(8,128)S(1)} %get-tuple-element.38.ends, ...), custom_call_target="tpu_custom_call" | custom-call | flops 603979776 | bytes 2000000 | tf_op jit(solution)/shard_map/pallas_call | solution.py:615
  47.6 10.5 %all-to-all-start.1 = ((f32[32,32,128]{2,1,0:T(8,128)}), f32[32,32,128]{2,1,0:T(8,128)S(1)}, u32[]{:S(2)}, u32[]{:S(2)}) async-start(f32[32,32,128]{2,1,0:T(8,128)} %get-tuple-element.50), calls=%async_computation.1 | async-start | bytes 1048576 | tf_op jit(solution)/shard_map/all_to_all | solution.py:735
  58.0 0.7 dynamic-slice_bitcast_fusion.phase
  58.7 12.1 %all-to-all-done.1.pieces = f32[32,32,128]{2,1,0:T(8,128)S(1)} async-done(((f32[32,32,128]{2,1,0:T(8,128)}), f32[32,32,128]{2,1,0:T(8,128)S(1)}, u32[]{:S(2)}, u32[]{:S(2)}) %all-to-all-start.1) | async-done | bytes 524320 | tf_op jit(solution)/shard_map/all_to_all | solution.py:735
  70.8 0.8 shard_map.148
  72.2 0.0 copy-start
  72.2 0.0 copy-start.1
  72.2 24.6 %all-gather = f32[1024,128]{1,0:T(8,128)S(1)} all-gather(f32[64,128]{1,0:T(8,128)S(1)} %get-tuple-element.54), channel_id=2, replica_groups=mesh['axial'=32,'girth'=16] {'girth'}, dimensions={0}, use_global_device_ids=true | all-gather | bytes 557056 | tf_op jit(solution)/shard_map/all_gather | solution.py:760
  96.9 0.0 copy-done
  96.9 0.0 copy-done.1
  96.9 1.2 %shard_map.149 = f32[2,16,4,128]{3,2,1,0:T(4,128)} custom-call(f32[16,64,128]{2,1,0:T(8,128)S(1)} %bitcast.12, f32[2,128]{1,0:T(2,128)S(1)} %dynamic-slice_bitcast_fusion.phase, bf16[2048,256]{1,0:T(8,128)(2,1)S(1)} %copy-done, bf16[2048,256]{1,0:T(8,128)(2,1)S(1)} %copy-done.1), custom_call_target="tpu_custom_call" | custom-call | flops 603979776 | bytes 2000000 | tf_op jit(solution)/shard_map/pallas_call | solution.py:615
  (3 shorter events, 0.0 us)
Async XLA Ops:
  0.6 9.3 %copy-start.2 = (bf16[1216,256]{1,0:T(8,128)(2,1)S(1)}, bf16[1216,256]{1,0:T(8,128)(2,1)}, u32[]{:S(2)}) copy-start(bf16[1216,256]{1,0:T(8,128)(2,1)} %constant.23.clone.table.tables.refs_0_) | copy-start | bytes 1867780
  0.6 9.3 %copy-start.4 = (f32[3,16,16,128]{3,2,1,0:T(8,128)S(1)}, f32[3,16,16,128]{3,2,1,0:T(8,128)}, u32[]{:S(2)}) copy-start(f32[3,16,16,128]{3,2,1,0:T(8,128)} %param.16) | copy-start | bytes 1179652
  3.1 9.4 %collective-permute-start = (f32[2,256,128]{2,1,0:T(8,128)}, f32[2,256,128]{2,1,0:T(8,128)S(1)}, u32[]{:S(2)}, u32[]{:S(2)}) collective-permute-start(f32[2,256,128]{2,1,0:T(8,128)} %get-tuple-element.33), channel_id=1, source_target_pairs={{0,1},{1,2},{2,3},{3,4},{4,5},{5,6},{6,7},{7,8},{8,9},{9,10},{10,1... | collective-permute-start | bytes 786440 | tf_op jit(solution)/shard_map/ppermute | solution.py:653
  5.8 6.7 %collective-permute-start.1 = (f32[2,256,128]{2,1,0:T(8,128)}, f32[2,256,128]{2,1,0:T(8,128)S(1)}, u32[]{:S(2)}, u32[]{:S(2)}) collective-permute-start(f32[2,256,128]{2,1,0:T(8,128)} %get-tuple-element.34), channel_id=1, source_target_pairs={{1,0},{2,1},{3,2},{4,3},{5,4},{6,5},{7,6},{8,7},{9,8},{10,9},{11,1... | collective-permute-start | bytes 786440 | tf_op jit(solution)/shard_map/ppermute | solution.py:654
  10.0 1.0 %copy-start.3 = (f32[4,16,16,128]{3,2,1,0:T(8,128)S(1)}, f32[4,16,16,128]{3,2,1,0:T(8,128)}, u32[]{:S(2)}) copy-start(f32[4,16,16,128]{3,2,1,0:T(8,128)} %param.15) | copy-start | bytes 1572868
  11.0 1.4 %copy-start.5 = (f32[16,16,128]{2,1,0:T(8,128)S(1)}, f32[16,16,128]{2,1,0:T(8,128)}, u32[]{:S(2)}) copy-start(f32[16,16,128]{2,1,0:T(8,128)} %param.17) | copy-start | bytes 393220
  12.5 8.2 %copy-start.6 = (f32[2,8,64]{2,1,0:T(8,128)S(1)}, f32[2,8,64]{2,1,0:T(8,128)}, u32[]{:S(2)}) copy-start(f32[2,8,64]{2,1,0:T(8,128)} %cycle_weights.1) | copy-start | bytes 12292
  12.5 8.2 %copy-start.7 = (f32[8,128]{1,0:T(8,128)S(1)}, f32[8,128]{1,0:T(8,128)}, u32[]{:S(2)}) copy-start(f32[8,128]{1,0:T(8,128)} %az_weights.1) | copy-start | bytes 12292
  15.9 4.8 %copy-start.11 = (s32[64]{0:T(128)S(1)}, s32[64]{0:T(128)}, u32[]{:S(2)}) copy-start(s32[64]{0:T(128)} %cycle_id.1) | copy-start | bytes 772
  15.9 4.8 %copy-start.8 = (s32[64]{0:T(128)S(1)}, s32[64]{0:T(128)}, u32[]{:S(2)}) copy-start(s32[64]{0:T(128)} %cycle_radial.1) | copy-start | bytes 772
  15.9 4.8 %copy-start.9 = (s32[64]{0:T(128)S(1)}, s32[64]{0:T(128)}, u32[]{:S(2)}) copy-start(s32[64]{0:T(128)} %cycle_axial.1) | copy-start | bytes 772
  16.0 4.8 %copy-start.10 = (s32[128]{0:T(128)S(1)}, s32[128]{0:T(128)}, u32[]{:S(2)}) copy-start(s32[128]{0:T(128)} %az_elem.1) | copy-start | bytes 1540
  16.0 7.4 %collective-permute-start.2 = (f32[16,3072]{1,0:T(8,128)S(1)}, f32[16,3072]{1,0:T(8,128)S(1)}, u32[]{:S(2)}, u32[]{:S(2)}) collective-permute-start(f32[16,3072]{1,0:T(8,128)S(1)} %get-tuple-element.40.high), channel_id=1, source_target_pairs={{0,16},{16,32},{32,48},{48,64},{64,80},{80,96},{96,112},{112,128},... | collective-permute-start | bytes 589832 | tf_op jit(solution)/shard_map/ppermute | solution.py:658
  19.4 7.0 %collective-permute-start.3 = (f32[16,3072]{1,0:T(8,128)S(1)}, f32[16,3072]{1,0:T(8,128)S(1)}, u32[]{:S(2)}, u32[]{:S(2)}) collective-permute-start(f32[16,3072]{1,0:T(8,128)S(1)} %get-tuple-element.39.low), channel_id=1, source_target_pairs={{16,0},{32,16},{48,32},{64,48},{80,64},{96,80},{112,96},{128,112},... | collective-permute-start | bytes 589832 | tf_op jit(solution)/shard_map/ppermute | solution.py:658
  31.6 9.9 %collective-permute-start.4 = (f32[16,1536]{1,0:T(8,128)S(1)}, f32[16,1536]{1,0:T(8,128)S(1)}, u32[]{:S(2)}, u32[]{:S(2)}) collective-permute-start(f32[16,1536]{1,0:T(8,128)S(1)} %get-tuple-element.44.own_high), channel_id=1, source_target_pairs={{0,16},{16,32},{32,48},{48,64},{64,80},{80,96},{96,112},{112,128},... | collective-permute-start | bytes 294920 | tf_op jit(solution)/shard_map/ppermute | solution.py:658
  37.6 7.2 %collective-permute-start.5 = (f32[16,1536]{1,0:T(8,128)S(1)}, f32[16,1536]{1,0:T(8,128)S(1)}, u32[]{:S(2)}, u32[]{:S(2)}) collective-permute-start(f32[16,1536]{1,0:T(8,128)S(1)} %get-tuple-element.43.own_low), channel_id=1, source_target_pairs={{16,0},{32,16},{48,32},{64,48},{80,64},{96,80},{112,96},{128,112},... | collective-permute-start | bytes 294920 | tf_op jit(solution)/shard_map/ppermute | solution.py:658
  47.6 23.2 %all-to-all-start.1 = ((f32[32,32,128]{2,1,0:T(8,128)}), f32[32,32,128]{2,1,0:T(8,128)S(1)}, u32[]{:S(2)}, u32[]{:S(2)}) async-start(f32[32,32,128]{2,1,0:T(8,128)} %get-tuple-element.50), calls=%async_computation.1 | async-start | bytes 1048576 | tf_op jit(solution)/shard_map/all_to_all | solution.py:735
  72.2 24.7 %copy-start = (bf16[2048,256]{1,0:T(8,128)(2,1)S(1)}, bf16[2048,256]{1,0:T(8,128)(2,1)}, u32[]{:S(2)}) copy-start(bf16[2048,256]{1,0:T(8,128)(2,1)} %constant.25.clone.table_high) | copy-start | bytes 3145732
  72.2 24.7 %copy-start.1 = (bf16[2048,256]{1,0:T(8,128)(2,1)S(1)}, bf16[2048,256]{1,0:T(8,128)(2,1)}, u32[]{:S(2)}) copy-start(bf16[2048,256]{1,0:T(8,128)(2,1)} %constant.26.clone.table_low) | copy-start | bytes 3145732

commit v6 on v5

--- a/solution.py
+++ b/solution.py
@@ -243,7 +243,7 @@
     return jnp.where((node == 7) | (node == 8), pair, v)
 
 
-def sum_girth(own, left, right, owners):
+def sum_girth(own, left, right, owners=None):
     lane = lax.broadcasted_iota(jnp.int32, left.shape, 1)
     first = lane % P_SIZE == 0
     last = lane % P_SIZE == P_SIZE - 1
@@ -259,6 +259,8 @@
         p = jnp.where(lane == 0, pltpu.roll(left, (LANES - HALO * c - HALO + 1) % LANES, 1), p)
         p = jnp.where(lane == LANES - 1, pltpu.roll(right, (LANES - 1 - HALO * c) % LANES, 1), p)
         sums.append(x + p)
+    if owners is None:
+        return sums
     p = inner(left)
     q = inner(right)
     for c, x in enumerate(owners):
@@ -276,31 +278,27 @@
 
 
 def pack_kernel(field_in, geom_in, mass_in, to_right, to_left, field, geom, mass, sems):
-    copies = [
-        pltpu.make_async_copy(field_in, field, sems.at[0]),
-        pltpu.make_async_copy(geom_in, geom, sems.at[1]),
-        pltpu.make_async_copy(mass_in, mass, sems.at[2]),
-    ]
+    pairs = [(field_in.at[c], field.at[c]) for c in range(C)]
+    pairs += [(geom_in.at[k], geom.at[k]) for k in range(3)] + [(mass_in, mass)]
+    copies = [pltpu.make_async_copy(x, y, sems.at[k]) for k, (x, y) in enumerate(pairs)]
     for copy in copies:
         copy.start()
     lane = lax.broadcasted_iota(jnp.int32, (NODES, LANES), 1)
 
-    def pack(arrays, start):
-        out = None
-        for k, x in enumerate(arrays):
-            moved = pltpu.roll(x, (HALO * k - start) % LANES, 1) if (HALO * k - start) else x
-            out = moved if out is None else jnp.where(lane // HALO == k, moved, out)
-        return out
-
-    copies[0].wait()
-    fields = [field[c] for c in range(C)]
-    to_right[0] = pack(fields, LANES - HALO)
-    to_left[0] = pack(fields, 0)
-    copies[1].wait()
-    copies[2].wait()
-    others = [geom[k] for k in range(3)] + [mass[...]]
-    to_right[1] = pack(others, LANES - HALO)
-    to_left[1] = pack(others, 0)
+    def add(out, k, x, start):
+        shift = (HALO * k - start) % LANES
+        moved = pltpu.roll(x, shift, 1) if shift else x
+        return moved if out is None else jnp.where(lane // HALO == k, moved, out)
+
+    for group in range(2):
+        right = left = None
+        for k in range(4):
+            copies[4 * group + k].wait()
+            x = field[k] if group == 0 else (geom[k] if k < 3 else mass[...])
+            right = add(right, k, x, LANES - HALO)
+            left = add(left, k, x, 0)
+        to_right[group] = right
+        to_left[group] = left
 
 
 def own_kernel(field, geom, table, out):
@@ -425,7 +423,7 @@
     return ref[:, STATIC + k * NARROW : STATIC + (k + 1) * NARROW]
 
 
-def finish_pair(state, second, inverse, ends, statics, own, got, tables):
+def finish_pair(state, second, inverse, ends, statics, own, got, tables, lanes=WIDE):
     low, high, got_low, got_high = statics
     own_low, own_high = own
     new_low, new_high = got
@@ -450,9 +448,14 @@
     node = lax.broadcasted_iota(jnp.int32, (16, 16, WIDE), 1)
     along = jnp.where(node < P_SIZE, w_low[:, None, :], w_high[:, None, :])
     change = wide(ends) * along.reshape(NODES, WIDE) + at_faces(face[:16], face[16:32], WIDE)
-    change = sum_nodes(shared_local([lanes_of(change, k) for k in range(6)]))
-    total = second + change.reshape(NODES, WIDE) + at_faces(beyond_low, beyond_high, WIDE)
-    return state + at_faces(w_low, w_high, WIDE) - total * wide(inverse)
+    parts = [lanes_of(change, k) for k in range(6)]
+    owners = parts[:4] if lanes == WIDE else None
+    summed = sum_girth(parts[:4], parts[4], parts[5], owners)
+    change = sum_nodes(jnp.concatenate(summed, axis=1)).reshape(NODES, lanes)
+    beyond = at_faces(beyond_low[:, :lanes], beyond_high[:, :lanes], lanes)
+    total = second[:, :lanes] + change + beyond
+    moved = state[:, :lanes] + at_faces(w_low[:, :lanes], w_high[:, :lanes], lanes)
+    return moved - total * wide(inverse)[:, :lanes]
 
 
 def middle_kernel(state, second, lumped, ends, low, high, got_low, got_high, geom, halo_geom, *refs):
@@ -500,12 +503,12 @@
         (own_low, own_high),
         (new_low, new_high),
         tables,
-    )
-    u = u[:, : C * LANES]
+        C * LANES,
+    )
     for c in range(C):
         out[c] = lanes_of(u, c)
     slab_high, slab_low = split(slab[...])
-    values = left_mul(jnp.concatenate([slab_high, slab_high, slab_low], axis=1), u)
+    values = left_pair(jnp.concatenate([slab_high, slab_low], axis=0), u)
     stacked = jnp.concatenate([lanes_of(values, c) for c in range(C)], axis=0)
     weight_high, weight_low = split(girth_weight[...])
     weights = jnp.concatenate([weight_high, weight_high, weight_low], axis=0)
@@ -599,7 +602,9 @@
         high, low = split(z)
         block = pl.ds(pair * 256, 256)
         th, tl = table_high[block, :], table_low[block, :]
-        part = dot(high, th) + dot(low, th) + dot(high, tl)
+        first = dot(jnp.concatenate([high, low], axis=0), th)
+        half = first.shape[0] // 2
+        part = first[:half] + first[half:] + dot(high, tl)
         total = part if total is None else total + part
     n = C * ROWS_DEV
     re = total[:n, :LANES] + total[n:, LANES:]
@@ -630,7 +635,7 @@
         in_specs=[hbm] * len(args),
         out_specs=[vmem] * 2,
         scratch_shapes=[pltpu.VMEM(x.shape, F32) for x in args]
-        + [pltpu.SemaphoreType.DMA((len(args),))],
+        + [pltpu.SemaphoreType.DMA((8,))],
         compiler_params=pltpu.CompilerParams(vmem_limit_bytes=LOAD_LIMIT),
     )(*args)
 

time: 98.5 us -> 98.7 us (level)
  no operation moved by 1% of the time
where the time goes in v6:
time: 98.7 us; the launch traced here: 98.3 us
  starting transfers between devices  29.5 us (30%)
  blocking collectives  24.6 us (25%)
  Pallas kernels  22.4 us (23%)
  waiting for transfers between devices  18.4 us (19%)
  local copies, waits for them, and re-layouts  1.8 us (2%)
  between operations  1.56 us (2%)
    all_gather x1, blocking collectives, body(): rows = lax.all_gather(rows, 'girth')  24.6 us
    pallas_call x8, Pallas kernels, call(): pl.pallas_call(kernel, out_shape=out_shape, in_specs=[vmem] * len(args),...  19 us
    ppermute x4, starting transfers between devices, exchange(): return (lax.ppermute(high, 'axial', up), lax.ppermute(low, 'axial', down))  12.1 us
    all_to_all x1, waiting for transfers between devices, body(): pieces = lax.all_to_all(packed, 'axial', 0, 0)  12.1 us
    all_to_all x1, starting transfers between devices, body(): pieces = lax.all_to_all(packed, 'axial', 0, 0)  10.4 us
    ppermute x4, waiting for transfers between devices, exchange(): return (lax.ppermute(high, 'axial', up), lax.ppermute(low, 'axial', down))  6.32 us
    ppermute x1, starting transfers between devices, body(): right = lax.ppermute(to_left, 'girth', back)  4.22 us
    pallas_call x1, Pallas kernels, pack_halos(): pl.pallas_call(pack_kernel, out_shape=[jax.ShapeDtypeStruct((2, NODES, LA...  2.71 us
  transfers between devices with their start and end apart: 7, of which 3 were waited for; matrix products, arithmetic and copies ran while one was open for 1% of the time, Pallas kernels for 7%

profile of v6, /device:TPU:1, one launch (start us, length us, event | category | flops | bytes accessed | tf_op | source)
XLA Modules:
  0.0 98.3 jit_solution(887759387478113724)
XLA Ops:
  0.6 0.0 copy-start.2
  0.6 0.0 copy-start.4
  0.7 2.7 %shard_map.140 = (f32[2,256,128]{2,1,0:T(8,128)}, f32[2,256,128]{2,1,0:T(8,128)}) custom-call(f32[4,256,128]{2,1,0:T(8,128)} %bitcast.13, f32[3,256,128]{2,1,0:T(8,128)} %bitcast.16, f32[256,128]{1,0:T(8,128)} %bitcast.22), custom_call_target="tpu_custom_call" | custom-call | tf_op jit(solution)/shard_map/pallas_call | solution.py:632
  3.4 2.7 %collective-permute-start = (f32[2,256,128]{2,1,0:T(8,128)}, f32[2,256,128]{2,1,0:T(8,128)S(1)}, u32[]{:S(2)}, u32[]{:S(2)}) collective-permute-start(f32[2,256,128]{2,1,0:T(8,128)} %get-tuple-element.33), channel_id=1, source_target_pairs={{0,1},{1,2},{2,3},{3,4},{4,5},{5,6},{6,7},{7,8},{8,9},{9,10},{10,1... | collective-permute-start | bytes 786440 | tf_op jit(solution)/shard_map/ppermute | solution.py:658
  6.1 4.2 %collective-permute-start.1 = (f32[2,256,128]{2,1,0:T(8,128)}, f32[2,256,128]{2,1,0:T(8,128)S(1)}, u32[]{:S(2)}, u32[]{:S(2)}) collective-permute-start(f32[2,256,128]{2,1,0:T(8,128)} %get-tuple-element.34), channel_id=1, source_target_pairs={{1,0},{2,1},{3,2},{4,3},{5,4},{6,5},{7,6},{8,7},{9,8},{10,9},{11,1... | collective-permute-start | bytes 786440 | tf_op jit(solution)/shard_map/ppermute | solution.py:659
  10.3 0.0 copy-done.2
  10.3 0.0 copy-done.4
  10.3 1.0 %copy-done.3 = f32[4,16,16,128]{3,2,1,0:T(8,128)S(1)} copy-done((f32[4,16,16,128]{3,2,1,0:T(8,128)S(1)}, f32[4,16,16,128]{3,2,1,0:T(8,128)}, u32[]{:S(2)}) %copy-start.3) | copy-done | bytes 524312
  11.3 1.4 %shard_map.141.own_total = f32[256,512]{1,0:T(8,128)S(1)} custom-call(f32[4,256,128]{2,1,0:T(8,128)S(1)} %bitcast.14, f32[3,256,128]{2,1,0:T(8,128)S(1)} %bitcast.17, bf16[1216,256]{1,0:T(8,128)(2,1)S(1)} %copy-done.2), custom_call_target="tpu_custom_call" | custom-call | flops 1207959552 | bytes 2000000 | tf_op jit(solution)/shard_map/pallas_call | solution.py:620
  12.8 0.0 collective-permute-done.left
  12.8 0.0 collective-permute-done.1.right
  12.8 0.0 copy-done.5
  12.8 0.0 copy-start.6
  12.8 0.0 copy-start.7
  12.8 3.4 %shard_map.142 = (f32[3,256,256]{2,1,0:T(8,128)S(1)}, f32[256,768]{1,0:T(8,128)S(1)}, f32[256,384]{1,0:T(8,128)S(1)}, f32[256,384]{1,0:T(8,128)S(1)}, f32[16,3072]{1,0:T(8,128)S(1)}, /*index=5*/f32[16,3072]{1,0:T(8,128)S(1)}) custom-call(f32[2,256,128]{2,1,0:T(8,128)S(1)} %collective-permute-done.left, f32[2,256,128]{2,1,0:T(8,128)S(1)} %collective-permute-done.1.right, ...), custom_call_target="tpu_custom_call" | custom-call | flops 1207959552 | bytes 2000000 | tf_op jit(solution)/shard_map/pallas_call | solution.py:620
  16.2 0.0 copy-start.11
  16.2 0.0 copy-start.8
  16.3 0.0 copy-start.9
  16.3 0.0 copy-start.10
  16.3 3.4 %collective-permute-start.2 = (f32[16,3072]{1,0:T(8,128)S(1)}, f32[16,3072]{1,0:T(8,128)S(1)}, u32[]{:S(2)}, u32[]{:S(2)}) collective-permute-start(f32[16,3072]{1,0:T(8,128)S(1)} %get-tuple-element.40.high), channel_id=1, source_target_pairs={{0,16},{16,32},{32,48},{48,64},{64,80},{80,96},{96,112},{112,128},... | collective-permute-start | bytes 589832 | tf_op jit(solution)/shard_map/ppermute | solution.py:663
  19.7 1.3 %collective-permute-start.3 = (f32[16,3072]{1,0:T(8,128)S(1)}, f32[16,3072]{1,0:T(8,128)S(1)}, u32[]{:S(2)}, u32[]{:S(2)}) collective-permute-start(f32[16,3072]{1,0:T(8,128)S(1)} %get-tuple-element.39.low), channel_id=1, source_target_pairs={{16,0},{32,16},{48,32},{64,48},{80,64},{96,80},{112,96},{128,112},... | collective-permute-start | bytes 589832 | tf_op jit(solution)/shard_map/ppermute | solution.py:663
  21.0 0.0 copy-done.6
  21.0 0.0 copy-done.7
  21.0 0.0 copy-done.11
  21.0 0.0 copy-done.8
  21.0 0.0 copy-done.9
  21.1 0.0 copy-done.10
  21.1 0.2 shard_map.146
  21.3 2.4 %shard_map.143.second = f32[256,768]{1,0:T(8,128)S(1)} custom-call(f32[256,768]{1,0:T(8,128)S(1)} %get-tuple-element.35.state, f32[3,256,128]{2,1,0:T(8,128)S(1)} %bitcast.19, f32[3,256,256]{2,1,0:T(8,128)S(1)} %get-tuple-element.36.halo_geom, bf16[1216,256]{1,0:T(8,128)(2,1)S(1)} %copy-done.2), custom_call_target="tpu_custom_call" | custom-call | flops 1811939328 | bytes 2000000 | tf_op jit(solution)/shard_map/pallas_call | solution.py:620
  23.7 0.0 collective-permute-done.2.got_low
  23.7 3.0 %collective-permute-done.3.got_high = f32[16,3072]{1,0:T(8,128)S(1)} collective-permute-done((f32[16,3072]{1,0:T(8,128)S(1)}, f32[16,3072]{1,0:T(8,128)S(1)}, u32[]{:S(2)}, u32[]{:S(2)}) %collective-permute-start.3) | collective-permute-done | bytes 196640 | tf_op jit(solution)/shard_map/ppermute | solution.py:663
  26.7 5.2 %shard_map.144 = (f32[256,768]{1,0:T(8,128)S(1)}, f32[256,384]{1,0:T(8,128)S(1)}, f32[16,1536]{1,0:T(8,128)S(1)}, f32[16,1536]{1,0:T(8,128)S(1)}) custom-call(f32[256,768]{1,0:T(8,128)S(1)} %get-tuple-element.35.state, f32[256,768]{1,0:T(8,128)S(1)} %shard_map.143.second, f32[256,384]{1,0:T(8,128)S(1)} %get-tuple-element.37.lumped, ...), custom_call_target="tpu_custom_call" | custom-call | flops 2415919104 | bytes 2000000 | tf_op jit(solution)/shard_map/pallas_call | solution.py:620
  31.9 6.0 %collective-permute-start.4 = (f32[16,1536]{1,0:T(8,128)S(1)}, f32[16,1536]{1,0:T(8,128)S(1)}, u32[]{:S(2)}, u32[]{:S(2)}) collective-permute-start(f32[16,1536]{1,0:T(8,128)S(1)} %get-tuple-element.44.own_high), channel_id=1, source_target_pairs={{0,16},{16,32},{32,48},{48,64},{64,80},{80,96},{96,112},{112,128},... | collective-permute-start | bytes 294920 | tf_op jit(solution)/shard_map/ppermute | solution.py:663
  37.9 1.5 %collective-permute-start.5 = (f32[16,1536]{1,0:T(8,128)S(1)}, f32[16,1536]{1,0:T(8,128)S(1)}, u32[]{:S(2)}, u32[]{:S(2)}) collective-permute-start(f32[16,1536]{1,0:T(8,128)S(1)} %get-tuple-element.43.own_low), channel_id=1, source_target_pairs={{16,0},{32,16},{48,32},{64,48},{80,64},{96,80},{112,96},{128,112},... | collective-permute-start | bytes 294920 | tf_op jit(solution)/shard_map/ppermute | solution.py:663
  39.4 2.4 %shard_map.145.second = f32[256,768]{1,0:T(8,128)S(1)} custom-call(f32[256,768]{1,0:T(8,128)S(1)} %get-tuple-element.41.state, f32[3,256,128]{2,1,0:T(8,128)S(1)} %bitcast.21, f32[3,256,256]{2,1,0:T(8,128)S(1)} %get-tuple-element.36.halo_geom, bf16[1216,256]{1,0:T(8,128)(2,1)S(1)} %copy-done.2), custom_call_target="tpu_custom_call" | custom-call | flops 1811939328 | bytes 2000000 | tf_op jit(solution)/shard_map/pallas_call | solution.py:620
  41.8 0.0 collective-permute-done.4.new_low
  41.8 3.3 %collective-permute-done.5.new_high = f32[16,1536]{1,0:T(8,128)S(1)} collective-permute-done((f32[16,1536]{1,0:T(8,128)S(1)}, f32[16,1536]{1,0:T(8,128)S(1)}, u32[]{:S(2)}, u32[]{:S(2)}) %collective-permute-start.5) | collective-permute-done | bytes 98336 | tf_op jit(solution)/shard_map/ppermute | solution.py:663
  45.1 2.6 %shard_map.147 = (f32[4,256,128]{2,1,0:T(8,128)}, f32[32,32,128]{2,1,0:T(8,128)}, f32[64,512]{1,0:T(8,128)S(1)}) custom-call(f32[256,768]{1,0:T(8,128)S(1)} %get-tuple-element.41.state, f32[256,768]{1,0:T(8,128)S(1)} %shard_map.145.second, f32[256,384]{1,0:T(8,128)S(1)} %get-tuple-element.42.inverse, f32[256,384]{1,0:T(8,128)S(1)} %get-tuple-element.38.ends, ...), custom_call_target="tpu_custom_call" | custom-call | flops 603979776 | bytes 2000000 | tf_op jit(solution)/shard_map/pallas_call | solution.py:620
  47.8 10.4 %all-to-all-start.1 = ((f32[32,32,128]{2,1,0:T(8,128)}), f32[32,32,128]{2,1,0:T(8,128)S(1)}, u32[]{:S(2)}, u32[]{:S(2)}) async-start(f32[32,32,128]{2,1,0:T(8,128)} %get-tuple-element.50), calls=%async_computation.1 | async-start | bytes 1048576 | tf_op jit(solution)/shard_map/all_to_all | solution.py:740
  58.2 0.7 dynamic-slice_bitcast_fusion.phase
  58.9 12.1 %all-to-all-done.1.pieces = f32[32,32,128]{2,1,0:T(8,128)S(1)} async-done(((f32[32,32,128]{2,1,0:T(8,128)}), f32[32,32,128]{2,1,0:T(8,128)S(1)}, u32[]{:S(2)}, u32[]{:S(2)}) %all-to-all-start.1) | async-done | bytes 524320 | tf_op jit(solution)/shard_map/all_to_all | solution.py:740
  71.0 0.8 shard_map.148
  72.4 0.0 copy-start
  72.4 0.0 copy-start.1
  72.4 24.6 %all-gather = f32[1024,128]{1,0:T(8,128)S(1)} all-gather(f32[64,128]{1,0:T(8,128)S(1)} %get-tuple-element.54), channel_id=2, replica_groups=mesh['axial'=32,'girth'=16] {'girth'}, dimensions={0}, use_global_device_ids=true | all-gather | bytes 557056 | tf_op jit(solution)/shard_map/all_gather | solution.py:765
  97.0 0.0 copy-done
  97.0 0.0 copy-done.1
  97.0 1.2 %shard_map.149 = f32[2,16,4,128]{3,2,1,0:T(4,128)} custom-call(f32[16,64,128]{2,1,0:T(8,128)S(1)} %bitcast.12, f32[2,128]{1,0:T(2,128)S(1)} %dynamic-slice_bitcast_fusion.phase, bf16[2048,256]{1,0:T(8,128)(2,1)S(1)} %copy-done, bf16[2048,256]{1,0:T(8,128)(2,1)S(1)} %copy-done.1), custom_call_target="tpu_custom_call" | custom-call | flops 603979776 | bytes 2000000 | tf_op jit(solution)/shard_map/pallas_call | solution.py:620
  (3 shorter events, 0.0 us)
Async XLA Ops:
  0.6 9.7 %copy-start.2 = (bf16[1216,256]{1,0:T(8,128)(2,1)S(1)}, bf16[1216,256]{1,0:T(8,128)(2,1)}, u32[]{:S(2)}) copy-start(bf16[1216,256]{1,0:T(8,128)(2,1)} %constant.23.clone.table.tables.refs_0_) | copy-start | bytes 1867780
  0.6 9.6 %copy-start.4 = (f32[3,16,16,128]{3,2,1,0:T(8,128)S(1)}, f32[3,16,16,128]{3,2,1,0:T(8,128)}, u32[]{:S(2)}) copy-start(f32[3,16,16,128]{3,2,1,0:T(8,128)} %param.16) | copy-start | bytes 1179652
  3.4 9.4 %collective-permute-start = (f32[2,256,128]{2,1,0:T(8,128)}, f32[2,256,128]{2,1,0:T(8,128)S(1)}, u32[]{:S(2)}, u32[]{:S(2)}) collective-permute-start(f32[2,256,128]{2,1,0:T(8,128)} %get-tuple-element.33), channel_id=1, source_target_pairs={{0,1},{1,2},{2,3},{3,4},{4,5},{5,6},{6,7},{7,8},{8,9},{9,10},{10,1... | collective-permute-start | bytes 786440 | tf_op jit(solution)/shard_map/ppermute | solution.py:658
  6.1 6.7 %collective-permute-start.1 = (f32[2,256,128]{2,1,0:T(8,128)}, f32[2,256,128]{2,1,0:T(8,128)S(1)}, u32[]{:S(2)}, u32[]{:S(2)}) collective-permute-start(f32[2,256,128]{2,1,0:T(8,128)} %get-tuple-element.34), channel_id=1, source_target_pairs={{1,0},{2,1},{3,2},{4,3},{5,4},{6,5},{7,6},{8,7},{9,8},{10,9},{11,1... | collective-permute-start | bytes 786440 | tf_op jit(solution)/shard_map/ppermute | solution.py:659
  10.3 1.0 %copy-start.3 = (f32[4,16,16,128]{3,2,1,0:T(8,128)S(1)}, f32[4,16,16,128]{3,2,1,0:T(8,128)}, u32[]{:S(2)}) copy-start(f32[4,16,16,128]{3,2,1,0:T(8,128)} %param.15) | copy-start | bytes 1572868
  11.3 1.4 %copy-start.5 = (f32[16,16,128]{2,1,0:T(8,128)S(1)}, f32[16,16,128]{2,1,0:T(8,128)}, u32[]{:S(2)}) copy-start(f32[16,16,128]{2,1,0:T(8,128)} %param.17) | copy-start | bytes 393220
  12.8 8.2 %copy-start.6 = (f32[2,8,64]{2,1,0:T(8,128)S(1)}, f32[2,8,64]{2,1,0:T(8,128)}, u32[]{:S(2)}) copy-start(f32[2,8,64]{2,1,0:T(8,128)} %cycle_weights.1) | copy-start | bytes 12292
  12.8 8.2 %copy-start.7 = (f32[8,128]{1,0:T(8,128)S(1)}, f32[8,128]{1,0:T(8,128)}, u32[]{:S(2)}) copy-start(f32[8,128]{1,0:T(8,128)} %az_weights.1) | copy-start | bytes 12292
  16.2 4.8 %copy-start.11 = (s32[64]{0:T(128)S(1)}, s32[64]{0:T(128)}, u32[]{:S(2)}) copy-start(s32[64]{0:T(128)} %cycle_id.1) | copy-start | bytes 772
  16.2 4.8 %copy-start.8 = (s32[64]{0:T(128)S(1)}, s32[64]{0:T(128)}, u32[]{:S(2)}) copy-start(s32[64]{0:T(128)} %cycle_radial.1) | copy-start | bytes 772
  16.3 4.8 %copy-start.9 = (s32[64]{0:T(128)S(1)}, s32[64]{0:T(128)}, u32[]{:S(2)}) copy-start(s32[64]{0:T(128)} %cycle_axial.1) | copy-start | bytes 772
  16.3 4.8 %copy-start.10 = (s32[128]{0:T(128)S(1)}, s32[128]{0:T(128)}, u32[]{:S(2)}) copy-start(s32[128]{0:T(128)} %az_elem.1) | copy-start | bytes 1540
  16.3 7.4 %collective-permute-start.2 = (f32[16,3072]{1,0:T(8,128)S(1)}, f32[16,3072]{1,0:T(8,128)S(1)}, u32[]{:S(2)}, u32[]{:S(2)}) collective-permute-start(f32[16,3072]{1,0:T(8,128)S(1)} %get-tuple-element.40.high), channel_id=1, source_target_pairs={{0,16},{16,32},{32,48},{48,64},{64,80},{80,96},{96,112},{112,128},... | collective-permute-start | bytes 589832 | tf_op jit(solution)/shard_map/ppermute | solution.py:663
  19.7 7.0 %collective-permute-start.3 = (f32[16,3072]{1,0:T(8,128)S(1)}, f32[16,3072]{1,0:T(8,128)S(1)}, u32[]{:S(2)}, u32[]{:S(2)}) collective-permute-start(f32[16,3072]{1,0:T(8,128)S(1)} %get-tuple-element.39.low), channel_id=1, source_target_pairs={{16,0},{32,16},{48,32},{64,48},{80,64},{96,80},{112,96},{128,112},... | collective-permute-start | bytes 589832 | tf_op jit(solution)/shard_map/ppermute | solution.py:663
  31.9 9.9 %collective-permute-start.4 = (f32[16,1536]{1,0:T(8,128)S(1)}, f32[16,1536]{1,0:T(8,128)S(1)}, u32[]{:S(2)}, u32[]{:S(2)}) collective-permute-start(f32[16,1536]{1,0:T(8,128)S(1)} %get-tuple-element.44.own_high), channel_id=1, source_target_pairs={{0,16},{16,32},{32,48},{48,64},{64,80},{80,96},{96,112},{112,128},... | collective-permute-start | bytes 294920 | tf_op jit(solution)/shard_map/ppermute | solution.py:663
  37.9 7.2 %collective-permute-start.5 = (f32[16,1536]{1,0:T(8,128)S(1)}, f32[16,1536]{1,0:T(8,128)S(1)}, u32[]{:S(2)}, u32[]{:S(2)}) collective-permute-start(f32[16,1536]{1,0:T(8,128)S(1)} %get-tuple-element.43.own_low), channel_id=1, source_target_pairs={{16,0},{32,16},{48,32},{64,48},{80,64},{96,80},{112,96},{128,112},... | collective-permute-start | bytes 294920 | tf_op jit(solution)/shard_map/ppermute | solution.py:663
  47.8 23.2 %all-to-all-start.1 = ((f32[32,32,128]{2,1,0:T(8,128)}), f32[32,32,128]{2,1,0:T(8,128)S(1)}, u32[]{:S(2)}, u32[]{:S(2)}) async-start(f32[32,32,128]{2,1,0:T(8,128)} %get-tuple-element.50), calls=%async_computation.1 | async-start | bytes 1048576 | tf_op jit(solution)/shard_map/all_to_all | solution.py:740
  72.4 24.6 %copy-start = (bf16[2048,256]{1,0:T(8,128)(2,1)S(1)}, bf16[2048,256]{1,0:T(8,128)(2,1)}, u32[]{:S(2)}) copy-start(bf16[2048,256]{1,0:T(8,128)(2,1)} %constant.25.clone.table_high) | copy-start | bytes 3145732
  72.4 24.6 %copy-start.1 = (bf16[2048,256]{1,0:T(8,128)(2,1)S(1)}, bf16[2048,256]{1,0:T(8,128)(2,1)}, u32[]{:S(2)}) copy-start(bf16[2048,256]{1,0:T(8,128)(2,1)} %constant.26.clone.table_low) | copy-start | bytes 3145732

commit v7 on v5

--- a/solution.py
+++ b/solution.py
@@ -243,7 +243,7 @@
     return jnp.where((node == 7) | (node == 8), pair, v)
 
 
-def sum_girth(own, left, right, owners):
+def sum_girth(own, left, right, owners=None):
     lane = lax.broadcasted_iota(jnp.int32, left.shape, 1)
     first = lane % P_SIZE == 0
     last = lane % P_SIZE == P_SIZE - 1
@@ -259,6 +259,8 @@
         p = jnp.where(lane == 0, pltpu.roll(left, (LANES - HALO * c - HALO + 1) % LANES, 1), p)
         p = jnp.where(lane == LANES - 1, pltpu.roll(right, (LANES - 1 - HALO * c) % LANES, 1), p)
         sums.append(x + p)
+    if owners is None:
+        return sums
     p = inner(left)
     q = inner(right)
     for c, x in enumerate(owners):
@@ -386,16 +388,41 @@
 NARROW = 3 * LANES
 
 
+def spread(x, k):
+    lane = lax.broadcasted_iota(jnp.int32, x.shape, 1)
+    y = jnp.where(lane // HALO == k, x, 0.0)
+    y = y + pltpu.roll(y, HALO, 1)
+    return y + pltpu.roll(y, 2 * HALO, 1)
+
+
+def to_send(face, out):
+    out[:, :STATIC] = face[:, :STATIC]
+    lane = lax.broadcasted_iota(jnp.int32, (16, LANES), 1) // HALO
+    for k in range(4):
+        out[:, STATIC + k * LANES : STATIC + (k + 1) * LANES] = static_part(face, k)[:, :LANES]
+    for k in range(2):
+        parts = []
+        for j in (2 * k, 2 * k + 1):
+            parts += [static_part(face, j)[:, LANES : 2 * LANES], static_part(face, j)[:, 2 * LANES :]]
+        block = parts[3]
+        for j in range(3):
+            block = jnp.where(lane == j, parts[j], block)
+        out[:, STATIC + (4 + k) * LANES : STATIC + (5 + k) * LANES] = block
+
+
+def as_sent(got):
+    pieces = [got[:, :STATIC]]
+    for k in range(4):
+        halos = got[:, STATIC + (4 + k // 2) * LANES : STATIC + (5 + k // 2) * LANES]
+        place = 2 * (k % 2)
+        pieces.append(got[:, STATIC + k * LANES : STATIC + (k + 1) * LANES])
+        pieces += [spread(halos, place), spread(halos, place + 1)]
+    return jnp.concatenate(pieces, axis=1)
+
+
 def halo_kernel(
-    left, right, own_total, field, mass, geom, tables, halo_geom, state, mass_out, ends_out, low, high
+    left, right, own_total, field, mass, geom, tables, halo_geom, state, mass_out, ends_out, low, high, *sent
 ):
-    lane = lax.broadcasted_iota(jnp.int32, (NODES, LANES), 1)
-
-    def spread(x, k):
-        y = jnp.where(lane // HALO == k, x, 0.0)
-        y = y + pltpu.roll(y, HALO, 1)
-        return y + pltpu.roll(y, 2 * HALO, 1)
-
     left_others, right_others = left[1], right[1]
     geoms = []
     for k in range(3):
@@ -419,13 +446,15 @@
         put_faces(x, low, high, STATIC + k * NARROW)
     start = jnp.concatenate([field[c] for c in range(C)] + [u], axis=1)
     two_steps(start, geom, halo_geom, 1.0 / lumped, first, (low, high), tables, state, low, high)
+    to_send(low, sent[0])
+    to_send(high, sent[1])
 
 
 def static_part(ref, k):
     return ref[:, STATIC + k * NARROW : STATIC + (k + 1) * NARROW]
 
 
-def finish_pair(state, second, inverse, ends, statics, own, got, tables):
+def finish_pair(state, second, inverse, ends, statics, own, got, tables, lanes=WIDE):
     low, high, got_low, got_high = statics
     own_low, own_high = own
     new_low, new_high = got
@@ -450,13 +479,19 @@
     node = lax.broadcasted_iota(jnp.int32, (16, 16, WIDE), 1)
     along = jnp.where(node < P_SIZE, w_low[:, None, :], w_high[:, None, :])
     change = wide(ends) * along.reshape(NODES, WIDE) + at_faces(face[:16], face[16:32], WIDE)
-    change = sum_nodes(shared_local([lanes_of(change, k) for k in range(6)]))
-    total = second + change.reshape(NODES, WIDE) + at_faces(beyond_low, beyond_high, WIDE)
-    return state + at_faces(w_low, w_high, WIDE) - total * wide(inverse)
+    parts = [lanes_of(change, k) for k in range(6)]
+    owners = parts[:4] if lanes == WIDE else None
+    summed = sum_girth(parts[:4], parts[4], parts[5], owners)
+    change = sum_nodes(jnp.concatenate(summed, axis=1)).reshape(NODES, lanes)
+    beyond = at_faces(beyond_low[:, :lanes], beyond_high[:, :lanes], lanes)
+    total = second[:, :lanes] + change + beyond
+    moved = state[:, :lanes] + at_faces(w_low[:, :lanes], w_high[:, :lanes], lanes)
+    return moved - total * wide(inverse)[:, :lanes]
 
 
 def middle_kernel(state, second, lumped, ends, low, high, got_low, got_high, geom, halo_geom, *refs):
     tables, state_out, inverse_out, next_low, next_high = refs
+    got_low, got_high = as_sent(got_low), as_sent(got_high)
     inverse = 1.0 / (
         lumped[...] + at_faces(static_part(got_low, 0), static_part(got_high, 0), NARROW)
     )
@@ -496,16 +531,16 @@
         second[...],
         inverse[...],
         ends[...],
-        (low, high, got_low, got_high),
+        (low, high, as_sent(got_low), as_sent(got_high)),
         (own_low, own_high),
         (new_low, new_high),
         tables,
-    )
-    u = u[:, : C * LANES]
+        C * LANES,
+    )
     for c in range(C):
         out[c] = lanes_of(u, c)
     slab_high, slab_low = split(slab[...])
-    values = left_mul(jnp.concatenate([slab_high, slab_high, slab_low], axis=1), u)
+    values = left_pair(jnp.concatenate([slab_high, slab_low], axis=0), u)
     stacked = jnp.concatenate([lanes_of(values, c) for c in range(C)], axis=0)
     weight_high, weight_low = split(girth_weight[...])
     weights = jnp.concatenate([weight_high, weight_high, weight_low], axis=0)
@@ -599,7 +634,9 @@
         high, low = split(z)
         block = pl.ds(pair * 256, 256)
         th, tl = table_high[block, :], table_low[block, :]
-        part = dot(high, th) + dot(low, th) + dot(high, tl)
+        first = dot(jnp.concatenate([high, low], axis=0), th)
+        half = first.shape[0] // 2
+        part = first[:half] + first[half:] + dot(high, tl)
         total = part if total is None else total + part
     n = C * ROWS_DEV
     re = total[:n, :LANES] + total[n:, LANES:]
@@ -658,10 +695,10 @@
         return lax.ppermute(high, "axial", up), lax.ppermute(low, "axial", down)
 
     whole, narrow = (NODES, WIDE), (NODES, NARROW)
-    face_static = (16, STATIC + 4 * NARROW)
-    halo_geom, state, lumped, ends, low, high = call(
+    face_static, sent = (16, STATIC + 4 * NARROW), (16, STATIC + 6 * LANES)
+    halo_geom, state, lumped, ends, low, high, send_low, send_high = call(
         halo_kernel,
-        [(3, NODES, 2 * LANES), whole, narrow, narrow, face_static, face_static],
+        [(3, NODES, 2 * LANES), whole, narrow, narrow, face_static, face_static, sent, sent],
         2 * tile_flops,
         left,
         right,
@@ -671,7 +708,7 @@
         geom,
         table,
     )
-    got_low, got_high = exchange(low, high)
+    got_low, got_high = exchange(send_low, send_high)
     (second,) = call(second_kernel, [whole], 3 * tile_flops, state, geom, halo_geom, table)
     state, inverse, own_low, own_high = call(
         middle_kernel,

time: 98.5 us -> 97.4 us (0.989)
  no operation moved by 1% of the time
where the time goes in v7:
time: 97.4 us; the launch traced here: 97 us
  starting transfers between devices  28.6 us (29%)
  blocking collectives  24.6 us (25%)
  Pallas kernels  22.3 us (23%)
  waiting for transfers between devices  18.2 us (19%)
  local copies, waits for them, and re-layouts  1.8 us (2%)
  between operations  1.54 us (2%)
    all_gather x1, blocking collectives, body(): rows = lax.all_gather(rows, 'girth')  24.6 us
    pallas_call x8, Pallas kernels, call(): pl.pallas_call(kernel, out_shape=out_shape, in_specs=[vmem] * len(args),...  19.2 us
    all_to_all x1, waiting for transfers between devices, body(): pieces = lax.all_to_all(packed, 'axial', 0, 0)  12.1 us
    ppermute x4, starting transfers between devices, exchange(): return (lax.ppermute(high, 'axial', up), lax.ppermute(low, 'axial', down))  11.2 us
    all_to_all x1, starting transfers between devices, body(): pieces = lax.all_to_all(packed, 'axial', 0, 0)  10.5 us
    ppermute x4, waiting for transfers between devices, exchange(): return (lax.ppermute(high, 'axial', up), lax.ppermute(low, 'axial', down))  6.1 us
    ppermute x1, starting transfers between devices, body(): right = lax.ppermute(to_left, 'girth', back)  4.22 us
    ppermute x1, starting transfers between devices, body(): left = lax.ppermute(to_right, 'girth', around)  2.7 us
  transfers between devices with their start and end apart: 7, of which 3 were waited for; matrix products, arithmetic and copies ran while one was open for 1% of the time, Pallas kernels for 7%

profile of v7, /device:TPU:1, one launch (start us, length us, event | category | flops | bytes accessed | tf_op | source)
XLA Modules:
  0.0 97.0 jit_solution(11296348386037174967)
XLA Ops:
  0.6 0.0 copy-start.2
  0.6 0.0 copy-start.6
  0.7 0.0 copy-start.7
  0.7 0.0 copy-start.4
  0.7 2.4 %shard_map.140 = (f32[2,256,128]{2,1,0:T(8,128)}, f32[2,256,128]{2,1,0:T(8,128)}) custom-call(f32[4,256,128]{2,1,0:T(8,128)} %bitcast.13, f32[3,256,128]{2,1,0:T(8,128)} %bitcast.16, f32[256,128]{1,0:T(8,128)} %bitcast.22), custom_call_target="tpu_custom_call" | custom-call | tf_op jit(solution)/shard_map/pallas_call | solution.py:664
  3.1 0.0 copy-start.11
  3.1 0.0 copy-start.8
  3.1 0.0 copy-start.9
  3.1 0.0 copy-start.10
  3.1 2.7 %collective-permute-start = (f32[2,256,128]{2,1,0:T(8,128)}, f32[2,256,128]{2,1,0:T(8,128)S(1)}, u32[]{:S(2)}, u32[]{:S(2)}) collective-permute-start(f32[2,256,128]{2,1,0:T(8,128)} %get-tuple-element.35), channel_id=1, source_target_pairs={{0,1},{1,2},{2,3},{3,4},{4,5},{5,6},{6,7},{7,8},{8,9},{9,10},{10,1... | collective-permute-start | bytes 786440 | tf_op jit(solution)/shard_map/ppermute | solution.py:690
  5.8 4.2 %collective-permute-start.1 = (f32[2,256,128]{2,1,0:T(8,128)}, f32[2,256,128]{2,1,0:T(8,128)S(1)}, u32[]{:S(2)}, u32[]{:S(2)}) collective-permute-start(f32[2,256,128]{2,1,0:T(8,128)} %get-tuple-element.36), channel_id=1, source_target_pairs={{1,0},{2,1},{3,2},{4,3},{5,4},{6,5},{7,6},{8,7},{9,8},{10,9},{11,1... | collective-permute-start | bytes 786440 | tf_op jit(solution)/shard_map/ppermute | solution.py:691
  10.0 0.0 copy-done.6
  10.0 0.0 copy-done.7
  10.0 0.0 copy-done.11
  10.0 0.0 copy-done.8
  10.0 0.0 copy-done.9
  10.1 0.0 copy-done.10
  10.1 0.2 shard_map.146
  10.3 0.0 copy-done.2
  10.3 0.0 copy-done.4
  10.3 0.0 copy-start.3
  10.3 1.0 %copy-done.3 = f32[4,16,16,128]{3,2,1,0:T(8,128)S(1)} copy-done((f32[4,16,16,128]{3,2,1,0:T(8,128)S(1)}, f32[4,16,16,128]{3,2,1,0:T(8,128)}, u32[]{:S(2)}) %copy-start.3) | copy-done | bytes 524312
  11.4 1.4 %shard_map.141.own_total = f32[256,512]{1,0:T(8,128)S(1)} custom-call(f32[4,256,128]{2,1,0:T(8,128)S(1)} %bitcast.14, f32[3,256,128]{2,1,0:T(8,128)S(1)} %bitcast.17, bf16[1216,256]{1,0:T(8,128)(2,1)S(1)} %copy-done.2), custom_call_target="tpu_custom_call" | custom-call | flops 1207959552 | bytes 2000000 | tf_op jit(solution)/shard_map/pallas_call | solution.py:652
  12.8 0.0 collective-permute-done.left
  12.8 0.0 collective-permute-done.1.right
  12.8 0.0 copy-done.5
  12.8 3.4 %shard_map.142 = (f32[3,256,256]{2,1,0:T(8,128)S(1)}, f32[256,768]{1,0:T(8,128)S(1)}, f32[256,384]{1,0:T(8,128)S(1)}, f32[256,384]{1,0:T(8,128)S(1)}, f32[16,307...) custom-call(f32[2,256,128]{2,1,0:T(8,128)S(1)} %collective-permute-done.left, ...), custom_call_target="tpu_custom_call" | custom-call | flops 1207959552 | bytes 2000000 | tf_op jit(solution)/shard_map/pallas_call | solution.py:652
  16.2 3.0 %collective-permute-start.2 = (f32[16,2304]{1,0:T(8,128)S(1)}, f32[16,2304]{1,0:T(8,128)S(1)}, u32[]{:S(2)}, u32[]{:S(2)}) collective-permute-start(f32[16,2304]{1,0:T(8,128)S(1)} %get-tuple-element.43), channel_id=1, source_target_pairs={{0,16},{16,32},{32,48},{48,64},{64,80},{80,96},{96,112},{112,128},... | collective-permute-start | bytes 442376 | tf_op jit(solution)/shard_map/ppermute | solution.py:695
  19.3 1.3 %collective-permute-start.3 = (f32[16,2304]{1,0:T(8,128)S(1)}, f32[16,2304]{1,0:T(8,128)S(1)}, u32[]{:S(2)}, u32[]{:S(2)}) collective-permute-start(f32[16,2304]{1,0:T(8,128)S(1)} %get-tuple-element.44), channel_id=1, source_target_pairs={{16,0},{32,16},{48,32},{64,48},{80,64},{96,80},{112,96},{128,112},... | collective-permute-start | bytes 442376 | tf_op jit(solution)/shard_map/ppermute | solution.py:695
  20.6 2.4 %shard_map.143.second = f32[256,768]{1,0:T(8,128)S(1)} custom-call(f32[256,768]{1,0:T(8,128)S(1)} %get-tuple-element.37.state, f32[3,256,128]{2,1,0:T(8,128)S(1)} %bitcast.19, f32[3,256,256]{2,1,0:T(8,128)S(1)} %get-tuple-element.38.halo_geom, bf16[1216,256]{1,0:T(8,128)(2,1)S(1)} %copy-done.2), custom_call_target="tpu_custom_call" | custom-call | flops 1811939328 | bytes 2000000 | tf_op jit(solution)/shard_map/pallas_call | solution.py:652
  23.0 0.0 collective-permute-done.2.got_low
  23.0 2.8 %collective-permute-done.3.got_high = f32[16,2304]{1,0:T(8,128)S(1)} collective-permute-done((f32[16,2304]{1,0:T(8,128)S(1)}, f32[16,2304]{1,0:T(8,128)S(1)}, u32[]{:S(2)}, u32[]{:S(2)}) %collective-permute-start.3) | collective-permute-done | bytes 147488 | tf_op jit(solution)/shard_map/ppermute | solution.py:695
  25.8 5.3 %shard_map.144 = (f32[256,768]{1,0:T(8,128)S(1)}, f32[256,384]{1,0:T(8,128)S(1)}, f32[16,1536]{1,0:T(8,128)S(1)}, f32[16,1536]{1,0:T(8,128)S(1)}) custom-call(f32[256,768]{1,0:T(8,128)S(1)} %get-tuple-element.37.state, f32[256,768]{1,0:T(8,128)S(1)} %shard_map.143.second, f32[256,384]{1,0:T(8,128)S(1)} %get-tuple-element.39.lumped, ...), custom_call_target="tpu_custom_call" | custom-call | flops 2415919104 | bytes 2000000 | tf_op jit(solution)/shard_map/pallas_call | solution.py:652
  31.1 5.5 %collective-permute-start.4 = (f32[16,1536]{1,0:T(8,128)S(1)}, f32[16,1536]{1,0:T(8,128)S(1)}, u32[]{:S(2)}, u32[]{:S(2)}) collective-permute-start(f32[16,1536]{1,0:T(8,128)S(1)} %get-tuple-element.48.own_high), channel_id=1, source_target_pairs={{0,16},{16,32},{32,48},{48,64},{64,80},{80,96},{96,112},{112,128},... | collective-permute-start | bytes 294920 | tf_op jit(solution)/shard_map/ppermute | solution.py:695
  36.6 1.5 %collective-permute-start.5 = (f32[16,1536]{1,0:T(8,128)S(1)}, f32[16,1536]{1,0:T(8,128)S(1)}, u32[]{:S(2)}, u32[]{:S(2)}) collective-permute-start(f32[16,1536]{1,0:T(8,128)S(1)} %get-tuple-element.47.own_low), channel_id=1, source_target_pairs={{16,0},{32,16},{48,32},{64,48},{80,64},{96,80},{112,96},{128,112},... | collective-permute-start | bytes 294920 | tf_op jit(solution)/shard_map/ppermute | solution.py:695
  38.1 2.4 %shard_map.145.second = f32[256,768]{1,0:T(8,128)S(1)} custom-call(f32[256,768]{1,0:T(8,128)S(1)} %get-tuple-element.45.state, f32[3,256,128]{2,1,0:T(8,128)S(1)} %bitcast.21, f32[3,256,256]{2,1,0:T(8,128)S(1)} %get-tuple-element.38.halo_geom, bf16[1216,256]{1,0:T(8,128)(2,1)S(1)} %copy-done.2), custom_call_target="tpu_custom_call" | custom-call | flops 1811939328 | bytes 2000000 | tf_op jit(solution)/shard_map/pallas_call | solution.py:652
  40.5 0.0 collective-permute-done.4.new_low
  40.5 3.3 %collective-permute-done.5.new_high = f32[16,1536]{1,0:T(8,128)S(1)} collective-permute-done((f32[16,1536]{1,0:T(8,128)S(1)}, f32[16,1536]{1,0:T(8,128)S(1)}, u32[]{:S(2)}, u32[]{:S(2)}) %collective-permute-start.5) | collective-permute-done | bytes 98336 | tf_op jit(solution)/shard_map/ppermute | solution.py:695
  43.8 2.7 %shard_map.147 = (f32[4,256,128]{2,1,0:T(8,128)}, f32[32,32,128]{2,1,0:T(8,128)}, f32[64,512]{1,0:T(8,128)S(1)}) custom-call(f32[256,768]{1,0:T(8,128)S(1)} %get-tuple-element.45.state, f32[256,768]{1,0:T(8,128)S(1)} %shard_map.145.second, f32[256,384]{1,0:T(8,128)S(1)} %get-tuple-element.46.inverse, f32[256,384]{1,0:T(8,128)S(1)} %get-tuple-element.40.ends, ...), custom_call_target="tpu_custom_call" | custom-call | flops 603979776 | bytes 2000000 | tf_op jit(solution)/shard_map/pallas_call | solution.py:652
  46.5 10.5 %all-to-all-start.1 = ((f32[32,32,128]{2,1,0:T(8,128)}), f32[32,32,128]{2,1,0:T(8,128)S(1)}, u32[]{:S(2)}, u32[]{:S(2)}) async-start(f32[32,32,128]{2,1,0:T(8,128)} %get-tuple-element.54), calls=%async_computation.1 | async-start | bytes 1048576 | tf_op jit(solution)/shard_map/all_to_all | solution.py:772
  57.0 0.7 dynamic-slice_bitcast_fusion.phase
  57.7 12.1 %all-to-all-done.1.pieces = f32[32,32,128]{2,1,0:T(8,128)S(1)} async-done(((f32[32,32,128]{2,1,0:T(8,128)}), f32[32,32,128]{2,1,0:T(8,128)S(1)}, u32[]{:S(2)}, u32[]{:S(2)}) %all-to-all-start.1) | async-done | bytes 524320 | tf_op jit(solution)/shard_map/all_to_all | solution.py:772
  69.8 0.8 shard_map.148
  71.2 0.0 copy-start
  71.2 0.0 copy-start.1
  71.2 24.6 %all-gather = f32[1024,128]{1,0:T(8,128)S(1)} all-gather(f32[64,128]{1,0:T(8,128)S(1)} %get-tuple-element.58), channel_id=2, replica_groups=mesh['axial'=32,'girth'=16] {'girth'}, dimensions={0}, use_global_device_ids=true | all-gather | bytes 557056 | tf_op jit(solution)/shard_map/all_gather | solution.py:797
  95.8 0.0 copy-done
  95.8 1.2 %shard_map.149 = f32[2,16,4,128]{3,2,1,0:T(4,128)} custom-call(f32[16,64,128]{2,1,0:T(8,128)S(1)} %bitcast.12, f32[2,128]{1,0:T(2,128)S(1)} %dynamic-slice_bitcast_fusion.phase, bf16[2048,256]{1,0:T(8,128)(2,1)S(1)} %copy-done, bf16[2048,256]{1,0:T(8,128)(2,1)S(1)} %copy-done.1), custom_call_target="tpu_custom_call" | custom-call | flops 603979776 | bytes 2000000 | tf_op jit(solution)/shard_map/pallas_call | solution.py:652
  (3 shorter events, 0.0 us)
Async XLA Ops:
  0.6 9.7 %copy-start.2 = (bf16[1216,256]{1,0:T(8,128)(2,1)S(1)}, bf16[1216,256]{1,0:T(8,128)(2,1)}, u32[]{:S(2)}) copy-start(bf16[1216,256]{1,0:T(8,128)(2,1)} %constant.23.clone.table.tables.refs_0_) | copy-start | bytes 1867780
  0.6 9.4 %copy-start.6 = (f32[2,8,64]{2,1,0:T(8,128)S(1)}, f32[2,8,64]{2,1,0:T(8,128)}, u32[]{:S(2)}) copy-start(f32[2,8,64]{2,1,0:T(8,128)} %cycle_weights.1) | copy-start | bytes 12292
  0.7 9.4 %copy-start.7 = (f32[8,128]{1,0:T(8,128)S(1)}, f32[8,128]{1,0:T(8,128)}, u32[]{:S(2)}) copy-start(f32[8,128]{1,0:T(8,128)} %az_weights.1) | copy-start | bytes 12292
  0.7 9.7 %copy-start.4 = (f32[3,16,16,128]{3,2,1,0:T(8,128)S(1)}, f32[3,16,16,128]{3,2,1,0:T(8,128)}, u32[]{:S(2)}) copy-start(f32[3,16,16,128]{3,2,1,0:T(8,128)} %param.16) | copy-start | bytes 1179652
  3.1 7.0 %copy-start.11 = (s32[64]{0:T(128)S(1)}, s32[64]{0:T(128)}, u32[]{:S(2)}) copy-start(s32[64]{0:T(128)} %cycle_id.1) | copy-start | bytes 772
  3.1 7.0 %copy-start.8 = (s32[64]{0:T(128)S(1)}, s32[64]{0:T(128)}, u32[]{:S(2)}) copy-start(s32[64]{0:T(128)} %cycle_radial.1) | copy-start | bytes 772
  3.1 7.0 %copy-start.9 = (s32[64]{0:T(128)S(1)}, s32[64]{0:T(128)}, u32[]{:S(2)}) copy-start(s32[64]{0:T(128)} %cycle_axial.1) | copy-start | bytes 772
  3.1 7.0 %copy-start.10 = (s32[128]{0:T(128)S(1)}, s32[128]{0:T(128)}, u32[]{:S(2)}) copy-start(s32[128]{0:T(128)} %az_elem.1) | copy-start | bytes 1540
  3.1 9.7 %collective-permute-start = (f32[2,256,128]{2,1,0:T(8,128)}, f32[2,256,128]{2,1,0:T(8,128)S(1)}, u32[]{:S(2)}, u32[]{:S(2)}) collective-permute-start(f32[2,256,128]{2,1,0:T(8,128)} %get-tuple-element.35), channel_id=1, source_target_pairs={{0,1},{1,2},{2,3},{3,4},{4,5},{5,6},{6,7},{7,8},{8,9},{9,10},{10,1... | collective-permute-start | bytes 786440 | tf_op jit(solution)/shard_map/ppermute | solution.py:690
  5.8 7.0 %collective-permute-start.1 = (f32[2,256,128]{2,1,0:T(8,128)}, f32[2,256,128]{2,1,0:T(8,128)S(1)}, u32[]{:S(2)}, u32[]{:S(2)}) collective-permute-start(f32[2,256,128]{2,1,0:T(8,128)} %get-tuple-element.36), channel_id=1, source_target_pairs={{1,0},{2,1},{3,2},{4,3},{5,4},{6,5},{7,6},{8,7},{9,8},{10,9},{11,1... | collective-permute-start | bytes 786440 | tf_op jit(solution)/shard_map/ppermute | solution.py:691
  10.3 1.1 %copy-start.3 = (f32[4,16,16,128]{3,2,1,0:T(8,128)S(1)}, f32[4,16,16,128]{3,2,1,0:T(8,128)}, u32[]{:S(2)}) copy-start(f32[4,16,16,128]{3,2,1,0:T(8,128)} %param.15) | copy-start | bytes 1572868
  11.4 1.4 %copy-start.5 = (f32[16,16,128]{2,1,0:T(8,128)S(1)}, f32[16,16,128]{2,1,0:T(8,128)}, u32[]{:S(2)}) copy-start(f32[16,16,128]{2,1,0:T(8,128)} %param.17) | copy-start | bytes 393220
  16.2 6.7 %collective-permute-start.2 = (f32[16,2304]{1,0:T(8,128)S(1)}, f32[16,2304]{1,0:T(8,128)S(1)}, u32[]{:S(2)}, u32[]{:S(2)}) collective-permute-start(f32[16,2304]{1,0:T(8,128)S(1)} %get-tuple-element.43), channel_id=1, source_target_pairs={{0,16},{16,32},{32,48},{48,64},{64,80},{80,96},{96,112},{112,128},... | collective-permute-start | bytes 442376 | tf_op jit(solution)/shard_map/ppermute | solution.py:695
  19.3 6.5 %collective-permute-start.3 = (f32[16,2304]{1,0:T(8,128)S(1)}, f32[16,2304]{1,0:T(8,128)S(1)}, u32[]{:S(2)}, u32[]{:S(2)}) collective-permute-start(f32[16,2304]{1,0:T(8,128)S(1)} %get-tuple-element.44), channel_id=1, source_target_pairs={{16,0},{32,16},{48,32},{64,48},{80,64},{96,80},{112,96},{128,112},... | collective-permute-start | bytes 442376 | tf_op jit(solution)/shard_map/ppermute | solution.py:695
  31.1 9.4 %collective-permute-start.4 = (f32[16,1536]{1,0:T(8,128)S(1)}, f32[16,1536]{1,0:T(8,128)S(1)}, u32[]{:S(2)}, u32[]{:S(2)}) collective-permute-start(f32[16,1536]{1,0:T(8,128)S(1)} %get-tuple-element.48.own_high), channel_id=1, source_target_pairs={{0,16},{16,32},{32,48},{48,64},{64,80},{80,96},{96,112},{112,128},... | collective-permute-start | bytes 294920 | tf_op jit(solution)/shard_map/ppermute | solution.py:695
  36.6 7.2 %collective-permute-start.5 = (f32[16,1536]{1,0:T(8,128)S(1)}, f32[16,1536]{1,0:T(8,128)S(1)}, u32[]{:S(2)}, u32[]{:S(2)}) collective-permute-start(f32[16,1536]{1,0:T(8,128)S(1)} %get-tuple-element.47.own_low), channel_id=1, source_target_pairs={{16,0},{32,16},{48,32},{64,48},{80,64},{96,80},{112,96},{128,112},... | collective-permute-start | bytes 294920 | tf_op jit(solution)/shard_map/ppermute | solution.py:695
  46.5 23.2 %all-to-all-start.1 = ((f32[32,32,128]{2,1,0:T(8,128)}), f32[32,32,128]{2,1,0:T(8,128)S(1)}, u32[]{:S(2)}, u32[]{:S(2)}) async-start(f32[32,32,128]{2,1,0:T(8,128)} %get-tuple-element.54), calls=%async_computation.1 | async-start | bytes 1048576 | tf_op jit(solution)/shard_map/all_to_all | solution.py:772
  71.2 24.6 %copy-start = (bf16[2048,256]{1,0:T(8,128)(2,1)S(1)}, bf16[2048,256]{1,0:T(8,128)(2,1)}, u32[]{:S(2)}) copy-start(bf16[2048,256]{1,0:T(8,128)(2,1)} %constant.25.clone.table_high) | copy-start | bytes 3145732
  71.2 24.6 %copy-start.1 = (bf16[2048,256]{1,0:T(8,128)(2,1)S(1)}, bf16[2048,256]{1,0:T(8,128)(2,1)}, u32[]{:S(2)}) copy-start(bf16[2048,256]{1,0:T(8,128)(2,1)} %constant.26.clone.table_low) | copy-start | bytes 3145732

commit v8 on v7

--- a/solution.py
+++ b/solution.py
@@ -192,6 +192,20 @@
     return jnp.broadcast_to(column[None], (16, 16, LANES)).reshape(rows, LANES)
 
 
+def axial_apply(x, matrix):
+    v = x.reshape(-1, P_SIZE, x.shape[1])
+    node = lax.broadcasted_iota(jnp.int32, (P_SIZE, x.shape[1]), 0)
+    out = None
+    for k in range(P_SIZE):
+        values = [float(matrix[i, (i - k) % P_SIZE]) for i in range(P_SIZE)]
+        factor = jnp.full(node.shape, values[0], F32)
+        for i in range(1, P_SIZE):
+            factor = jnp.where(node == i, values[i], factor)
+        term = factor[None] * (pltpu.roll(v, k, 1) if k else v)
+        out = term if out is None else out + term
+    return out.reshape(x.shape)
+
+
 def stiff_many(us, geoms, table):
     d = derivative_table()
     halves = [split(u) for u in us]
@@ -204,7 +218,7 @@
         axial = dot(axial_left(table), jnp.concatenate([high, low, high], axis=0)) * ga
         radial = radial_apply(radial_apply(u, d) * gr, d.T)
         part = girth[k * NODES : (k + 1) * NODES]
-        outs.append(left_mul(axial_left_t(table), axial) + part + radial)
+        outs.append(axial_apply(axial, d.T) + part + radial)
     return outs
 
 

time: 97.4 us -> 97.4 us (level)
  no operation moved by 1% of the time
where the time goes in v8:
time: 97.4 us; the launch traced here: 97 us
  starting transfers between devices  28.5 us (29%)
  blocking collectives  24.6 us (25%)
  Pallas kernels  22.2 us (23%)
  waiting for transfers between devices  18.3 us (19%)
  local copies, waits for them, and re-layouts  1.8 us (2%)
  between operations  1.54 us (2%)
    all_gather x1, blocking collectives, body(): rows = lax.all_gather(rows, 'girth')  24.6 us
    pallas_call x8, Pallas kernels, call(): pl.pallas_call(kernel, out_shape=out_shape, in_specs=[vmem] * len(args),...  19.1 us
    all_to_all x1, waiting for transfers between devices, body(): pieces = lax.all_to_all(packed, 'axial', 0, 0)  12.1 us
    ppermute x4, starting transfers between devices, exchange(): return (lax.ppermute(high, 'axial', up), lax.ppermute(low, 'axial', down))  11.2 us
    all_to_all x1, starting transfers between devices, body(): pieces = lax.all_to_all(packed, 'axial', 0, 0)  10.5 us
    ppermute x4, waiting for transfers between devices, exchange(): return (lax.ppermute(high, 'axial', up), lax.ppermute(low, 'axial', down))  6.24 us
    ppermute x1, starting transfers between devices, body(): right = lax.ppermute(to_left, 'girth', back)  4.22 us
    ppermute x1, starting transfers between devices, body(): left = lax.ppermute(to_right, 'girth', around)  2.7 us
  transfers between devices with their start and end apart: 7, of which 3 were waited for; matrix products, arithmetic and copies ran while one was open for 1% of the time, Pallas kernels for 7%

profile of v8, /device:TPU:1, one launch (start us, length us, event | category | flops | bytes accessed | tf_op | source)
XLA Modules:
  0.0 97.0 jit_solution(14138452659966344092)
XLA Ops:
  0.6 0.0 copy-start.2
  0.6 0.0 copy-start.6
  0.7 0.0 copy-start.7
  0.7 0.0 copy-start.4
  0.7 2.4 %shard_map.140 = (f32[2,256,128]{2,1,0:T(8,128)}, f32[2,256,128]{2,1,0:T(8,128)}) custom-call(f32[4,256,128]{2,1,0:T(8,128)} %bitcast.13, f32[3,256,128]{2,1,0:T(8,128)} %bitcast.16, f32[256,128]{1,0:T(8,128)} %bitcast.22), custom_call_target="tpu_custom_call" | custom-call | tf_op jit(solution)/shard_map/pallas_call | solution.py:678
  3.1 0.0 copy-start.11
  3.1 0.0 copy-start.8
  3.1 0.0 copy-start.9
  3.1 0.0 copy-start.10
  3.1 2.7 %collective-permute-start = (f32[2,256,128]{2,1,0:T(8,128)}, f32[2,256,128]{2,1,0:T(8,128)S(1)}, u32[]{:S(2)}, u32[]{:S(2)}) collective-permute-start(f32[2,256,128]{2,1,0:T(8,128)} %get-tuple-element.35), channel_id=1, source_target_pairs={{0,1},{1,2},{2,3},{3,4},{4,5},{5,6},{6,7},{7,8},{8,9},{9,10},{10,1... | collective-permute-start | bytes 786440 | tf_op jit(solution)/shard_map/ppermute | solution.py:704
  5.8 4.2 %collective-permute-start.1 = (f32[2,256,128]{2,1,0:T(8,128)}, f32[2,256,128]{2,1,0:T(8,128)S(1)}, u32[]{:S(2)}, u32[]{:S(2)}) collective-permute-start(f32[2,256,128]{2,1,0:T(8,128)} %get-tuple-element.36), channel_id=1, source_target_pairs={{1,0},{2,1},{3,2},{4,3},{5,4},{6,5},{7,6},{8,7},{9,8},{10,9},{11,1... | collective-permute-start | bytes 786440 | tf_op jit(solution)/shard_map/ppermute | solution.py:705
  10.0 0.0 copy-done.6
  10.0 0.0 copy-done.7
  10.0 0.0 copy-done.11
  10.0 0.0 copy-done.8
  10.0 0.0 copy-done.9
  10.1 0.0 copy-done.10
  10.1 0.2 shard_map.146
  10.3 0.0 copy-done.2
  10.3 0.0 copy-done.4
  10.3 0.0 copy-start.3
  10.3 1.0 %copy-done.3 = f32[4,16,16,128]{3,2,1,0:T(8,128)S(1)} copy-done((f32[4,16,16,128]{3,2,1,0:T(8,128)S(1)}, f32[4,16,16,128]{3,2,1,0:T(8,128)}, u32[]{:S(2)}) %copy-start.3) | copy-done | bytes 524312
  11.4 1.5 %shard_map.141.own_total = f32[256,512]{1,0:T(8,128)S(1)} custom-call(f32[4,256,128]{2,1,0:T(8,128)S(1)} %bitcast.14, f32[3,256,128]{2,1,0:T(8,128)S(1)} %bitcast.17, bf16[1216,256]{1,0:T(8,128)(2,1)S(1)} %copy-done.2), custom_call_target="tpu_custom_call" | custom-call | flops 1207959552 | bytes 2000000 | tf_op jit(solution)/shard_map/pallas_call | solution.py:666
  12.9 0.0 collective-permute-done.left
  12.9 0.0 collective-permute-done.1.right
  12.9 0.0 copy-done.5
  12.9 3.6 %shard_map.142 = (f32[3,256,256]{2,1,0:T(8,128)S(1)}, f32[256,768]{1,0:T(8,128)S(1)}, f32[256,384]{1,0:T(8,128)S(1)}, f32[256,384]{1,0:T(8,128)S(1)}, f32[16,307...) custom-call(f32[2,256,128]{2,1,0:T(8,128)S(1)} %collective-permute-done.left, ...), custom_call_target="tpu_custom_call" | custom-call | flops 1207959552 | bytes 2000000 | tf_op jit(solution)/shard_map/pallas_call | solution.py:666
  16.5 2.9 %collective-permute-start.2 = (f32[16,2304]{1,0:T(8,128)S(1)}, f32[16,2304]{1,0:T(8,128)S(1)}, u32[]{:S(2)}, u32[]{:S(2)}) collective-permute-start(f32[16,2304]{1,0:T(8,128)S(1)} %get-tuple-element.43), channel_id=1, source_target_pairs={{0,16},{16,32},{32,48},{48,64},{64,80},{80,96},{96,112},{112,128},... | collective-permute-start | bytes 442376 | tf_op jit(solution)/shard_map/ppermute | solution.py:709
  19.5 1.5 %collective-permute-start.3 = (f32[16,2304]{1,0:T(8,128)S(1)}, f32[16,2304]{1,0:T(8,128)S(1)}, u32[]{:S(2)}, u32[]{:S(2)}) collective-permute-start(f32[16,2304]{1,0:T(8,128)S(1)} %get-tuple-element.44), channel_id=1, source_target_pairs={{16,0},{32,16},{48,32},{64,48},{80,64},{96,80},{112,96},{128,112},... | collective-permute-start | bytes 442376 | tf_op jit(solution)/shard_map/ppermute | solution.py:709
  20.9 2.3 %shard_map.143.second = f32[256,768]{1,0:T(8,128)S(1)} custom-call(f32[256,768]{1,0:T(8,128)S(1)} %get-tuple-element.37.state, f32[3,256,128]{2,1,0:T(8,128)S(1)} %bitcast.19, f32[3,256,256]{2,1,0:T(8,128)S(1)} %get-tuple-element.38.halo_geom, bf16[1216,256]{1,0:T(8,128)(2,1)S(1)} %copy-done.2), custom_call_target="tpu_custom_call" | custom-call | flops 1811939328 | bytes 2000000 | tf_op jit(solution)/shard_map/pallas_call | solution.py:666
  23.3 0.0 collective-permute-done.2.got_low
  23.3 2.7 %collective-permute-done.3.got_high = f32[16,2304]{1,0:T(8,128)S(1)} collective-permute-done((f32[16,2304]{1,0:T(8,128)S(1)}, f32[16,2304]{1,0:T(8,128)S(1)}, u32[]{:S(2)}, u32[]{:S(2)}) %collective-permute-start.3) | collective-permute-done | bytes 147488 | tf_op jit(solution)/shard_map/ppermute | solution.py:709
  26.0 5.1 %shard_map.144 = (f32[256,768]{1,0:T(8,128)S(1)}, f32[256,384]{1,0:T(8,128)S(1)}, f32[16,1536]{1,0:T(8,128)S(1)}, f32[16,1536]{1,0:T(8,128)S(1)}) custom-call(f32[256,768]{1,0:T(8,128)S(1)} %get-tuple-element.37.state, f32[256,768]{1,0:T(8,128)S(1)} %shard_map.143.second, f32[256,384]{1,0:T(8,128)S(1)} %get-tuple-element.39.lumped, ...), custom_call_target="tpu_custom_call" | custom-call | flops 2415919104 | bytes 2000000 | tf_op jit(solution)/shard_map/pallas_call | solution.py:666
  31.1 5.5 %collective-permute-start.4 = (f32[16,1536]{1,0:T(8,128)S(1)}, f32[16,1536]{1,0:T(8,128)S(1)}, u32[]{:S(2)}, u32[]{:S(2)}) collective-permute-start(f32[16,1536]{1,0:T(8,128)S(1)} %get-tuple-element.48.own_high), channel_id=1, source_target_pairs={{0,16},{16,32},{32,48},{48,64},{64,80},{80,96},{96,112},{112,128},... | collective-permute-start | bytes 294920 | tf_op jit(solution)/shard_map/ppermute | solution.py:709
  36.5 1.3 %collective-permute-start.5 = (f32[16,1536]{1,0:T(8,128)S(1)}, f32[16,1536]{1,0:T(8,128)S(1)}, u32[]{:S(2)}, u32[]{:S(2)}) collective-permute-start(f32[16,1536]{1,0:T(8,128)S(1)} %get-tuple-element.47.own_low), channel_id=1, source_target_pairs={{16,0},{32,16},{48,32},{64,48},{80,64},{96,80},{112,96},{128,112},... | collective-permute-start | bytes 294920 | tf_op jit(solution)/shard_map/ppermute | solution.py:709
  37.8 2.3 %shard_map.145.second = f32[256,768]{1,0:T(8,128)S(1)} custom-call(f32[256,768]{1,0:T(8,128)S(1)} %get-tuple-element.45.state, f32[3,256,128]{2,1,0:T(8,128)S(1)} %bitcast.21, f32[3,256,256]{2,1,0:T(8,128)S(1)} %get-tuple-element.38.halo_geom, bf16[1216,256]{1,0:T(8,128)(2,1)S(1)} %copy-done.2), custom_call_target="tpu_custom_call" | custom-call | flops 1811939328 | bytes 2000000 | tf_op jit(solution)/shard_map/pallas_call | solution.py:666
  40.2 0.0 collective-permute-done.4.new_low
  40.2 3.5 %collective-permute-done.5.new_high = f32[16,1536]{1,0:T(8,128)S(1)} collective-permute-done((f32[16,1536]{1,0:T(8,128)S(1)}, f32[16,1536]{1,0:T(8,128)S(1)}, u32[]{:S(2)}, u32[]{:S(2)}) %collective-permute-start.5) | collective-permute-done | bytes 98336 | tf_op jit(solution)/shard_map/ppermute | solution.py:709
  43.7 2.7 %shard_map.147 = (f32[4,256,128]{2,1,0:T(8,128)}, f32[32,32,128]{2,1,0:T(8,128)}, f32[64,512]{1,0:T(8,128)S(1)}) custom-call(f32[256,768]{1,0:T(8,128)S(1)} %get-tuple-element.45.state, f32[256,768]{1,0:T(8,128)S(1)} %shard_map.145.second, f32[256,384]{1,0:T(8,128)S(1)} %get-tuple-element.46.inverse, f32[256,384]{1,0:T(8,128)S(1)} %get-tuple-element.40.ends, ...), custom_call_target="tpu_custom_call" | custom-call | flops 603979776 | bytes 2000000 | tf_op jit(solution)/shard_map/pallas_call | solution.py:666
  46.5 10.5 %all-to-all-start.1 = ((f32[32,32,128]{2,1,0:T(8,128)}), f32[32,32,128]{2,1,0:T(8,128)S(1)}, u32[]{:S(2)}, u32[]{:S(2)}) async-start(f32[32,32,128]{2,1,0:T(8,128)} %get-tuple-element.54), calls=%async_computation.1 | async-start | bytes 1048576 | tf_op jit(solution)/shard_map/all_to_all | solution.py:786
  56.9 0.7 dynamic-slice_bitcast_fusion.phase
  57.6 12.1 %all-to-all-done.1.pieces = f32[32,32,128]{2,1,0:T(8,128)S(1)} async-done(((f32[32,32,128]{2,1,0:T(8,128)}), f32[32,32,128]{2,1,0:T(8,128)S(1)}, u32[]{:S(2)}, u32[]{:S(2)}) %all-to-all-start.1) | async-done | bytes 524320 | tf_op jit(solution)/shard_map/all_to_all | solution.py:786
  69.7 0.8 shard_map.148
  71.1 0.0 copy-start
  71.1 0.0 copy-start.1
  71.1 24.6 %all-gather = f32[1024,128]{1,0:T(8,128)S(1)} all-gather(f32[64,128]{1,0:T(8,128)S(1)} %get-tuple-element.58), channel_id=2, replica_groups=mesh['axial'=32,'girth'=16] {'girth'}, dimensions={0}, use_global_device_ids=true | all-gather | bytes 557056 | tf_op jit(solution)/shard_map/all_gather | solution.py:811
  95.7 0.0 copy-done
  95.7 1.2 %shard_map.149 = f32[2,16,4,128]{3,2,1,0:T(4,128)} custom-call(f32[16,64,128]{2,1,0:T(8,128)S(1)} %bitcast.12, f32[2,128]{1,0:T(2,128)S(1)} %dynamic-slice_bitcast_fusion.phase, bf16[2048,256]{1,0:T(8,128)(2,1)S(1)} %copy-done, bf16[2048,256]{1,0:T(8,128)(2,1)S(1)} %copy-done.1), custom_call_target="tpu_custom_call" | custom-call | flops 603979776 | bytes 2000000 | tf_op jit(solution)/shard_map/pallas_call | solution.py:666
  (3 shorter events, 0.0 us)
Async XLA Ops:
  0.6 9.7 %copy-start.2 = (bf16[1216,256]{1,0:T(8,128)(2,1)S(1)}, bf16[1216,256]{1,0:T(8,128)(2,1)}, u32[]{:S(2)}) copy-start(bf16[1216,256]{1,0:T(8,128)(2,1)} %constant.23.clone.table.tables.refs_0_) | copy-start | bytes 1867780
  0.6 9.4 %copy-start.6 = (f32[2,8,64]{2,1,0:T(8,128)S(1)}, f32[2,8,64]{2,1,0:T(8,128)}, u32[]{:S(2)}) copy-start(f32[2,8,64]{2,1,0:T(8,128)} %cycle_weights.1) | copy-start | bytes 12292
  0.7 9.4 %copy-start.7 = (f32[8,128]{1,0:T(8,128)S(1)}, f32[8,128]{1,0:T(8,128)}, u32[]{:S(2)}) copy-start(f32[8,128]{1,0:T(8,128)} %az_weights.1) | copy-start | bytes 12292
  0.7 9.7 %copy-start.4 = (f32[3,16,16,128]{3,2,1,0:T(8,128)S(1)}, f32[3,16,16,128]{3,2,1,0:T(8,128)}, u32[]{:S(2)}) copy-start(f32[3,16,16,128]{3,2,1,0:T(8,128)} %param.16) | copy-start | bytes 1179652
  3.1 7.0 %copy-start.11 = (s32[64]{0:T(128)S(1)}, s32[64]{0:T(128)}, u32[]{:S(2)}) copy-start(s32[64]{0:T(128)} %cycle_id.1) | copy-start | bytes 772
  3.1 7.0 %copy-start.8 = (s32[64]{0:T(128)S(1)}, s32[64]{0:T(128)}, u32[]{:S(2)}) copy-start(s32[64]{0:T(128)} %cycle_radial.1) | copy-start | bytes 772
  3.1 7.0 %copy-start.9 = (s32[64]{0:T(128)S(1)}, s32[64]{0:T(128)}, u32[]{:S(2)}) copy-start(s32[64]{0:T(128)} %cycle_axial.1) | copy-start | bytes 772
  3.1 7.0 %copy-start.10 = (s32[128]{0:T(128)S(1)}, s32[128]{0:T(128)}, u32[]{:S(2)}) copy-start(s32[128]{0:T(128)} %az_elem.1) | copy-start | bytes 1540
  3.1 9.7 %collective-permute-start = (f32[2,256,128]{2,1,0:T(8,128)}, f32[2,256,128]{2,1,0:T(8,128)S(1)}, u32[]{:S(2)}, u32[]{:S(2)}) collective-permute-start(f32[2,256,128]{2,1,0:T(8,128)} %get-tuple-element.35), channel_id=1, source_target_pairs={{0,1},{1,2},{2,3},{3,4},{4,5},{5,6},{6,7},{7,8},{8,9},{9,10},{10,1... | collective-permute-start | bytes 786440 | tf_op jit(solution)/shard_map/ppermute | solution.py:704
  5.8 7.1 %collective-permute-start.1 = (f32[2,256,128]{2,1,0:T(8,128)}, f32[2,256,128]{2,1,0:T(8,128)S(1)}, u32[]{:S(2)}, u32[]{:S(2)}) collective-permute-start(f32[2,256,128]{2,1,0:T(8,128)} %get-tuple-element.36), channel_id=1, source_target_pairs={{1,0},{2,1},{3,2},{4,3},{5,4},{6,5},{7,6},{8,7},{9,8},{10,9},{11,1... | collective-permute-start | bytes 786440 | tf_op jit(solution)/shard_map/ppermute | solution.py:705
  10.3 1.1 %copy-start.3 = (f32[4,16,16,128]{3,2,1,0:T(8,128)S(1)}, f32[4,16,16,128]{3,2,1,0:T(8,128)}, u32[]{:S(2)}) copy-start(f32[4,16,16,128]{3,2,1,0:T(8,128)} %param.15) | copy-start | bytes 1572868
  11.4 1.5 %copy-start.5 = (f32[16,16,128]{2,1,0:T(8,128)S(1)}, f32[16,16,128]{2,1,0:T(8,128)}, u32[]{:S(2)}) copy-start(f32[16,16,128]{2,1,0:T(8,128)} %param.17) | copy-start | bytes 393220
  16.5 6.8 %collective-permute-start.2 = (f32[16,2304]{1,0:T(8,128)S(1)}, f32[16,2304]{1,0:T(8,128)S(1)}, u32[]{:S(2)}, u32[]{:S(2)}) collective-permute-start(f32[16,2304]{1,0:T(8,128)S(1)} %get-tuple-element.43), channel_id=1, source_target_pairs={{0,16},{16,32},{32,48},{48,64},{64,80},{80,96},{96,112},{112,128},... | collective-permute-start | bytes 442376 | tf_op jit(solution)/shard_map/ppermute | solution.py:709
  19.5 6.5 %collective-permute-start.3 = (f32[16,2304]{1,0:T(8,128)S(1)}, f32[16,2304]{1,0:T(8,128)S(1)}, u32[]{:S(2)}, u32[]{:S(2)}) collective-permute-start(f32[16,2304]{1,0:T(8,128)S(1)} %get-tuple-element.44), channel_id=1, source_target_pairs={{16,0},{32,16},{48,32},{64,48},{80,64},{96,80},{112,96},{128,112},... | collective-permute-start | bytes 442376 | tf_op jit(solution)/shard_map/ppermute | solution.py:709
  31.1 9.1 %collective-permute-start.4 = (f32[16,1536]{1,0:T(8,128)S(1)}, f32[16,1536]{1,0:T(8,128)S(1)}, u32[]{:S(2)}, u32[]{:S(2)}) collective-permute-start(f32[16,1536]{1,0:T(8,128)S(1)} %get-tuple-element.48.own_high), channel_id=1, source_target_pairs={{0,16},{16,32},{32,48},{48,64},{64,80},{80,96},{96,112},{112,128},... | collective-permute-start | bytes 294920 | tf_op jit(solution)/shard_map/ppermute | solution.py:709
  36.5 7.2 %collective-permute-start.5 = (f32[16,1536]{1,0:T(8,128)S(1)}, f32[16,1536]{1,0:T(8,128)S(1)}, u32[]{:S(2)}, u32[]{:S(2)}) collective-permute-start(f32[16,1536]{1,0:T(8,128)S(1)} %get-tuple-element.47.own_low), channel_id=1, source_target_pairs={{16,0},{32,16},{48,32},{64,48},{80,64},{96,80},{112,96},{128,112},... | collective-permute-start | bytes 294920 | tf_op jit(solution)/shard_map/ppermute | solution.py:709
  46.5 23.2 %all-to-all-start.1 = ((f32[32,32,128]{2,1,0:T(8,128)}), f32[32,32,128]{2,1,0:T(8,128)S(1)}, u32[]{:S(2)}, u32[]{:S(2)}) async-start(f32[32,32,128]{2,1,0:T(8,128)} %get-tuple-element.54), calls=%async_computation.1 | async-start | bytes 1048576 | tf_op jit(solution)/shard_map/all_to_all | solution.py:786
  71.1 24.6 %copy-start = (bf16[2048,256]{1,0:T(8,128)(2,1)S(1)}, bf16[2048,256]{1,0:T(8,128)(2,1)}, u32[]{:S(2)}) copy-start(bf16[2048,256]{1,0:T(8,128)(2,1)} %constant.25.clone.table_high) | copy-start | bytes 3145732
  71.1 24.6 %copy-start.1 = (bf16[2048,256]{1,0:T(8,128)(2,1)S(1)}, bf16[2048,256]{1,0:T(8,128)(2,1)}, u32[]{:S(2)}) copy-start(bf16[2048,256]{1,0:T(8,128)(2,1)} %constant.26.clone.table_low) | copy-start | bytes 3145732

commit v9 on v7

--- a/solution.py
+++ b/solution.py
@@ -395,11 +395,31 @@
     return y + pltpu.roll(y, 2 * HALO, 1)
 
 
+OWN = C * LANES
+FIRST_SENT = WIDE + OWN + LANES
+SECOND_SENT = OWN + LANES + OWN
+
+
+def near(shape):
+    return lax.broadcasted_iota(jnp.int32, shape, 1) % HALO >= HALO // 2
+
+
+def join_halves(x):
+    return jnp.where(near((16, LANES)), x[:, :LANES], x[:, LANES:])
+
+
+def part_halves(x):
+    inside = near(x.shape)
+    return [jnp.where(inside, x, 0.0), jnp.where(inside, 0.0, x)]
+
+
 def to_send(face, out):
-    out[:, :STATIC] = face[:, :STATIC]
+    out[:, : WIDE + OWN] = face[:, : WIDE + OWN]
+    out[:, WIDE + OWN : FIRST_SENT] = join_halves(face[:, WIDE + OWN : STATIC])
     lane = lax.broadcasted_iota(jnp.int32, (16, LANES), 1) // HALO
     for k in range(4):
-        out[:, STATIC + k * LANES : STATIC + (k + 1) * LANES] = static_part(face, k)[:, :LANES]
+        at = FIRST_SENT + k * LANES
+        out[:, at : at + LANES] = static_part(face, k)[:, :LANES]
     for k in range(2):
         parts = []
         for j in (2 * k, 2 * k + 1):
@@ -407,16 +427,30 @@
         block = parts[3]
         for j in range(3):
             block = jnp.where(lane == j, parts[j], block)
-        out[:, STATIC + (4 + k) * LANES : STATIC + (5 + k) * LANES] = block
+        at = FIRST_SENT + (4 + k) * LANES
+        out[:, at : at + LANES] = block
 
 
 def as_sent(got):
-    pieces = [got[:, :STATIC]]
+    pieces = [got[:, : WIDE + OWN]] + part_halves(got[:, WIDE + OWN : FIRST_SENT])
     for k in range(4):
-        halos = got[:, STATIC + (4 + k // 2) * LANES : STATIC + (5 + k // 2) * LANES]
+        at = FIRST_SENT + (4 + k // 2) * LANES
+        halos = got[:, at : at + LANES]
         place = 2 * (k % 2)
-        pieces.append(got[:, STATIC + k * LANES : STATIC + (k + 1) * LANES])
+        pieces.append(got[:, FIRST_SENT + k * LANES : FIRST_SENT + (k + 1) * LANES])
         pieces += [spread(halos, place), spread(halos, place + 1)]
+    return jnp.concatenate(pieces, axis=1)
+
+
+def to_send_second(face, out):
+    out[:, :OWN] = face[:, :OWN]
+    out[:, OWN : OWN + LANES] = join_halves(face[:, OWN:WIDE])
+    out[:, OWN + LANES :] = face[:, WIDE : WIDE + OWN]
+
+
+def second_as_sent(got):
+    pieces = [got[:, :OWN]] + part_halves(got[:, OWN : OWN + LANES])
+    pieces += [got[:, OWN + LANES :], jnp.zeros((16, 2 * LANES), F32)]
     return jnp.concatenate(pieces, axis=1)
 
 
@@ -490,7 +524,7 @@
 
 
 def middle_kernel(state, second, lumped, ends, low, high, got_low, got_high, geom, halo_geom, *refs):
-    tables, state_out, inverse_out, next_low, next_high = refs
+    tables, state_out, inverse_out, next_low, next_high, *sent = refs
     got_low, got_high = as_sent(got_low), as_sent(got_high)
     inverse = 1.0 / (
         lumped[...] + at_faces(static_part(got_low, 0), static_part(got_high, 0), NARROW)
@@ -502,6 +536,8 @@
     )
     first = action(u, geom, halo_geom, tables)
     two_steps(u, geom, halo_geom, inverse, first, (low, high), tables, state_out, next_low, next_high)
+    to_send_second(next_low, sent[0])
+    to_send_second(next_high, sent[1])
 
 
 def last_kernel(
@@ -533,7 +569,7 @@
         ends[...],
         (low, high, as_sent(got_low), as_sent(got_high)),
         (own_low, own_high),
-        (new_low, new_high),
+        (second_as_sent(new_low), second_as_sent(new_high)),
         tables,
         C * LANES,
     )
@@ -695,7 +731,7 @@
         return lax.ppermute(high, "axial", up), lax.ppermute(low, "axial", down)
 
     whole, narrow = (NODES, WIDE), (NODES, NARROW)
-    face_static, sent = (16, STATIC + 4 * NARROW), (16, STATIC + 6 * LANES)
+    face_static, sent = (16, STATIC + 4 * NARROW), (16, FIRST_SENT + 6 * LANES)
     halo_geom, state, lumped, ends, low, high, send_low, send_high = call(
         halo_kernel,
         [(3, NODES, 2 * LANES), whole, narrow, narrow, face_static, face_static, sent, sent],
@@ -710,9 +746,9 @@
     )
     got_low, got_high = exchange(send_low, send_high)
     (second,) = call(second_kernel, [whole], 3 * tile_flops, state, geom, halo_geom, table)
-    state, inverse, own_low, own_high = call(
+    state, inverse, own_low, own_high, send_low, send_high = call(
         middle_kernel,
-        [whole, narrow, (16, STATIC), (16, STATIC)],
+        [whole, narrow, (16, STATIC), (16, STATIC), (16, SECOND_SENT), (16, SECOND_SENT)],
         4 * tile_flops,
         state,
         second,
@@ -726,7 +762,7 @@
         halo_geom,
         table,
     )
-    new_low, new_high = exchange(own_low, own_high)
+    new_low, new_high = exchange(send_low, send_high)
     (second,) = call(second_kernel, [whole], 3 * tile_flops, state, geom, halo_geom, table)
 
     slot_count = cycle_id.shape[0]

time: 97.4 us -> 96.5 us (level)
  no operation moved by 1% of the time
where the time goes in v9:
time: 96.5 us; the launch traced here: 96.1 us
  starting transfers between devices  28.5 us (30%)
  blocking collectives  24.1 us (25%)
  Pallas kernels  22.3 us (23%)
  waiting for transfers between devices  17.9 us (19%)
  local copies, waits for them, and re-layouts  1.8 us (2%)
  between operations  1.54 us (2%)
    all_gather x1, blocking collectives, body(): rows = lax.all_gather(rows, 'girth')  24.1 us
    pallas_call x8, Pallas kernels, call(): pl.pallas_call(kernel, out_shape=out_shape, in_specs=[vmem] * len(args),...  19.2 us
    all_to_all x1, waiting for transfers between devices, body(): pieces = lax.all_to_all(packed, 'axial', 0, 0)  12.1 us
    ppermute x4, starting transfers between devices, exchange(): return (lax.ppermute(high, 'axial', up), lax.ppermute(low, 'axial', down))  11.1 us
    all_to_all x1, starting transfers between devices, body(): pieces = lax.all_to_all(packed, 'axial', 0, 0)  10.5 us
    ppermute x4, waiting for transfers between devices, exchange(): return (lax.ppermute(high, 'axial', up), lax.ppermute(low, 'axial', down))  5.77 us
    ppermute x1, starting transfers between devices, body(): right = lax.ppermute(to_left, 'girth', back)  4.22 us
    ppermute x1, starting transfers between devices, body(): left = lax.ppermute(to_right, 'girth', around)  2.7 us
  transfers between devices with their start and end apart: 7, of which 3 were waited for; matrix products, arithmetic and copies ran while one was open for 1% of the time, Pallas kernels for 7%

profile of v9, /device:TPU:1, one launch (start us, length us, event | category | flops | bytes accessed | tf_op | source)
XLA Modules:
  0.0 96.1 jit_solution(3176403249701085915)
XLA Ops:
  0.6 0.0 copy-start.2
  0.6 0.0 copy-start.6
  0.7 0.0 copy-start.7
  0.7 0.0 copy-start.4
  0.7 2.4 %shard_map.140 = (f32[2,256,128]{2,1,0:T(8,128)}, f32[2,256,128]{2,1,0:T(8,128)}) custom-call(f32[4,256,128]{2,1,0:T(8,128)} %bitcast.13, f32[3,256,128]{2,1,0:T(8,128)} %bitcast.16, f32[256,128]{1,0:T(8,128)} %bitcast.22), custom_call_target="tpu_custom_call" | custom-call | tf_op jit(solution)/shard_map/pallas_call | solution.py:700
  3.1 0.0 copy-start.11
  3.1 0.0 copy-start.8
  3.1 0.0 copy-start.9
  3.1 0.0 copy-start.10
  3.1 2.7 %collective-permute-start = (f32[2,256,128]{2,1,0:T(8,128)}, f32[2,256,128]{2,1,0:T(8,128)S(1)}, u32[]{:S(2)}, u32[]{:S(2)}) collective-permute-start(f32[2,256,128]{2,1,0:T(8,128)} %get-tuple-element.37), channel_id=1, source_target_pairs={{0,1},{1,2},{2,3},{3,4},{4,5},{5,6},{6,7},{7,8},{8,9},{9,10},{10,1... | collective-permute-start | bytes 786440 | tf_op jit(solution)/shard_map/ppermute | solution.py:726
  5.8 4.2 %collective-permute-start.1 = (f32[2,256,128]{2,1,0:T(8,128)}, f32[2,256,128]{2,1,0:T(8,128)S(1)}, u32[]{:S(2)}, u32[]{:S(2)}) collective-permute-start(f32[2,256,128]{2,1,0:T(8,128)} %get-tuple-element.38), channel_id=1, source_target_pairs={{1,0},{2,1},{3,2},{4,3},{5,4},{6,5},{7,6},{8,7},{9,8},{10,9},{11,1... | collective-permute-start | bytes 786440 | tf_op jit(solution)/shard_map/ppermute | solution.py:727
  10.0 0.0 copy-done.6
  10.0 0.0 copy-done.7
  10.0 0.0 copy-done.11
  10.0 0.0 copy-done.8
  10.0 0.0 copy-done.9
  10.1 0.0 copy-done.10
  10.1 0.2 shard_map.146
  10.3 0.0 copy-done.2
  10.3 0.0 copy-done.4
  10.3 0.0 copy-start.3
  10.3 1.0 %copy-done.3 = f32[4,16,16,128]{3,2,1,0:T(8,128)S(1)} copy-done((f32[4,16,16,128]{3,2,1,0:T(8,128)S(1)}, f32[4,16,16,128]{3,2,1,0:T(8,128)}, u32[]{:S(2)}) %copy-start.3) | copy-done | bytes 524312
  11.4 1.4 %shard_map.141.own_total = f32[256,512]{1,0:T(8,128)S(1)} custom-call(f32[4,256,128]{2,1,0:T(8,128)S(1)} %bitcast.14, f32[3,256,128]{2,1,0:T(8,128)S(1)} %bitcast.17, bf16[1216,256]{1,0:T(8,128)(2,1)S(1)} %copy-done.2), custom_call_target="tpu_custom_call" | custom-call | flops 1207959552 | bytes 2000000 | tf_op jit(solution)/shard_map/pallas_call | solution.py:688
  12.8 0.0 collective-permute-done.left
  12.8 0.0 collective-permute-done.1.right
  12.8 0.0 copy-done.5
  12.8 3.4 %shard_map.142 = (f32[3,256,256]{2,1,0:T(8,128)S(1)}, f32[256,768]{1,0:T(8,128)S(1)}, f32[256,384]{1,0:T(8,128)S(1)}, f32[256,384]{1,0:T(8,128)S(1)}, f32[16,307...) custom-call(f32[2,256,128]{2,1,0:T(8,128)S(1)} %collective-permute-done.left, ...), custom_call_target="tpu_custom_call" | custom-call | flops 1207959552 | bytes 2000000 | tf_op jit(solution)/shard_map/pallas_call | solution.py:688
  16.3 3.0 %collective-permute-start.2 = (f32[16,2176]{1,0:T(8,128)S(1)}, f32[16,2176]{1,0:T(8,128)S(1)}, u32[]{:S(2)}, u32[]{:S(2)}) collective-permute-start(f32[16,2176]{1,0:T(8,128)S(1)} %get-tuple-element.45), channel_id=1, source_target_pairs={{0,16},{16,32},{32,48},{48,64},{64,80},{80,96},{96,112},{112,128},... | collective-permute-start | bytes 417800 | tf_op jit(solution)/shard_map/ppermute | solution.py:731
  19.3 1.3 %collective-permute-start.3 = (f32[16,2176]{1,0:T(8,128)S(1)}, f32[16,2176]{1,0:T(8,128)S(1)}, u32[]{:S(2)}, u32[]{:S(2)}) collective-permute-start(f32[16,2176]{1,0:T(8,128)S(1)} %get-tuple-element.46), channel_id=1, source_target_pairs={{16,0},{32,16},{48,32},{64,48},{80,64},{96,80},{112,96},{128,112},... | collective-permute-start | bytes 417800 | tf_op jit(solution)/shard_map/ppermute | solution.py:731
  20.6 2.4 %shard_map.143.second = f32[256,768]{1,0:T(8,128)S(1)} custom-call(f32[256,768]{1,0:T(8,128)S(1)} %get-tuple-element.39.state, f32[3,256,128]{2,1,0:T(8,128)S(1)} %bitcast.19, f32[3,256,256]{2,1,0:T(8,128)S(1)} %get-tuple-element.40.halo_geom, bf16[1216,256]{1,0:T(8,128)(2,1)S(1)} %copy-done.2), custom_call_target="tpu_custom_call" | custom-call | flops 1811939328 | bytes 2000000 | tf_op jit(solution)/shard_map/pallas_call | solution.py:688
  23.0 0.0 collective-permute-done.2.got_low
  23.0 2.7 %collective-permute-done.3.got_high = f32[16,2176]{1,0:T(8,128)S(1)} collective-permute-done((f32[16,2176]{1,0:T(8,128)S(1)}, f32[16,2176]{1,0:T(8,128)S(1)}, u32[]{:S(2)}, u32[]{:S(2)}) %collective-permute-start.3) | collective-permute-done | bytes 139296 | tf_op jit(solution)/shard_map/ppermute | solution.py:731
  25.7 5.3 %shard_map.144 = (f32[256,768]{1,0:T(8,128)S(1)}, f32[256,384]{1,0:T(8,128)S(1)}, f32[16,1536]{1,0:T(8,128)S(1)}, f32[16,1536]{1,0:T(8,128)S(1)}, f32[16,1152]{1,0:T(8,128)S(1)}, /*index=5*/f32[16,1152]{1,0:T(8,128)S(1)}) custom-call(f32[256,768]{1,0:T(8,128)S(1)} %get-tuple-element.39.state, f32[256,768]{1,0:T(8,128)S(1)} %shard_map.143.second, ...), custom_call_target="tpu_custom_call" | custom-call | flops 2415919104 | bytes 2000000 | tf_op jit(solution)/shard_map/pallas_call | solution.py:688
  31.0 5.4 %collective-permute-start.4 = (f32[16,1152]{1,0:T(8,128)S(1)}, f32[16,1152]{1,0:T(8,128)S(1)}, u32[]{:S(2)}, u32[]{:S(2)}) collective-permute-start(f32[16,1152]{1,0:T(8,128)S(1)} %get-tuple-element.51), channel_id=1, source_target_pairs={{0,16},{16,32},{32,48},{48,64},{64,80},{80,96},{96,112},{112,128},... | collective-permute-start | bytes 221192 | tf_op jit(solution)/shard_map/ppermute | solution.py:731
  36.4 1.5 %collective-permute-start.5 = (f32[16,1152]{1,0:T(8,128)S(1)}, f32[16,1152]{1,0:T(8,128)S(1)}, u32[]{:S(2)}, u32[]{:S(2)}) collective-permute-start(f32[16,1152]{1,0:T(8,128)S(1)} %get-tuple-element.52), channel_id=1, source_target_pairs={{16,0},{32,16},{48,32},{64,48},{80,64},{96,80},{112,96},{128,112},... | collective-permute-start | bytes 221192 | tf_op jit(solution)/shard_map/ppermute | solution.py:731
  37.9 2.4 %shard_map.145.second = f32[256,768]{1,0:T(8,128)S(1)} custom-call(f32[256,768]{1,0:T(8,128)S(1)} %get-tuple-element.47.state, f32[3,256,128]{2,1,0:T(8,128)S(1)} %bitcast.21, f32[3,256,256]{2,1,0:T(8,128)S(1)} %get-tuple-element.40.halo_geom, bf16[1216,256]{1,0:T(8,128)(2,1)S(1)} %copy-done.2), custom_call_target="tpu_custom_call" | custom-call | flops 1811939328 | bytes 2000000 | tf_op jit(solution)/shard_map/pallas_call | solution.py:688
  40.3 0.0 collective-permute-done.4.new_low
  40.3 3.0 %collective-permute-done.5.new_high = f32[16,1152]{1,0:T(8,128)S(1)} collective-permute-done((f32[16,1152]{1,0:T(8,128)S(1)}, f32[16,1152]{1,0:T(8,128)S(1)}, u32[]{:S(2)}, u32[]{:S(2)}) %collective-permute-start.5) | collective-permute-done | bytes 73760 | tf_op jit(solution)/shard_map/ppermute | solution.py:731
  43.4 2.7 %shard_map.147 = (f32[4,256,128]{2,1,0:T(8,128)}, f32[32,32,128]{2,1,0:T(8,128)}, f32[64,512]{1,0:T(8,128)S(1)}) custom-call(f32[256,768]{1,0:T(8,128)S(1)} %get-tuple-element.47.state, f32[256,768]{1,0:T(8,128)S(1)} %shard_map.145.second, f32[256,384]{1,0:T(8,128)S(1)} %get-tuple-element.48.inverse, f32[256,384]{1,0:T(8,128)S(1)} %get-tuple-element.42.ends, ...), custom_call_target="tpu_custom_call" | custom-call | flops 603979776 | bytes 2000000 | tf_op jit(solution)/shard_map/pallas_call | solution.py:688
  46.1 10.5 %all-to-all-start.1 = ((f32[32,32,128]{2,1,0:T(8,128)}), f32[32,32,128]{2,1,0:T(8,128)S(1)}, u32[]{:S(2)}, u32[]{:S(2)}) async-start(f32[32,32,128]{2,1,0:T(8,128)} %get-tuple-element.58), calls=%async_computation.1 | async-start | bytes 1048576 | tf_op jit(solution)/shard_map/all_to_all | solution.py:808
  56.5 0.7 dynamic-slice_bitcast_fusion.phase
  57.2 12.1 %all-to-all-done.1.pieces = f32[32,32,128]{2,1,0:T(8,128)S(1)} async-done(((f32[32,32,128]{2,1,0:T(8,128)}), f32[32,32,128]{2,1,0:T(8,128)S(1)}, u32[]{:S(2)}, u32[]{:S(2)}) %all-to-all-start.1) | async-done | bytes 524320 | tf_op jit(solution)/shard_map/all_to_all | solution.py:808
  69.3 0.8 shard_map.148
  70.7 0.0 copy-start
  70.7 0.0 copy-start.1
  70.8 24.1 %all-gather = f32[1024,128]{1,0:T(8,128)S(1)} all-gather(f32[64,128]{1,0:T(8,128)S(1)} %get-tuple-element.62), channel_id=2, replica_groups=mesh['axial'=32,'girth'=16] {'girth'}, dimensions={0}, use_global_device_ids=true | all-gather | bytes 557056 | tf_op jit(solution)/shard_map/all_gather | solution.py:833
  94.8 0.0 copy-done
  94.9 1.2 %shard_map.149 = f32[2,16,4,128]{3,2,1,0:T(4,128)} custom-call(f32[16,64,128]{2,1,0:T(8,128)S(1)} %bitcast.12, f32[2,128]{1,0:T(2,128)S(1)} %dynamic-slice_bitcast_fusion.phase, bf16[2048,256]{1,0:T(8,128)(2,1)S(1)} %copy-done, bf16[2048,256]{1,0:T(8,128)(2,1)S(1)} %copy-done.1), custom_call_target="tpu_custom_call" | custom-call | flops 603979776 | bytes 2000000 | tf_op jit(solution)/shard_map/pallas_call | solution.py:688
  (3 shorter events, 0.0 us)
Async XLA Ops:
  0.6 9.7 %copy-start.2 = (bf16[1216,256]{1,0:T(8,128)(2,1)S(1)}, bf16[1216,256]{1,0:T(8,128)(2,1)}, u32[]{:S(2)}) copy-start(bf16[1216,256]{1,0:T(8,128)(2,1)} %constant.23.clone.table.tables.refs_0_) | copy-start | bytes 1867780
  0.6 9.4 %copy-start.6 = (f32[2,8,64]{2,1,0:T(8,128)S(1)}, f32[2,8,64]{2,1,0:T(8,128)}, u32[]{:S(2)}) copy-start(f32[2,8,64]{2,1,0:T(8,128)} %cycle_weights.1) | copy-start | bytes 12292
  0.7 9.4 %copy-start.7 = (f32[8,128]{1,0:T(8,128)S(1)}, f32[8,128]{1,0:T(8,128)}, u32[]{:S(2)}) copy-start(f32[8,128]{1,0:T(8,128)} %az_weights.1) | copy-start | bytes 12292
  0.7 9.7 %copy-start.4 = (f32[3,16,16,128]{3,2,1,0:T(8,128)S(1)}, f32[3,16,16,128]{3,2,1,0:T(8,128)}, u32[]{:S(2)}) copy-start(f32[3,16,16,128]{3,2,1,0:T(8,128)} %param.16) | copy-start | bytes 1179652
  3.1 7.0 %copy-start.11 = (s32[64]{0:T(128)S(1)}, s32[64]{0:T(128)}, u32[]{:S(2)}) copy-start(s32[64]{0:T(128)} %cycle_id.1) | copy-start | bytes 772
  3.1 7.0 %copy-start.8 = (s32[64]{0:T(128)S(1)}, s32[64]{0:T(128)}, u32[]{:S(2)}) copy-start(s32[64]{0:T(128)} %cycle_radial.1) | copy-start | bytes 772
  3.1 7.0 %copy-start.9 = (s32[64]{0:T(128)S(1)}, s32[64]{0:T(128)}, u32[]{:S(2)}) copy-start(s32[64]{0:T(128)} %cycle_axial.1) | copy-start | bytes 772
  3.1 7.0 %copy-start.10 = (s32[128]{0:T(128)S(1)}, s32[128]{0:T(128)}, u32[]{:S(2)}) copy-start(s32[128]{0:T(128)} %az_elem.1) | copy-start | bytes 1540
  3.1 9.7 %collective-permute-start = (f32[2,256,128]{2,1,0:T(8,128)}, f32[2,256,128]{2,1,0:T(8,128)S(1)}, u32[]{:S(2)}, u32[]{:S(2)}) collective-permute-start(f32[2,256,128]{2,1,0:T(8,128)} %get-tuple-element.37), channel_id=1, source_target_pairs={{0,1},{1,2},{2,3},{3,4},{4,5},{5,6},{6,7},{7,8},{8,9},{9,10},{10,1... | collective-permute-start | bytes 786440 | tf_op jit(solution)/shard_map/ppermute | solution.py:726
  5.8 7.0 %collective-permute-start.1 = (f32[2,256,128]{2,1,0:T(8,128)}, f32[2,256,128]{2,1,0:T(8,128)S(1)}, u32[]{:S(2)}, u32[]{:S(2)}) collective-permute-start(f32[2,256,128]{2,1,0:T(8,128)} %get-tuple-element.38), channel_id=1, source_target_pairs={{1,0},{2,1},{3,2},{4,3},{5,4},{6,5},{7,6},{8,7},{9,8},{10,9},{11,1... | collective-permute-start | bytes 786440 | tf_op jit(solution)/shard_map/ppermute | solution.py:727
  10.3 1.1 %copy-start.3 = (f32[4,16,16,128]{3,2,1,0:T(8,128)S(1)}, f32[4,16,16,128]{3,2,1,0:T(8,128)}, u32[]{:S(2)}) copy-start(f32[4,16,16,128]{3,2,1,0:T(8,128)} %param.15) | copy-start | bytes 1572868
  11.4 1.4 %copy-start.5 = (f32[16,16,128]{2,1,0:T(8,128)S(1)}, f32[16,16,128]{2,1,0:T(8,128)}, u32[]{:S(2)}) copy-start(f32[16,16,128]{2,1,0:T(8,128)} %param.17) | copy-start | bytes 393220
  16.3 6.7 %collective-permute-start.2 = (f32[16,2176]{1,0:T(8,128)S(1)}, f32[16,2176]{1,0:T(8,128)S(1)}, u32[]{:S(2)}, u32[]{:S(2)}) collective-permute-start(f32[16,2176]{1,0:T(8,128)S(1)} %get-tuple-element.45), channel_id=1, source_target_pairs={{0,16},{16,32},{32,48},{48,64},{64,80},{80,96},{96,112},{112,128},... | collective-permute-start | bytes 417800 | tf_op jit(solution)/shard_map/ppermute | solution.py:731
  19.3 6.4 %collective-permute-start.3 = (f32[16,2176]{1,0:T(8,128)S(1)}, f32[16,2176]{1,0:T(8,128)S(1)}, u32[]{:S(2)}, u32[]{:S(2)}) collective-permute-start(f32[16,2176]{1,0:T(8,128)S(1)} %get-tuple-element.46), channel_id=1, source_target_pairs={{16,0},{32,16},{48,32},{64,48},{80,64},{96,80},{112,96},{128,112},... | collective-permute-start | bytes 417800 | tf_op jit(solution)/shard_map/ppermute | solution.py:731
  31.0 9.3 %collective-permute-start.4 = (f32[16,1152]{1,0:T(8,128)S(1)}, f32[16,1152]{1,0:T(8,128)S(1)}, u32[]{:S(2)}, u32[]{:S(2)}) collective-permute-start(f32[16,1152]{1,0:T(8,128)S(1)} %get-tuple-element.51), channel_id=1, source_target_pairs={{0,16},{16,32},{32,48},{48,64},{64,80},{80,96},{96,112},{112,128},... | collective-permute-start | bytes 221192 | tf_op jit(solution)/shard_map/ppermute | solution.py:731
  36.4 7.0 %collective-permute-start.5 = (f32[16,1152]{1,0:T(8,128)S(1)}, f32[16,1152]{1,0:T(8,128)S(1)}, u32[]{:S(2)}, u32[]{:S(2)}) collective-permute-start(f32[16,1152]{1,0:T(8,128)S(1)} %get-tuple-element.52), channel_id=1, source_target_pairs={{16,0},{32,16},{48,32},{64,48},{80,64},{96,80},{112,96},{128,112},... | collective-permute-start | bytes 221192 | tf_op jit(solution)/shard_map/ppermute | solution.py:731
  46.1 23.2 %all-to-all-start.1 = ((f32[32,32,128]{2,1,0:T(8,128)}), f32[32,32,128]{2,1,0:T(8,128)S(1)}, u32[]{:S(2)}, u32[]{:S(2)}) async-start(f32[32,32,128]{2,1,0:T(8,128)} %get-tuple-element.58), calls=%async_computation.1 | async-start | bytes 1048576 | tf_op jit(solution)/shard_map/all_to_all | solution.py:808
  70.7 24.1 %copy-start = (bf16[2048,256]{1,0:T(8,128)(2,1)S(1)}, bf16[2048,256]{1,0:T(8,128)(2,1)}, u32[]{:S(2)}) copy-start(bf16[2048,256]{1,0:T(8,128)(2,1)} %constant.25.clone.table_high) | copy-start | bytes 3145732
  70.7 24.1 %copy-start.1 = (bf16[2048,256]{1,0:T(8,128)(2,1)S(1)}, bf16[2048,256]{1,0:T(8,128)(2,1)}, u32[]{:S(2)}) copy-start(bf16[2048,256]{1,0:T(8,128)(2,1)} %constant.26.clone.table_low) | copy-start | bytes 3145732

commit v10 on v9

--- a/solution.py
+++ b/solution.py
@@ -652,12 +652,13 @@
     column = lax.broadcasted_iota(jnp.int32, (sources * SLOTS, LANES), 1).astype(F32)
     chosen = jnp.transpose(jnp.where(row == column + 1.0, 1.0, 0.0))[:ROWS_DEV].astype(BF16)
     both = jnp.concatenate([chosen, chosen], axis=1)
+    columns = [
+        pieces[:, c * SLOTS : (c + 1) * SLOTS, :].reshape(sources * SLOTS, LANES) for c in range(C)
+    ]
+    high, low = split(jnp.concatenate(columns, axis=1))
+    rows = dot(both, jnp.concatenate([high, low], axis=0))
     for c in range(C):
-        x = pieces[:, c * SLOTS : (c + 1) * SLOTS, :].reshape(sources * SLOTS, LANES)
-        high, low = split(x)
-        out[c * ROWS_DEV : (c + 1) * ROWS_DEV, :] = dot(
-            both, jnp.concatenate([high, low], axis=0)
-        )
+        out[c * ROWS_DEV : (c + 1) * ROWS_DEV, :] = lanes_of(rows, c)
 
 
 def dft_kernel(rows, phase, table_high, table_low, out):

time: 96.5 us -> 96.4 us (level)
  no operation moved by 1% of the time
where the time goes in v10:
time: 96.4 us; the launch traced here: 96 us
  starting transfers between devices  28.5 us (30%)
  blocking collectives  24.1 us (25%)
  Pallas kernels  22.2 us (23%)
  waiting for transfers between devices  17.9 us (19%)
  local copies, waits for them, and re-layouts  1.8 us (2%)
  between operations  1.54 us (2%)
    all_gather x1, blocking collectives, body(): rows = lax.all_gather(rows, 'girth')  24.1 us
    pallas_call x8, Pallas kernels, call(): pl.pallas_call(kernel, out_shape=out_shape, in_specs=[vmem] * len(args),...  19.2 us
    all_to_all x1, waiting for transfers between devices, body(): pieces = lax.all_to_all(packed, 'axial', 0, 0)  12.1 us
    ppermute x4, starting transfers between devices, exchange(): return (lax.ppermute(high, 'axial', up), lax.ppermute(low, 'axial', down))  11.1 us
    all_to_all x1, starting transfers between devices, body(): pieces = lax.all_to_all(packed, 'axial', 0, 0)  10.5 us
    ppermute x4, waiting for transfers between devices, exchange(): return (lax.ppermute(high, 'axial', up), lax.ppermute(low, 'axial', down))  5.77 us
    ppermute x1, starting transfers between devices, body(): right = lax.ppermute(to_left, 'girth', back)  4.22 us
    ppermute x1, starting transfers between devices, body(): left = lax.ppermute(to_right, 'girth', around)  2.7 us
  transfers between devices with their start and end apart: 7, of which 3 were waited for; matrix products, arithmetic and copies ran while one was open for 1% of the time, Pallas kernels for 7%

profile of v10, /device:TPU:1, one launch (start us, length us, event | category | flops | bytes accessed | tf_op | source)
XLA Modules:
  0.0 96.0 jit_solution(9481859124682679892)
XLA Ops:
  0.6 0.0 copy-start.2
  0.6 0.0 copy-start.6
  0.7 0.0 copy-start.7
  0.7 0.0 copy-start.4
  0.7 2.4 %shard_map.140 = (f32[2,256,128]{2,1,0:T(8,128)}, f32[2,256,128]{2,1,0:T(8,128)}) custom-call(f32[4,256,128]{2,1,0:T(8,128)} %bitcast.13, f32[3,256,128]{2,1,0:T(8,128)} %bitcast.16, f32[256,128]{1,0:T(8,128)} %bitcast.22), custom_call_target="tpu_custom_call" | custom-call | tf_op jit(solution)/shard_map/pallas_call | solution.py:701
  3.1 0.0 copy-start.11
  3.1 0.0 copy-start.8
  3.1 0.0 copy-start.9
  3.1 0.0 copy-start.10
  3.1 2.7 %collective-permute-start = (f32[2,256,128]{2,1,0:T(8,128)}, f32[2,256,128]{2,1,0:T(8,128)S(1)}, u32[]{:S(2)}, u32[]{:S(2)}) collective-permute-start(f32[2,256,128]{2,1,0:T(8,128)} %get-tuple-element.37), channel_id=1, source_target_pairs={{0,1},{1,2},{2,3},{3,4},{4,5},{5,6},{6,7},{7,8},{8,9},{9,10},{10,1... | collective-permute-start | bytes 786440 | tf_op jit(solution)/shard_map/ppermute | solution.py:727
  5.8 4.2 %collective-permute-start.1 = (f32[2,256,128]{2,1,0:T(8,128)}, f32[2,256,128]{2,1,0:T(8,128)S(1)}, u32[]{:S(2)}, u32[]{:S(2)}) collective-permute-start(f32[2,256,128]{2,1,0:T(8,128)} %get-tuple-element.38), channel_id=1, source_target_pairs={{1,0},{2,1},{3,2},{4,3},{5,4},{6,5},{7,6},{8,7},{9,8},{10,9},{11,1... | collective-permute-start | bytes 786440 | tf_op jit(solution)/shard_map/ppermute | solution.py:728
  10.0 0.0 copy-done.6
  10.0 0.0 copy-done.7
  10.0 0.0 copy-done.11
  10.0 0.0 copy-done.8
  10.0 0.0 copy-done.9
  10.1 0.0 copy-done.10
  10.1 0.2 shard_map.146
  10.3 0.0 copy-done.2
  10.3 0.0 copy-done.4
  10.3 0.0 copy-start.3
  10.3 1.0 %copy-done.3 = f32[4,16,16,128]{3,2,1,0:T(8,128)S(1)} copy-done((f32[4,16,16,128]{3,2,1,0:T(8,128)S(1)}, f32[4,16,16,128]{3,2,1,0:T(8,128)}, u32[]{:S(2)}) %copy-start.3) | copy-done | bytes 524312
  11.4 1.4 %shard_map.141.own_total = f32[256,512]{1,0:T(8,128)S(1)} custom-call(f32[4,256,128]{2,1,0:T(8,128)S(1)} %bitcast.14, f32[3,256,128]{2,1,0:T(8,128)S(1)} %bitcast.17, bf16[1216,256]{1,0:T(8,128)(2,1)S(1)} %copy-done.2), custom_call_target="tpu_custom_call" | custom-call | flops 1207959552 | bytes 2000000 | tf_op jit(solution)/shard_map/pallas_call | solution.py:689
  12.8 0.0 collective-permute-done.left
  12.8 0.0 collective-permute-done.1.right
  12.8 0.0 copy-done.5
  12.8 3.4 %shard_map.142 = (f32[3,256,256]{2,1,0:T(8,128)S(1)}, f32[256,768]{1,0:T(8,128)S(1)}, f32[256,384]{1,0:T(8,128)S(1)}, f32[256,384]{1,0:T(8,128)S(1)}, f32[16,307...) custom-call(f32[2,256,128]{2,1,0:T(8,128)S(1)} %collective-permute-done.left, ...), custom_call_target="tpu_custom_call" | custom-call | flops 1207959552 | bytes 2000000 | tf_op jit(solution)/shard_map/pallas_call | solution.py:689
  16.3 3.0 %collective-permute-start.2 = (f32[16,2176]{1,0:T(8,128)S(1)}, f32[16,2176]{1,0:T(8,128)S(1)}, u32[]{:S(2)}, u32[]{:S(2)}) collective-permute-start(f32[16,2176]{1,0:T(8,128)S(1)} %get-tuple-element.45), channel_id=1, source_target_pairs={{0,16},{16,32},{32,48},{48,64},{64,80},{80,96},{96,112},{112,128},... | collective-permute-start | bytes 417800 | tf_op jit(solution)/shard_map/ppermute | solution.py:732
  19.3 1.3 %collective-permute-start.3 = (f32[16,2176]{1,0:T(8,128)S(1)}, f32[16,2176]{1,0:T(8,128)S(1)}, u32[]{:S(2)}, u32[]{:S(2)}) collective-permute-start(f32[16,2176]{1,0:T(8,128)S(1)} %get-tuple-element.46), channel_id=1, source_target_pairs={{16,0},{32,16},{48,32},{64,48},{80,64},{96,80},{112,96},{128,112},... | collective-permute-start | bytes 417800 | tf_op jit(solution)/shard_map/ppermute | solution.py:732
  20.6 2.4 %shard_map.143.second = f32[256,768]{1,0:T(8,128)S(1)} custom-call(f32[256,768]{1,0:T(8,128)S(1)} %get-tuple-element.39.state, f32[3,256,128]{2,1,0:T(8,128)S(1)} %bitcast.19, f32[3,256,256]{2,1,0:T(8,128)S(1)} %get-tuple-element.40.halo_geom, bf16[1216,256]{1,0:T(8,128)(2,1)S(1)} %copy-done.2), custom_call_target="tpu_custom_call" | custom-call | flops 1811939328 | bytes 2000000 | tf_op jit(solution)/shard_map/pallas_call | solution.py:689
  23.0 0.0 collective-permute-done.2.got_low
  23.0 2.7 %collective-permute-done.3.got_high = f32[16,2176]{1,0:T(8,128)S(1)} collective-permute-done((f32[16,2176]{1,0:T(8,128)S(1)}, f32[16,2176]{1,0:T(8,128)S(1)}, u32[]{:S(2)}, u32[]{:S(2)}) %collective-permute-start.3) | collective-permute-done | bytes 139296 | tf_op jit(solution)/shard_map/ppermute | solution.py:732
  25.7 5.3 %shard_map.144 = (f32[256,768]{1,0:T(8,128)S(1)}, f32[256,384]{1,0:T(8,128)S(1)}, f32[16,1536]{1,0:T(8,128)S(1)}, f32[16,1536]{1,0:T(8,128)S(1)}, f32[16,1152]{1,0:T(8,128)S(1)}, /*index=5*/f32[16,1152]{1,0:T(8,128)S(1)}) custom-call(f32[256,768]{1,0:T(8,128)S(1)} %get-tuple-element.39.state, f32[256,768]{1,0:T(8,128)S(1)} %shard_map.143.second, ...), custom_call_target="tpu_custom_call" | custom-call | flops 2415919104 | bytes 2000000 | tf_op jit(solution)/shard_map/pallas_call | solution.py:689
  31.0 5.4 %collective-permute-start.4 = (f32[16,1152]{1,0:T(8,128)S(1)}, f32[16,1152]{1,0:T(8,128)S(1)}, u32[]{:S(2)}, u32[]{:S(2)}) collective-permute-start(f32[16,1152]{1,0:T(8,128)S(1)} %get-tuple-element.51), channel_id=1, source_target_pairs={{0,16},{16,32},{32,48},{48,64},{64,80},{80,96},{96,112},{112,128},... | collective-permute-start | bytes 221192 | tf_op jit(solution)/shard_map/ppermute | solution.py:732
  36.4 1.5 %collective-permute-start.5 = (f32[16,1152]{1,0:T(8,128)S(1)}, f32[16,1152]{1,0:T(8,128)S(1)}, u32[]{:S(2)}, u32[]{:S(2)}) collective-permute-start(f32[16,1152]{1,0:T(8,128)S(1)} %get-tuple-element.52), channel_id=1, source_target_pairs={{16,0},{32,16},{48,32},{64,48},{80,64},{96,80},{112,96},{128,112},... | collective-permute-start | bytes 221192 | tf_op jit(solution)/shard_map/ppermute | solution.py:732
  37.9 2.4 %shard_map.145.second = f32[256,768]{1,0:T(8,128)S(1)} custom-call(f32[256,768]{1,0:T(8,128)S(1)} %get-tuple-element.47.state, f32[3,256,128]{2,1,0:T(8,128)S(1)} %bitcast.21, f32[3,256,256]{2,1,0:T(8,128)S(1)} %get-tuple-element.40.halo_geom, bf16[1216,256]{1,0:T(8,128)(2,1)S(1)} %copy-done.2), custom_call_target="tpu_custom_call" | custom-call | flops 1811939328 | bytes 2000000 | tf_op jit(solution)/shard_map/pallas_call | solution.py:689
  40.3 0.0 collective-permute-done.4.new_low
  40.3 3.0 %collective-permute-done.5.new_high = f32[16,1152]{1,0:T(8,128)S(1)} collective-permute-done((f32[16,1152]{1,0:T(8,128)S(1)}, f32[16,1152]{1,0:T(8,128)S(1)}, u32[]{:S(2)}, u32[]{:S(2)}) %collective-permute-start.5) | collective-permute-done | bytes 73760 | tf_op jit(solution)/shard_map/ppermute | solution.py:732
  43.4 2.7 %shard_map.147 = (f32[4,256,128]{2,1,0:T(8,128)}, f32[32,32,128]{2,1,0:T(8,128)}, f32[64,512]{1,0:T(8,128)S(1)}) custom-call(f32[256,768]{1,0:T(8,128)S(1)} %get-tuple-element.47.state, f32[256,768]{1,0:T(8,128)S(1)} %shard_map.145.second, f32[256,384]{1,0:T(8,128)S(1)} %get-tuple-element.48.inverse, f32[256,384]{1,0:T(8,128)S(1)} %get-tuple-element.42.ends, ...), custom_call_target="tpu_custom_call" | custom-call | flops 603979776 | bytes 2000000 | tf_op jit(solution)/shard_map/pallas_call | solution.py:689
  46.1 10.5 %all-to-all-start.1 = ((f32[32,32,128]{2,1,0:T(8,128)}), f32[32,32,128]{2,1,0:T(8,128)S(1)}, u32[]{:S(2)}, u32[]{:S(2)}) async-start(f32[32,32,128]{2,1,0:T(8,128)} %get-tuple-element.58), calls=%async_computation.1 | async-start | bytes 1048576 | tf_op jit(solution)/shard_map/all_to_all | solution.py:809
  56.5 0.7 dynamic-slice_bitcast_fusion.phase
  57.2 12.1 %all-to-all-done.1.pieces = f32[32,32,128]{2,1,0:T(8,128)S(1)} async-done(((f32[32,32,128]{2,1,0:T(8,128)}), f32[32,32,128]{2,1,0:T(8,128)S(1)}, u32[]{:S(2)}, u32[]{:S(2)}) %all-to-all-start.1) | async-done | bytes 524320 | tf_op jit(solution)/shard_map/all_to_all | solution.py:809
  69.3 0.7 shard_map.148
  70.6 0.0 copy-start
  70.7 0.0 copy-start.1
  70.7 24.1 %all-gather = f32[1024,128]{1,0:T(8,128)S(1)} all-gather(f32[64,128]{1,0:T(8,128)S(1)} %get-tuple-element.62), channel_id=2, replica_groups=mesh['axial'=32,'girth'=16] {'girth'}, dimensions={0}, use_global_device_ids=true | all-gather | bytes 557056 | tf_op jit(solution)/shard_map/all_gather | solution.py:834
  94.8 0.0 copy-done.1
  94.8 1.2 %shard_map.149 = f32[2,16,4,128]{3,2,1,0:T(4,128)} custom-call(f32[16,64,128]{2,1,0:T(8,128)S(1)} %bitcast.12, f32[2,128]{1,0:T(2,128)S(1)} %dynamic-slice_bitcast_fusion.phase, bf16[2048,256]{1,0:T(8,128)(2,1)S(1)} %copy-done, bf16[2048,256]{1,0:T(8,128)(2,1)S(1)} %copy-done.1), custom_call_target="tpu_custom_call" | custom-call | flops 603979776 | bytes 2000000 | tf_op jit(solution)/shard_map/pallas_call | solution.py:689
  (3 shorter events, 0.0 us)
Async XLA Ops:
  0.6 9.7 %copy-start.2 = (bf16[1216,256]{1,0:T(8,128)(2,1)S(1)}, bf16[1216,256]{1,0:T(8,128)(2,1)}, u32[]{:S(2)}) copy-start(bf16[1216,256]{1,0:T(8,128)(2,1)} %constant.23.clone.table.tables.refs_0_) | copy-start | bytes 1867780
  0.6 9.4 %copy-start.6 = (f32[2,8,64]{2,1,0:T(8,128)S(1)}, f32[2,8,64]{2,1,0:T(8,128)}, u32[]{:S(2)}) copy-start(f32[2,8,64]{2,1,0:T(8,128)} %cycle_weights.1) | copy-start | bytes 12292
  0.7 9.4 %copy-start.7 = (f32[8,128]{1,0:T(8,128)S(1)}, f32[8,128]{1,0:T(8,128)}, u32[]{:S(2)}) copy-start(f32[8,128]{1,0:T(8,128)} %az_weights.1) | copy-start | bytes 12292
  0.7 9.7 %copy-start.4 = (f32[3,16,16,128]{3,2,1,0:T(8,128)S(1)}, f32[3,16,16,128]{3,2,1,0:T(8,128)}, u32[]{:S(2)}) copy-start(f32[3,16,16,128]{3,2,1,0:T(8,128)} %param.16) | copy-start | bytes 1179652
  3.1 7.0 %copy-start.11 = (s32[64]{0:T(128)S(1)}, s32[64]{0:T(128)}, u32[]{:S(2)}) copy-start(s32[64]{0:T(128)} %cycle_id.1) | copy-start | bytes 772
  3.1 7.0 %copy-start.8 = (s32[64]{0:T(128)S(1)}, s32[64]{0:T(128)}, u32[]{:S(2)}) copy-start(s32[64]{0:T(128)} %cycle_radial.1) | copy-start | bytes 772
  3.1 7.0 %copy-start.9 = (s32[64]{0:T(128)S(1)}, s32[64]{0:T(128)}, u32[]{:S(2)}) copy-start(s32[64]{0:T(128)} %cycle_axial.1) | copy-start | bytes 772
  3.1 7.0 %copy-start.10 = (s32[128]{0:T(128)S(1)}, s32[128]{0:T(128)}, u32[]{:S(2)}) copy-start(s32[128]{0:T(128)} %az_elem.1) | copy-start | bytes 1540
  3.1 9.7 %collective-permute-start = (f32[2,256,128]{2,1,0:T(8,128)}, f32[2,256,128]{2,1,0:T(8,128)S(1)}, u32[]{:S(2)}, u32[]{:S(2)}) collective-permute-start(f32[2,256,128]{2,1,0:T(8,128)} %get-tuple-element.37), channel_id=1, source_target_pairs={{0,1},{1,2},{2,3},{3,4},{4,5},{5,6},{6,7},{7,8},{8,9},{9,10},{10,1... | collective-permute-start | bytes 786440 | tf_op jit(solution)/shard_map/ppermute | solution.py:727
  5.8 7.0 %collective-permute-start.1 = (f32[2,256,128]{2,1,0:T(8,128)}, f32[2,256,128]{2,1,0:T(8,128)S(1)}, u32[]{:S(2)}, u32[]{:S(2)}) collective-permute-start(f32[2,256,128]{2,1,0:T(8,128)} %get-tuple-element.38), channel_id=1, source_target_pairs={{1,0},{2,1},{3,2},{4,3},{5,4},{6,5},{7,6},{8,7},{9,8},{10,9},{11,1... | collective-permute-start | bytes 786440 | tf_op jit(solution)/shard_map/ppermute | solution.py:728
  10.3 1.1 %copy-start.3 = (f32[4,16,16,128]{3,2,1,0:T(8,128)S(1)}, f32[4,16,16,128]{3,2,1,0:T(8,128)}, u32[]{:S(2)}) copy-start(f32[4,16,16,128]{3,2,1,0:T(8,128)} %param.15) | copy-start | bytes 1572868
  11.4 1.4 %copy-start.5 = (f32[16,16,128]{2,1,0:T(8,128)S(1)}, f32[16,16,128]{2,1,0:T(8,128)}, u32[]{:S(2)}) copy-start(f32[16,16,128]{2,1,0:T(8,128)} %param.17) | copy-start | bytes 393220
  16.3 6.7 %collective-permute-start.2 = (f32[16,2176]{1,0:T(8,128)S(1)}, f32[16,2176]{1,0:T(8,128)S(1)}, u32[]{:S(2)}, u32[]{:S(2)}) collective-permute-start(f32[16,2176]{1,0:T(8,128)S(1)} %get-tuple-element.45), channel_id=1, source_target_pairs={{0,16},{16,32},{32,48},{48,64},{64,80},{80,96},{96,112},{112,128},... | collective-permute-start | bytes 417800 | tf_op jit(solution)/shard_map/ppermute | solution.py:732
  19.3 6.4 %collective-permute-start.3 = (f32[16,2176]{1,0:T(8,128)S(1)}, f32[16,2176]{1,0:T(8,128)S(1)}, u32[]{:S(2)}, u32[]{:S(2)}) collective-permute-start(f32[16,2176]{1,0:T(8,128)S(1)} %get-tuple-element.46), channel_id=1, source_target_pairs={{16,0},{32,16},{48,32},{64,48},{80,64},{96,80},{112,96},{128,112},... | collective-permute-start | bytes 417800 | tf_op jit(solution)/shard_map/ppermute | solution.py:732
  31.0 9.3 %collective-permute-start.4 = (f32[16,1152]{1,0:T(8,128)S(1)}, f32[16,1152]{1,0:T(8,128)S(1)}, u32[]{:S(2)}, u32[]{:S(2)}) collective-permute-start(f32[16,1152]{1,0:T(8,128)S(1)} %get-tuple-element.51), channel_id=1, source_target_pairs={{0,16},{16,32},{32,48},{48,64},{64,80},{80,96},{96,112},{112,128},... | collective-permute-start | bytes 221192 | tf_op jit(solution)/shard_map/ppermute | solution.py:732
  36.4 7.0 %collective-permute-start.5 = (f32[16,1152]{1,0:T(8,128)S(1)}, f32[16,1152]{1,0:T(8,128)S(1)}, u32[]{:S(2)}, u32[]{:S(2)}) collective-permute-start(f32[16,1152]{1,0:T(8,128)S(1)} %get-tuple-element.52), channel_id=1, source_target_pairs={{16,0},{32,16},{48,32},{64,48},{80,64},{96,80},{112,96},{128,112},... | collective-permute-start | bytes 221192 | tf_op jit(solution)/shard_map/ppermute | solution.py:732
  46.1 23.2 %all-to-all-start.1 = ((f32[32,32,128]{2,1,0:T(8,128)}), f32[32,32,128]{2,1,0:T(8,128)S(1)}, u32[]{:S(2)}, u32[]{:S(2)}) async-start(f32[32,32,128]{2,1,0:T(8,128)} %get-tuple-element.58), calls=%async_computation.1 | async-start | bytes 1048576 | tf_op jit(solution)/shard_map/all_to_all | solution.py:809
  70.6 24.1 %copy-start = (bf16[2048,256]{1,0:T(8,128)(2,1)S(1)}, bf16[2048,256]{1,0:T(8,128)(2,1)}, u32[]{:S(2)}) copy-start(bf16[2048,256]{1,0:T(8,128)(2,1)} %constant.25.clone.table_high) | copy-start | bytes 3145732
  70.7 24.1 %copy-start.1 = (bf16[2048,256]{1,0:T(8,128)(2,1)S(1)}, bf16[2048,256]{1,0:T(8,128)(2,1)}, u32[]{:S(2)}) copy-start(bf16[2048,256]{1,0:T(8,128)(2,1)} %constant.26.clone.table_low) | copy-start | bytes 3145732
